TPU v7x, 32 devices: a whole 2x2x4 slice. The times are simulated.
32 devices in a mesh: batch: 4 (over z), blk: 8 (over y, x, core).
Axes of the slice: x: 2, y: 2, z: 4, core: 2. Of those that a mesh axis runs over, the one named last changes fastest.
Arguments:
- tokens: bfloat16 [4, 8192, 1024], P('batch', 'blk'), may hold values from -6 to 6
- out_cot: bfloat16 [4, 8192, 1024], P('batch', 'blk'), may hold values from -6 to 6
- norm_gain: float32 [1024], replicated, may hold values from 0.5 to 1.5
- in_weight: bfloat16 [1024, 4096], replicated, may hold values from -0.1875 to 0.1875
- conv_weight: float32 [4, 2048], replicated, may hold values from -3 to 3
- conv_bias: float32 [2048], replicated, may hold values from -0.5 to 0.5
- xproj_weight: bfloat16 [2048, 96], replicated, may hold values from -0.5 to 0.5
- dt_weight: bfloat16 [64, 2048], replicated, may hold values from -0.75 to 0.75
- dt_bias: float32 [2048], replicated, may hold values from -10 to -3
- a_log: float32 [16, 2048], replicated, may hold values from 0 to 1.4
- d_skip: float32 [2048], replicated, may hold values from 0.5 to 1.5
- out_weight: bfloat16 [2048, 1024], replicated, may hold values from -0.375 to 0.375
- moment_one: float32 [6667264], P(('batch', 'blk')), may hold values from -0.0006 to 0.0006
- moment_two: float32 [6667264], P(('batch', 'blk')), may hold values from 1e-09 to 1e-07
Outputs:
- result: bfloat16 [4, 8192, 1024], P('batch', 'blk')
- grad_tokens: bfloat16 [4, 8192, 1024], P('batch', 'blk')
- grads: float32 [6667264], P(('batch', 'blk'))
- grad_norm: float32 [], replicated
- param_step: float32 [6667264], P(('batch', 'blk'))
- new_one: float32 [6667264], P(('batch', 'blk'))
- new_two: float32 [6667264], P(('batch', 'blk'))
All inputs are finite; a program needn't handle non-finite values.
Results may differ from a plain program's by a relative error of at most 0.012.
The roundings to bfloat16 on the way count: a program that leaves them out, or rounds other values in their place, can miss the bound.
Values sent between devices are 32-bit elements; how exact they have to be, the bound alone decides.
A program may use at most 704 MiB of HBM per device.

v0:
```python
import jax
import jax.numpy as jnp
from jax import lax
from jax.sharding import PartitionSpec as P

ADAM_STEP = 100


EPS = 1e-05
RATE = 0.002
BETA_ONE = 0.9
BETA_TWO = 0.95
ADAM_EPS = 1e-08
DECAY = 0.1
CLIP = 1.0


def shifted(x, axis, by):
    count = lax.axis_size(axis)
    pairs = [(i, i + by) for i in range(count) if 0 <= i + by < count]
    return lax.ppermute(x, axis, pairs)


def silu(value):
    return value * jax.nn.sigmoid(value)


def silu_slope(value):
    sig = jax.nn.sigmoid(value)
    return sig * (1.0 + value * (1.0 - sig))


def link(earlier, later):
    return (earlier[0] * later[0], later[0] * earlier[1] + later[1])


def to_blocks(value, sub_len):
    count = value.shape[0] // sub_len
    return value.reshape((count, sub_len) + value.shape[1:])


def from_blocks(value):
    return value.reshape((value.shape[0] * value.shape[1],) + value.shape[2:])


def pick(value, index):
    return lax.dynamic_index_in_dim(value, index, 1, keepdims=False)


def place_row(buffer, row, index):
    return lax.dynamic_update_index_in_dim(buffer, row[:, None], index, 1)


def sub_prefix(totals, ends):
    inc_decay, inc_state = lax.associative_scan(link, (totals, ends))
    ex_decay = jnp.concatenate([jnp.ones_like(inc_decay[:1]), inc_decay[:-1]], 0)
    ex_state = jnp.concatenate([jnp.zeros_like(inc_state[:1]), inc_state[:-1]], 0)
    return (ex_decay, ex_state, inc_decay[-1], inc_state[-1])


def local(
    tokens,
    out_cot,
    norm_gain,
    in_weight,
    conv_weight,
    conv_bias,
    xproj_weight,
    dt_weight,
    dt_bias,
    a_log,
    d_skip,
    out_weight,
    moment_one,
    moment_two,
):
    f32 = jnp.float32
    bf16 = jnp.bfloat16
    contract = (((0,), (0,)), ((), ()))
    backward = (((1,), (1,)), ((), ()))
    source = tokens[0].astype(f32)
    cot_low = out_cot[0]
    cotangent = cot_low.astype(f32)
    length = source.shape[0]
    inner = dt_bias.shape[0]
    state = a_log.shape[0]
    rank = dt_weight.shape[0]
    width = conv_weight.shape[0]
    sub_len = 16
    count = length // sub_len
    positions = jnp.arange(sub_len, dtype=jnp.int32)
    scale = lax.rsqrt(jnp.mean(source * source, axis=-1, keepdims=True) + EPS)
    normed = (source * scale * norm_gain).astype(bf16)
    projected = jnp.dot(normed, in_weight, preferred_element_type=f32)
    stream = projected[:, :inner]
    gating = projected[:, inner:]
    tail = shifted(stream[length - width + 1 :], "blk", 1)

    def delayed(offset):
        lag = width - 1 - offset
        return jnp.concatenate([tail[width - 1 - lag :], stream[: length - lag]], 0)

    conv_sum = conv_bias + conv_weight[width - 1] * stream
    for offset in range(width - 1):
        conv_sum = conv_sum + conv_weight[offset] * delayed(offset)
    conv_low = silu(conv_sum).astype(bf16)
    conv_val = conv_low.astype(f32)
    selectors = jnp.dot(conv_low, xproj_weight, preferred_element_type=f32)
    step_low = selectors[:, :rank].astype(bf16)
    inject = selectors[:, rank : rank + state]
    readout = selectors[:, rank + state :]
    step_pre = jnp.dot(step_low, dt_weight, preferred_element_type=f32) + dt_bias
    step_size = jax.nn.softplus(step_pre)
    rates = -jnp.exp(a_log)
    step_rows = to_blocks(step_size, sub_len)
    conv_rows = to_blocks(conv_val, sub_len)
    drive_rows = step_rows * conv_rows
    inject_rows = to_blocks(inject, sub_len)
    readout_rows = to_blocks(readout, sub_len)

    def local_step(carry, index):
        fresh = (
            jnp.exp(pick(step_rows, index)[:, None, :] * rates) * carry
            + pick(drive_rows, index)[:, None, :] * pick(inject_rows, index)[:, :, None]
        )
        return (fresh, None)

    zero_state = jnp.zeros((count, state, inner), f32)
    ends, _ = lax.scan(local_step, zero_state, positions)
    totals = jnp.exp(jnp.sum(step_rows, 1)[:, None, :] * rates)
    ex_decay, ex_state, group_decay, group_state = sub_prefix(totals, ends)

    def pass_state(turn, incoming):
        return shifted(group_decay * incoming + group_state, "blk", 1)

    entry = lax.fori_loop(0, lax.axis_size("blk") - 1, pass_state, jnp.zeros_like(group_state))
    starts = ex_state + ex_decay * entry[None]

    def exact_step(carry, index):
        prior, outputs = carry
        fresh = (
            jnp.exp(pick(step_rows, index)[:, None, :] * rates) * prior
            + pick(drive_rows, index)[:, None, :] * pick(inject_rows, index)[:, :, None]
        )
        outputs = place_row(
            outputs, jnp.sum(pick(readout_rows, index)[:, :, None] * fresh, 1), index
        )
        return ((fresh, outputs), prior)

    (_, scan_rows), before = lax.scan(
        exact_step, (starts, jnp.zeros((count, sub_len, inner), f32)), positions
    )
    scanned = from_blocks(scan_rows) + d_skip * conv_val
    gate_val = silu(gating)
    gated = (scanned * gate_val).astype(bf16)
    output = jnp.dot(gated, out_weight, preferred_element_type=f32)
    result = (source + output).astype(bf16)[None]
    grad_out_weight = lax.dot_general(gated, cot_low, contract, preferred_element_type=f32)
    grad_gated = lax.dot_general(cot_low, out_weight, backward, preferred_element_type=f32)
    grad_scanned = grad_gated * gate_val
    grad_gating = grad_gated * scanned * silu_slope(gating)
    grad_d_skip = jnp.sum(grad_scanned * conv_val, 0)
    grad_rows = to_blocks(grad_scanned, sub_len)

    def local_back(carry, index):
        adjoint = pick(grad_rows, index)[:, None, :] * pick(readout_rows, index)[:, :, None] + carry
        return (jnp.exp(pick(step_rows, index)[:, None, :] * rates) * adjoint, None)

    exits, _ = lax.scan(local_back, zero_state, positions, reverse=True)
    rev_decay, rev_state, group_rdecay, group_rstate = sub_prefix(
        jnp.flip(totals, 0), jnp.flip(exits, 0)
    )
    rev_decay = jnp.flip(rev_decay, 0)
    rev_state = jnp.flip(rev_state, 0)

    def pass_adjoint(turn, incoming):
        return shifted(group_rdecay * incoming + group_rstate, "blk", -1)

    arriving = lax.fori_loop(
        0, lax.axis_size("blk") - 1, pass_adjoint, jnp.zeros_like(group_rstate)
    )
    finals = rev_state + rev_decay * arriving[None]

    def exact_back(carry, row):
        adjoint_in, grad_rates, step_buf, conv_buf, inject_buf, readout_buf = carry
        index, prior = row
        step_row = pick(step_rows, index)
        drive_row = pick(drive_rows, index)
        conv_row = pick(conv_rows, index)
        inject_row = pick(inject_rows, index)
        readout_row = pick(readout_rows, index)
        grad_row = pick(grad_rows, index)
        decay = jnp.exp(step_row[:, None, :] * rates)
        adjoint = grad_row[:, None, :] * readout_row[:, :, None] + adjoint_in
        fresh = decay * prior + drive_row[:, None, :] * inject_row[:, :, None]
        through = adjoint * prior * decay
        feed = jnp.sum(adjoint * inject_row[:, :, None], 1)
        grad_step = jnp.sum(through * rates, 1) + conv_row * feed
        grad_conv = step_row * feed
        grad_inject = jnp.sum(adjoint * drive_row[:, None, :], 2)
        grad_readout = jnp.sum(grad_row[:, None, :] * fresh, 2)
        grad_rates = grad_rates + jnp.sum(through * step_row[:, None, :], 0)
        step_buf = place_row(step_buf, grad_step, index)
        conv_buf = place_row(conv_buf, grad_conv, index)
        inject_buf = place_row(inject_buf, grad_inject, index)
        readout_buf = place_row(readout_buf, grad_readout, index)
        return ((decay * adjoint, grad_rates, step_buf, conv_buf, inject_buf, readout_buf), None)

    wide_zero = jnp.zeros((count, sub_len, inner), f32)
    thin_zero = jnp.zeros((count, sub_len, state), f32)
    (_, grad_rates, step_grads, conv_grads, inject_grads, readout_grads), _ = lax.scan(
        exact_back,
        (finals, jnp.zeros_like(rates), wide_zero, wide_zero, thin_zero, thin_zero),
        (positions, before),
        reverse=True,
    )
    grad_a_log = grad_rates * rates
    grad_pre = from_blocks(step_grads) * jax.nn.sigmoid(step_pre)
    grad_dt_bias = jnp.sum(grad_pre, 0)
    grad_pre_low = grad_pre.astype(bf16)
    grad_dt_weight = lax.dot_general(step_low, grad_pre_low, contract, preferred_element_type=f32)
    grad_step_low = lax.dot_general(grad_pre_low, dt_weight, backward, preferred_element_type=f32)
    grad_selectors = jnp.concatenate(
        [grad_step_low, from_blocks(inject_grads), from_blocks(readout_grads)], 1
    ).astype(bf16)
    grad_xproj = lax.dot_general(conv_low, grad_selectors, contract, preferred_element_type=f32)
    grad_conv_out = (
        grad_scanned * d_skip
        + from_blocks(conv_grads)
        + lax.dot_general(grad_selectors, xproj_weight, backward, preferred_element_type=f32)
    )
    grad_conv = grad_conv_out * silu_slope(conv_sum)
    ahead = shifted(grad_conv[: width - 1], "blk", -1)
    grad_stream = conv_weight[width - 1] * grad_conv
    tap_grads = []
    for offset in range(width - 1):
        lead = width - 1 - offset
        grad_stream = grad_stream + conv_weight[offset] * jnp.concatenate(
            [grad_conv[lead:], ahead[:lead]], 0
        )
        tap_grads.append(jnp.sum(grad_conv * delayed(offset), 0))
    tap_grads.append(jnp.sum(grad_conv * stream, 0))
    grad_conv_weight = jnp.stack(tap_grads, 0)
    grad_conv_bias = jnp.sum(grad_conv, 0)
    grad_projected = jnp.concatenate([grad_stream, grad_gating], 1).astype(bf16)
    grad_in_weight = lax.dot_general(normed, grad_projected, contract, preferred_element_type=f32)
    grad_normed = lax.dot_general(grad_projected, in_weight, backward, preferred_element_type=f32)
    grad_gain = jnp.sum(grad_normed * source * scale, 0)
    weighted = grad_normed * norm_gain
    grad_source = (
        scale * weighted
        - source * scale**3 * jnp.mean(weighted * source, axis=-1, keepdims=True)
        + cotangent
    )
    grad_tokens = grad_source.astype(bf16)[None]
    pieces = (
        grad_gain,
        grad_in_weight,
        grad_conv_weight,
        grad_conv_bias,
        grad_xproj,
        grad_dt_weight,
        grad_dt_bias,
        grad_a_log,
        grad_d_skip,
        grad_out_weight,
    )
    flat = jnp.concatenate([value.reshape(-1) for value in pieces])
    shard = lax.psum_scatter(flat, ("batch", "blk"), scatter_dimension=0, tiled=True)
    squares = lax.psum(jnp.sum(shard * shard), ("batch", "blk"))
    grad_norm = jnp.sqrt(squares)
    params = (
        norm_gain,
        in_weight,
        conv_weight,
        conv_bias,
        xproj_weight,
        dt_weight,
        dt_bias,
        a_log,
        d_skip,
        out_weight,
    )
    counts = [value.size for value in params]
    lower = sum(counts[:6])
    upper = sum(counts[:9])
    span = shard.shape[0]
    begin = lax.axis_index(("batch", "blk")) * span
    every = jnp.concatenate([value.astype(f32).reshape(-1) for value in params])
    owned = lax.dynamic_slice_in_dim(every, begin, span)
    place = begin + lax.iota(jnp.int32, span)
    keep = jnp.where((place >= lower) & (place < upper), 0.0, 1.0).astype(f32)
    clipped = shard * jnp.minimum(1.0, CLIP / (grad_norm + 1e-06))
    new_one = BETA_ONE * moment_one + (1.0 - BETA_ONE) * clipped
    new_two = BETA_TWO * moment_two + (1.0 - BETA_TWO) * clipped * clipped
    first = new_one / (1.0 - BETA_ONE**ADAM_STEP)
    second = new_two / (1.0 - BETA_TWO**ADAM_STEP)
    param_step = -RATE * (first / (jnp.sqrt(second) + ADAM_EPS) + DECAY * keep * owned)
    return (result, grad_tokens, shard, grad_norm, param_step, new_one, new_two)


def solution(mesh):
    return jax.shard_map(
        local,
        mesh=mesh,
        in_specs=(
            P("batch", "blk", None),
            P("batch", "blk", None),
            P(),
            P(),
            P(),
            P(),
            P(),
            P(),
            P(),
            P(),
            P(),
            P(),
            P(("batch", "blk")),
            P(("batch", "blk")),
        ),
        out_specs=(
            P("batch", "blk", None),
            P("batch", "blk", None),
            P(("batch", "blk")),
            P(),
            P(("batch", "blk")),
            P(("batch", "blk")),
            P(("batch", "blk")),
        ),
        check_vma=False,
    )
```

profile of v0, /device:TPU:0, one launch (start us, length us, event | category | flops | bytes accessed | tf_op | source)
XLA Modules:
  0.0 3135.4 jit_solution(1821891081656599619)
XLA Ops:
  42.4 14.6 copy.157
  103.3 24.8 multiply_reduce_fusion.5
  143.0 19.8 copy_multiply_fusion
  171.3 166.4 %while.88 = (s32[]{:T(128)}, f32[64,16,2048]{2,1,0:T(8,128)}, s32[16]{0:T(128)S(1)}, f32[64,16,2048]{2,0,1:T(8,128)}, f32[16,2048]{1,0:T(8,128)S(1)}, /*index=5*...) while((s32[]{:T(128)}, f32[64,16,2048]{2,1,0:T(8,128)}, ...), condition=%wide.region_2.3_spmd.clone, body=%wide.region_1.2_spmd.clone.sunk | while | flops 10485766 | bytes 20066468 | solution.py:129
  350.0 165.5 %while.89 = (s32[]{:T(128)}, f32[64,16,2048]{2,1,0:T(8,128)}, s32[16]{0:T(128)S(1)}, f32[64,16,2048]{2,0,1:T(8,128)}, f32[16,2048]{1,0:T(8,128)S(1)}, /*index=5*...) while((s32[]{:T(128)}, f32[64,16,2048]{2,1,0:T(8,128)}, ...), condition=%wide.region_10.11_spmd.clone, body=%wide.region_9.10_spmd.clone.sunk | while | flops 10485767 | bytes 20066488 | solution.py:169
  760.3 14.1 fusion.81
  808.4 21.0 pad.419
  829.5 21.2 pad.187
  873.7 21.1 pad.417
  894.8 21.1 pad.199
  915.9 21.2 pad.415
  937.1 21.1 pad.163
  958.1 21.0 pad.413
  979.2 21.1 pad.175
  1004.9 21.2 pad.162
  1040.1 21.0 pad.174
  1073.9 40.9 %while.85 = (s32[]{:T(128)}, f32[16,2048]{1,0:T(8,128)S(1)}, f32[16,2048]{1,0:T(8,128)S(1)}, f32[16,2048]{1,0:T(8,128)S(1)}, s32[]{:T(128)}) while((s32[]{:T(128)}, f32[16,2048]{1,0:T(8,128)S(1)}, f32[16,2048]{1,0:T(8,128)S(1)}, f32[16,2048]{1,0:T(8,128)S(1)}, s32[]{:T(128)}) %tuple.248), condition=%wide.region_5.6_spmd, body=%wide.region_4.5_spmd.sunk | while | flops 65538 | bytes 1048677 | solution.py:136
  1128.6 502.3 %while.86 = (s32[]{:T(128)}, f32[64,16,2048]{2,1,0:T(8,128)}, f32[64,16,2048]{2,1,0:T(8,128)}, f32[16,64,16,2048]{3,2,1,0:T(8,128)}, s32[16]{0:T(128)S(1)}, /*in...) while((s32[]{:T(128)}, f32[64,16,2048]{2,1,0:T(8,128)}, ...), condition=%wide.region_8.9_spmd, body=%wide.region_6.8_spmd.sunk | while | flops 12451845 | bytes 39477944 | solution.py:150
  1645.0 21.4 pad.186
  1688.2 21.1 pad.198
  1728.8 50.1 %while.87 = (s32[]{:T(128)}, f32[16,2048]{1,0:T(8,128)S(1)}, f32[16,2048]{1,0:T(8,128)S(1)}, f32[16,2048]{1,0:T(8,128)S(1)}, s32[]{:T(128)}) while((s32[]{:T(128)}, f32[16,2048]{1,0:T(8,128)S(1)}, f32[16,2048]{1,0:T(8,128)S(1)}, f32[16,2048]{1,0:T(8,128)S(1)}, s32[]{:T(128)}) %tuple.254), condition=%wide.region_12.13_spmd, body=%wide.region_11.12_spmd.sunk | while | flops 65538 | bytes 1048677 | solution.py:179
  1799.6 698.3 %while.90 = (s32[]{:T(128)}, f32[64,16,2048]{2,1,0:T(8,128)}, f32[16,2048]{1,0:T(8,128)S(1)}, f32[64,16,2048]{2,1,0:T(8,128)}, f32[64,16,2048]{2,1,0:T(8,128)}, ...) while((s32[]{:T(128)}, f32[64,16,2048]{2,1,0:T(8,128)}, ...), condition=%wide.region_19.20_spmd.clone, body=%wide.region_13.19_spmd.clone.sunk | while | flops 40007684 | bytes 39022876 | solution.py:211
  1805.5 13.8 multiply_reduce_fusion.14
  1936.3 13.8 multiply_reduce_fusion.14
  2067.2 13.8 multiply_reduce_fusion.14
  2285.4 13.8 multiply_reduce_fusion.14
  2329.0 13.8 multiply_reduce_fusion.14
  2513.6 36.7 %fusion.75 = (f32[2048]{0:T(1024)}, f32[2048]{0:T(1024)}, f32[2048]{0:T(1024)}, f32[2048]{0:T(1024)}, f32[2048]{0:T(1024)}, /*index=5*/bf16[1024,2048]{1,0:T(8,1...) fusion(f32[1024,4096]{1,0:T(8,128)} %copy-done.4, f32[1023,2048]{1,0:T(8,128)} %slice.604, f32[1,2048]{1,0:T(1,128)} %copy-done.78, ...), kind=kOutput, calls=%fused_computation.255 | convolution fusion | flops 485021696 | bytes 105496576 | tf_op jit(solution)/shard_map/dot_general | solution.py:230
  2600.6 16.9 convolution_bitcast_fusion
  2617.5 14.9 fusion.26
  2676.8 403.8 %all-reduce.55.cloned.1.call-done = f32[6667264]{0:T(1024)} async-done(((f32[6667264]{0:T(1024)}), f32[6667264]{0:T(1024)}) %all-reduce.55.cloned.1.call-update) | async-done | bytes 26669072
  3082.7 40.0 %psum.7 = f32[]{:T(128)} all-reduce(f32[]{:T(128)} %get-tuple-element.941), channel_id=1, replica_groups=mesh['batch'=4,'blk'=8] {'batch','blk'}, use_global_device_ids=true, to_apply=%region_31.32 | all-reduce | flops 1 | bytes 8 | tf_op jit(solution)/shard_map/psum | solution.py:270
  (898 shorter events, 2083.1 us)
Async XLA Ops:
  7.2 3073.5 %all-reduce.55.cloned.1.call-start = ((), (), s32[]{:S(2)}) async-start(), calls=%async_computation | async-start | bytes 53338112
  27.7 75.5 %collective-permute-start.2 = (f32[3,2048]{1,0:T(4,128)S(1)}, f32[3,2048]{1,0:T(4,128)S(1)}, u32[]{:S(2)}, u32[]{:S(2)}) collective-permute-start(f32[3,2048]{1,0:T(4,128)S(1)} %slice.599), channel_id=1, source_target_pairs={{0,1},{1,2},{2,3},{3,4},{4,5},{5,6},{6,7},{8,9},{9,10},{10,11},{11... | collective-permute-start | bytes 73736 | tf_op jit(solution)/shard_map/ppermute | solution.py:21
  42.3 60.9 %copy-start.59 = (f32[1,2048]{1,0:T(1,128)}, f32[1,2048]{1,0:T(1,128)S(1)}, u32[]{:S(2)}) copy-start(f32[1,2048]{1,0:T(1,128)S(1)} %get-tuple-element.1035) | copy-start | bytes 24580
  42.3 60.9 %copy-start.61 = (f32[1,2048]{1,0:T(1,128)}, f32[1,2048]{1,0:T(1,128)S(1)}, u32[]{:S(2)}) copy-start(f32[1,2048]{1,0:T(1,128)S(1)} %get-tuple-element.1036) | copy-start | bytes 24580
  42.3 60.9 %copy-start.63 = (f32[1,2048]{1,0:T(1,128)}, f32[1,2048]{1,0:T(1,128)S(1)}, u32[]{:S(2)}) copy-start(f32[1,2048]{1,0:T(1,128)S(1)} %get-tuple-element.1037) | copy-start | bytes 24580
  42.4 60.9 %copy-start.65 = (f32[1,2048]{1,0:T(1,128)}, f32[1,2048]{1,0:T(1,128)S(1)}, u32[]{:S(2)}) copy-start(f32[1,2048]{1,0:T(1,128)S(1)} %get-tuple-element.1038) | copy-start | bytes 24580
  103.2 24.9 copy-start.67
  103.2 24.9 copy-start.73
  103.3 24.8 copy-start.78
  753.6 20.9 slice-start
  829.5 21.2 copy-start.20
  829.5 28.6 copy-start.49
  1074.0 5.5 collective-permute-start
  1079.5 3.9 collective-permute-start
  1083.3 6.3 collective-permute-start
  1089.6 6.3 collective-permute-start
  1096.0 6.3 collective-permute-start
  1102.3 6.3 collective-permute-start
  1108.6 6.3 collective-permute-start
  1728.8 6.2 collective-permute-start.1
  1735.0 7.3 collective-permute-start.1
  1742.3 7.0 collective-permute-start.1
  1749.4 7.9 collective-permute-start.1
  1757.3 7.2 collective-permute-start.1
  1764.5 7.2 collective-permute-start.1
  1771.7 7.2 collective-permute-start.1
  1799.6 698.3 %copy-start.58 = (f32[2048]{0:T(1024)S(1)}, f32[2048]{0:T(1024)}, u32[]{:S(2)}) copy-start(f32[2048]{0:T(1024)} %param.34) | copy-start | bytes 24580
  2513.6 39.5 %copy-start.44 = (f32[16,2048]{1,0:T(8,128)S(1)}, f32[16,2048]{1,0:T(8,128)}, u32[]{:S(2)}) copy-start(f32[16,2048]{1,0:T(8,128)} %param.35) | copy-start | bytes 393220
  2513.6 40.1 %copy-start.35 = (bf16[1,1024,1024]{2,1,0:T(8,128)(2,1)S(1)}, bf16[1,1024,1024]{2,1,0:T(8,128)(2,1)}, u32[]{:S(2)}) copy-start(bf16[1,1024,1024]{2,1,0:T(8,128)(2,1)} %param.27) | copy-start | bytes 6291460
  2551.7 34.6 %collective-permute-start.3 = (f32[3,2048]{1,0:T(4,128)}, f32[3,2048]{1,0:T(4,128)}, u32[]{:S(2)}, u32[]{:S(2)}) collective-permute-start(f32[3,2048]{1,0:T(4,128)} %slice.688), channel_id=1, source_target_pairs={{1,0},{2,1},{3,2},{4,3},{5,4},{6,5},{7,6},{9,8},{10,9},{11,10},{12... | collective-permute-start | bytes 73736 | tf_op jit(solution)/shard_map/ppermute | solution.py:21
  2674.4 449.0 %copy-start.47 = (f32[208352]{0:T(1024)S(1)}, f32[208352]{0:T(1024)}, u32[]{:S(2)}) copy-start(f32[208352]{0:T(1024)} %param.38) | copy-start | bytes 2500228
  3082.7 44.6 %copy-start.33 = (f32[208352]{0:T(1024)}, f32[208352]{0:T(1024)S(1)}, u32[]{:S(2)}) copy-start(f32[208352]{0:T(1024)S(1)} %get-tuple-element.942) | copy-start | bytes 2500228
  (81 other events, 793.4 us)
Sparse Core Ops, SparseCore 0:
  2659.1 421.4 all-reduce.54
where the time goes:
time: 3170 us; the launch traced here: 3140 us
  local copies, waits for them, and re-layouts  1420 us (45%)
  other arithmetic  890 us (28%)
  waiting for transfers between devices  451 us (14%)
  matrix products  141 us (4%)
  loops' own time  127 us (4%)
  starting transfers between devices  46.8 us (1%)
  blocking collectives  40 us (1%)
    dynamic_update_slice x112, local copies, waits for them, and re-layouts, place_row(): return lax.dynamic_update_index_in_dim(buffer, row[:, None], index, 1)  536 us
    unnamed x2, waiting for transfers between devices  404 us
    pad x40, local copies, waits for them, and re-layouts, sub_prefix(): inc_decay, inc_state = lax.associative_scan(link, (totals, ends))  314 us
    reduce_sum x16, other arithmetic, exact_back(): grad_step = jnp.sum(through * rates, 1) + conv_row * feed  221 us
    unnamed x226, local copies, waits for them, and re-layouts  180 us
    reduce_sum x16, other arithmetic, exact_step(): jnp.sum(pick(readout_rows, index)[:, :, None] * fresh, 1)  125 us
    dynamic_update_slice x16, local copies, waits for them, and re-layouts, local(): lax.scan(exact_step, (starts, jnp.zeros((count, sub_len, inner), f32)), p...  125 us
    add x16, other arithmetic, local_step(): jnp.exp(pick(step_rows, index)[:, None, :] * rates) * carry  105 us
  transfers between devices with their start and end apart: 17, of which 15 were waited for; matrix products, arithmetic and copies ran while one was open for 4% of the time, Pallas kernels for 0%

commit v1 on v0

v1 whole, which is shorter than its diff:
```python
import functools
import math

import jax
import jax.numpy as jnp
from jax import lax
from jax.experimental import pallas as pl
from jax.experimental.pallas import tpu as pltpu
from jax.sharding import PartitionSpec as P

ADAM_STEP = 100
EPS = 1e-05
RATE = 0.002
BETA_ONE = 0.9
BETA_TWO = 0.95
ADAM_EPS = 1e-08
DECAY = 0.1
CLIP = 1.0

LOG2E = 1.0 / math.log(2.0)
LN2 = math.log(2.0)
SUB = 8
LANE = 128
ROW = 1024
VMEM_BYTES = 56 * 2**20

MESH = pl.DeviceIdType.MESH

f32 = jnp.float32
bf16 = jnp.bfloat16


def shifted(x, axis, by):
    count = lax.axis_size(axis)
    pairs = [(i, i + by) for i in range(count) if 0 <= i + by < count]
    return lax.ppermute(x, axis, pairs)


def silu_slope(value):
    sig = jax.nn.sigmoid(value)
    return sig * (1.0 + value * (1.0 - sig))


def interleave(x):
    rows, width = x.shape
    return x.reshape(SUB, rows // SUB, width).transpose(1, 0, 2).reshape(rows, width)


def restore(x):
    rows, width = x.shape
    return x.reshape(rows // SUB, SUB, width).transpose(1, 0, 2).reshape(rows, width)


def at(start, size):
    return pl.ds(pl.multiple_of(start, size), size)


def spread(sel_ref, base, state, tiles, out_ref):
    def one(i, carry):
        tile = sel_ref[at(i * SUB, SUB), :]
        for n in range(state):
            out_ref[at((i * state + n) * SUB, SUB), :] = jnp.broadcast_to(
                tile[:, base + n : base + n + 1], (SUB, LANE)
            )
        return carry

    lax.fori_loop(0, tiles, one, 0)


def gather_lanes(src_ref, state, tiles, out_ref):
    lane = lax.broadcasted_iota(jnp.int32, (SUB, LANE), 1)

    def one(i, carry):
        total = jnp.zeros((SUB, LANE), f32)
        for n in range(state):
            part = jnp.sum(src_ref[at((i * state + n) * SUB, SUB), :], axis=1, keepdims=True)
            total = jnp.where(lane == n, part, total)
        out_ref[at(i * SUB, SUB), :] = total
        return carry

    lax.fori_loop(0, tiles, one, 0)


def summary_kernel(
    shape,
    step_ref,
    drive_ref,
    grad_ref,
    sel_ref,
    rates_ref,
    pre_decay_ref,
    pre_state_ref,
    post_decay_ref,
    post_state_ref,
    totals_ref,
    end_ref,
    exit_ref,
    prod_ref,
    inject_ref,
    readout_ref,
):
    tiles, state, inner, rank, cols, group = shape
    turn = pl.program_id(0)

    @pl.when(turn == 0)
    def _():
        end_ref[...] = jnp.zeros_like(end_ref)
        exit_ref[...] = jnp.zeros_like(exit_ref)
        prod_ref[...] = jnp.ones_like(prod_ref)

    spread(sel_ref, rank, state, tiles, inject_ref)
    spread(sel_ref, rank + state, state, tiles, readout_ref)

    def columns(c, carry):
        lanes = [at((c * cols + k) * LANE, LANE) for k in range(cols)]
        for first in range(0, state, group):
            spots = [(n, k) for n in range(group) for k in range(cols)]
            where = [(slice((first + n) * SUB, (first + n + 1) * SUB), lanes[k]) for n, k in spots]
            rates = [rates_ref[w] for w in where]

            def advance(i, carry):
                ends, exits, prods = carry
                here = at(i * SUB, SUB)
                step = [step_ref[here, l] for l in lanes]
                drive = [drive_ref[here, l] for l in lanes]
                grad = [grad_ref[here, l] for l in lanes]
                inject = [inject_ref[at((i * state + first + n) * SUB, SUB), :] for n in range(group)]
                readout = [readout_ref[at((i * state + first + n) * SUB, SUB), :] for n in range(group)]
                new = ([], [], [])
                for s, (n, k) in enumerate(spots):
                    decay = jnp.exp2(step[k] * rates[s])
                    prod = prods[s] * decay
                    new[0].append(ends[s] * decay + drive[k] * inject[n])
                    new[1].append(exits[s] + prod * (grad[k] * readout[n]))
                    new[2].append(prod)
                return tuple(tuple(x) for x in new)

            start = tuple(tuple(ref[w] for w in where) for ref in (end_ref, exit_ref, prod_ref))
            ends, exits, prods = lax.fori_loop(0, tiles, advance, start, unroll=8)
            for s, w in enumerate(where):
                end_ref[w] = ends[s]
                exit_ref[w] = exits[s]
                prod_ref[w] = prods[s]
        return carry

    lax.fori_loop(0, inner // (LANE * cols), columns, 0)

    @pl.when(turn == pl.num_programs(0) - 1)
    def _():
        row = lax.broadcasted_iota(jnp.int32, (SUB, LANE), 0)

        def columns(c, carry):
            lanes = at(c * LANE, LANE)
            for n in range(state):
                here = (slice(n * SUB, (n + 1) * SUB), lanes)
                for way, src, decay_out, state_out, total_row in (
                    (1, end_ref, pre_decay_ref, pre_state_ref, 1),
                    (-1, exit_ref, post_decay_ref, post_state_ref, 2),
                ):
                    decay, value = prod_ref[here], src[here]

                    def seen(by):
                        return row >= by if way > 0 else row < SUB - by

                    for by in (1, 2, 4):
                        far_decay = pltpu.roll(decay, by if way > 0 else SUB - by, 0)
                        far_value = pltpu.roll(value, by if way > 0 else SUB - by, 0)
                        value = jnp.where(seen(by), value + decay * far_value, value)
                        decay = jnp.where(seen(by), decay * far_decay, decay)
                    last = SUB - 1 if way > 0 else 0
                    totals_ref[pl.ds(n, 1), lanes] = decay[last : last + 1]
                    totals_ref[pl.ds(total_row * state + n, 1), lanes] = value[last : last + 1]
                    turn_by = 1 if way > 0 else SUB - 1
                    decay_out[here] = jnp.where(seen(1), pltpu.roll(decay, turn_by, 0), 1.0)
                    state_out[here] = jnp.where(seen(1), pltpu.roll(value, turn_by, 0), 0.0)
            return carry

        lax.fori_loop(0, inner // LANE, columns, 0)


def forward_kernel(
    shape,
    step_ref,
    drive_ref,
    grad_ref,
    sel_ref,
    rates_ref,
    pre_decay_ref,
    pre_state_ref,
    entry_ref,
    scanned_ref,
    prior_ref,
    readout_grad_ref,
    state_ref,
    inject_ref,
    readout_ref,
    sums_ref,
):
    tiles, state, inner, rank, cols, group = shape

    @pl.when(pl.program_id(0) == 0)
    def _():
        for n in range(state):
            here = slice(n * SUB, (n + 1) * SUB)
            state_ref[here, :] = pre_state_ref[here, :] + pre_decay_ref[here, :] * entry_ref[n : n + 1, :]

    spread(sel_ref, rank, state, tiles, inject_ref)
    spread(sel_ref, rank + state, state, tiles, readout_ref)
    sums_ref[...] = jnp.zeros_like(sums_ref)

    def columns(c, carry):
        lanes = [at((c * cols + k) * LANE, LANE) for k in range(cols)]
        for first in range(0, state, group):
            spots = [(n, k) for n in range(group) for k in range(cols)]
            where = [(slice((first + n) * SUB, (first + n + 1) * SUB), lanes[k]) for n, k in spots]
            rates = [rates_ref[w] for w in where]

            def advance(i, states):
                here = at(i * SUB, SUB)
                step = [step_ref[here, l] for l in lanes]
                drive = [drive_ref[here, l] for l in lanes]
                grad = [grad_ref[here, l] for l in lanes]
                outs = [None] * cols
                new = []
                for n in range(group):
                    spot = at((i * state + first + n) * SUB, SUB)
                    inject = inject_ref[spot, :]
                    readout = readout_ref[spot, :]
                    total = None
                    for k in range(cols):
                        s = n * cols + k
                        decay = jnp.exp2(step[k] * rates[s])
                        fresh = decay * states[s] + drive[k] * inject
                        new.append(fresh)
                        part = readout * fresh
                        outs[k] = part if outs[k] is None else outs[k] + part
                        part = grad[k] * fresh
                        total = part if total is None else total + part
                    sums_ref[spot, :] += total
                    if n % 2 == 1:
                        pair = pl.ds(pl.multiple_of((i * state + first + n - 1) * SUB, 2 * SUB), 2 * SUB)
                        for k in range(cols):
                            prior_ref[pair, lanes[k]] = jnp.concatenate(
                                [states[(n - 1) * cols + k], states[n * cols + k]], 0
                            ).astype(bf16)
                for k in range(cols):
                    if first == 0:
                        scanned_ref[here, lanes[k]] = outs[k]
                    else:
                        scanned_ref[here, lanes[k]] += outs[k]
                return tuple(new)

            states = lax.fori_loop(0, tiles, advance, tuple(state_ref[w] for w in where), unroll=4)
            for s, w in enumerate(where):
                state_ref[w] = states[s]
        return carry

    lax.fori_loop(0, inner // (LANE * cols), columns, 0)
    gather_lanes(sums_ref, state, tiles, readout_grad_ref)


def backward_kernel(
    shape,
    step_ref,
    drive_ref,
    grad_ref,
    sel_ref,
    rates_ref,
    post_decay_ref,
    post_state_ref,
    arriving_ref,
    prior_ref,
    through_ref,
    feed_ref,
    inject_grad_ref,
    rate_grad_ref,
    carry_ref,
    inject_ref,
    readout_ref,
    sums_ref,
):
    tiles, state, inner, rank, cols, group = shape

    @pl.when(pl.program_id(0) == 0)
    def _():
        rate_grad_ref[...] = jnp.zeros_like(rate_grad_ref)
        for n in range(state):
            here = slice(n * SUB, (n + 1) * SUB)
            carry_ref[here, :] = post_state_ref[here, :] + post_decay_ref[here, :] * arriving_ref[n : n + 1, :]

    spread(sel_ref, rank, state, tiles, inject_ref)
    spread(sel_ref, rank + state, state, tiles, readout_ref)
    sums_ref[...] = jnp.zeros_like(sums_ref)

    def columns(c, carry):
        lanes = [at((c * cols + k) * LANE, LANE) for k in range(cols)]
        for first in range(0, state, group):
            spots = [(n, k) for n in range(group) for k in range(cols)]
            where = [(slice((first + n) * SUB, (first + n + 1) * SUB), lanes[k]) for n, k in spots]
            rates = [rates_ref[w] for w in where]

            def retreat(turn, carry):
                carries, rate_grads = carry
                i = tiles - 1 - turn
                here = at(i * SUB, SUB)
                step = [step_ref[here, l] for l in lanes]
                drive = [drive_ref[here, l] for l in lanes]
                grad = [grad_ref[here, l] for l in lanes]
                throughs = [None] * cols
                feeds = [None] * cols
                new = ([], [])
                for n in range(group):
                    spot = at((i * state + first + n) * SUB, SUB)
                    inject = inject_ref[spot, :]
                    readout = readout_ref[spot, :]
                    if n % 2 == 0:
                        pair = pl.ds(pl.multiple_of((i * state + first + n) * SUB, 2 * SUB), 2 * SUB)
                        pairs = [prior_ref[pair, lanes[k]].astype(f32) for k in range(cols)]
                    total = None
                    for k in range(cols):
                        s = n * cols + k
                        prior = pairs[k][(n % 2) * SUB : (n % 2 + 1) * SUB]
                        power = step[k] * rates[s]
                        adjoint = grad[k] * readout + carries[s]
                        back = jnp.exp2(power) * adjoint
                        through = back * prior * power
                        new[0].append(back)
                        new[1].append(rate_grads[s] + through)
                        throughs[k] = through if throughs[k] is None else throughs[k] + through
                        part = adjoint * inject
                        feeds[k] = part if feeds[k] is None else feeds[k] + part
                        part = adjoint * drive[k]
                        total = part if total is None else total + part
                    sums_ref[spot, :] += total
                for k in range(cols):
                    if first == 0:
                        through_ref[here, lanes[k]] = throughs[k]
                        feed_ref[here, lanes[k]] = feeds[k]
                    else:
                        through_ref[here, lanes[k]] += throughs[k]
                        feed_ref[here, lanes[k]] += feeds[k]
                return tuple(tuple(x) for x in new)

            start = tuple(tuple(ref[w] for w in where) for ref in (carry_ref, rate_grad_ref))
            carries, rate_grads = lax.fori_loop(0, tiles, retreat, start, unroll=4)
            for s, w in enumerate(where):
                carry_ref[w] = carries[s]
                rate_grad_ref[w] = rate_grads[s]
        return carry

    lax.fori_loop(0, inner // (LANE * cols), columns, 0)
    gather_lanes(sums_ref, state, tiles, inject_grad_ref)


def scan_shapes(rows, state, inner):
    tiles = min(16, rows // SUB)
    count = rows // (SUB * tiles)
    return tiles, count


def summary_call(step, drive, grad, sel, rates, rank):
    rows, inner = step.shape
    state = rates.shape[0] // SUB
    tiles, count = scan_shapes(rows, state, inner)
    wide = pl.BlockSpec((tiles * SUB, inner), lambda t: (t, 0))
    thin = pl.BlockSpec((tiles * SUB, sel.shape[1]), lambda t: (t, 0))
    whole = pl.BlockSpec((state * SUB, inner), lambda t: (0, 0))
    total = pl.BlockSpec((3 * state, inner), lambda t: (0, 0))
    shape = (tiles, state, inner, rank, 2, 4)
    big = jax.ShapeDtypeStruct((state * SUB, inner), f32)
    return pl.pallas_call(
        functools.partial(summary_kernel, shape),
        name="scan_summary",
        grid=(count,),
        in_specs=[wide, wide, wide, thin, whole],
        out_specs=[whole] * 4 + [total],
        out_shape=[big] * 4 + [jax.ShapeDtypeStruct((3 * state, inner), f32)],
        scratch_shapes=[pltpu.VMEM((state * SUB, inner), f32)] * 3
        + [pltpu.VMEM((tiles * state * SUB, LANE), f32)] * 2,
        compiler_params=pltpu.CompilerParams(vmem_limit_bytes=VMEM_BYTES),
    )(step, drive, grad, sel, rates)


def forward_call(step, drive, grad, sel, rates, pre_decay, pre_state, entry, rank):
    rows, inner = step.shape
    state = rates.shape[0] // SUB
    tiles, count = scan_shapes(rows, state, inner)
    wide = pl.BlockSpec((tiles * SUB, inner), lambda t: (t, 0))
    thin = pl.BlockSpec((tiles * SUB, sel.shape[1]), lambda t: (t, 0))
    whole = pl.BlockSpec((state * SUB, inner), lambda t: (0, 0), pipeline_mode=pl.Buffered(1))
    short = pl.BlockSpec((state, inner), lambda t: (0, 0))
    shape = (tiles, state, inner, rank, 2, 8)
    return pl.pallas_call(
        functools.partial(forward_kernel, shape),
        name="scan_forward",
        grid=(count,),
        in_specs=[wide, wide, wide, thin, whole, whole, whole, short],
        out_specs=[
            wide,
            pl.BlockSpec((tiles * state * SUB, inner), lambda t: (t, 0)),
            pl.BlockSpec((tiles * SUB, LANE), lambda t: (t, 0)),
        ],
        out_shape=[
            jax.ShapeDtypeStruct((rows, inner), f32),
            jax.ShapeDtypeStruct((rows * state, inner), bf16),
            jax.ShapeDtypeStruct((rows, LANE), f32),
        ],
        scratch_shapes=[pltpu.VMEM((state * SUB, inner), f32)]
        + [pltpu.VMEM((tiles * state * SUB, LANE), f32)] * 3,
        compiler_params=pltpu.CompilerParams(vmem_limit_bytes=VMEM_BYTES),
    )(step, drive, grad, sel, rates, pre_decay, pre_state, entry)


def backward_call(step, drive, grad, sel, rates, post_decay, post_state, arriving, prior, rank):
    rows, inner = step.shape
    state = rates.shape[0] // SUB
    tiles, count = scan_shapes(rows, state, inner)

    def back(t):
        return (count - 1 - t, 0)

    wide = pl.BlockSpec((tiles * SUB, inner), back)
    thin = pl.BlockSpec((tiles * SUB, sel.shape[1]), back)
    whole = pl.BlockSpec((state * SUB, inner), lambda t: (0, 0), pipeline_mode=pl.Buffered(1))
    short = pl.BlockSpec((state, inner), lambda t: (0, 0))
    shape = (tiles, state, inner, rank, 2, 4)
    return pl.pallas_call(
        functools.partial(backward_kernel, shape),
        name="scan_backward",
        grid=(count,),
        in_specs=[wide, wide, wide, thin, whole, whole, whole, short]
        + [pl.BlockSpec((tiles * state * SUB, inner), back)],
        out_specs=[
            wide,
            wide,
            pl.BlockSpec((tiles * SUB, LANE), back),
            pl.BlockSpec((state * SUB, inner), lambda t: (0, 0)),
        ],
        out_shape=[
            jax.ShapeDtypeStruct((rows, inner), f32),
            jax.ShapeDtypeStruct((rows, inner), f32),
            jax.ShapeDtypeStruct((rows, LANE), f32),
            jax.ShapeDtypeStruct((state * SUB, inner), f32),
        ],
        scratch_shapes=[pltpu.VMEM((state * SUB, inner), f32)]
        + [pltpu.VMEM((tiles * state * SUB, LANE), f32)] * 3,
        compiler_params=pltpu.CompilerParams(vmem_limit_bytes=VMEM_BYTES),
    )(step, drive, grad, sel, rates, post_decay, post_state, arriving, prior)


def flatten_kernel(rows_in, rows_out, in_base, small_base, out_base, stream_ref, gate_ref, out_w_ref, gain_ref, small_ref, flat_ref, in_buf, out_buf, sems):
    turn = pl.program_id(0)
    count = pl.num_programs(0)
    slot = turn % 2
    half = stream_ref.shape[1] // LANE
    wide = 2 * half

    def copies(step, slot):
        size_in, size_out = rows_in * wide // SUB, rows_out
        return (
            pltpu.make_async_copy(
                in_buf.at[slot], flat_ref.at[pl.ds(in_base + step * size_in, size_in)], sems.at[slot]
            ),
            pltpu.make_async_copy(
                out_buf.at[slot], flat_ref.at[pl.ds(out_base + step * size_out, size_out)], sems.at[2 + slot]
            ),
        )

    def extras():
        return (
            pltpu.make_async_copy(gain_ref, flat_ref.at[pl.ds(0, gain_ref.shape[0])], sems.at[4]),
            pltpu.make_async_copy(
                small_ref, flat_ref.at[pl.ds(small_base, small_ref.shape[0])], sems.at[5]
            ),
        )

    @pl.when(turn == 0)
    def _():
        for copy in extras():
            copy.start()

    @pl.when(turn >= 2)
    def _():
        for copy in copies(turn - 2, slot):
            copy.wait()

    for r in range(rows_in // SUB):
        rows = slice(r * SUB, (r + 1) * SUB)
        for a in range(wide):
            src = stream_ref if a < half else gate_ref
            tile = src[rows, (a % half) * LANE : (a % half + 1) * LANE]
            for_tile = in_buf.at[slot, r * wide : (r + 1) * wide]
            for_tile[pl.ds(a // SUB, SUB, stride=wide // SUB), a % SUB, :] = tile
    deep = out_w_ref.shape[1] // LANE
    for r in range(rows_out // SUB):
        rows = slice(r * SUB, (r + 1) * SUB)
        for a in range(deep):
            out_buf[slot, rows, a, :] = out_w_ref[rows, a * LANE : (a + 1) * LANE]
    for copy in copies(turn, slot):
        copy.start()

    @pl.when(turn == count - 1)
    def _():
        for copy in copies(turn - 1, 1 - slot):
            copy.wait()
        for copy in copies(turn, slot):
            copy.wait()
        for copy in extras():
            copy.wait()


def flatten_call(stream, gate, out_w, gain, small, total):
    depth, half = stream.shape
    steps = 16
    rows_in, rows_out = depth // steps, out_w.shape[0] // steps
    wide = 2 * half // LANE
    in_base = gain.shape[0]
    small_base = in_base + depth * wide // SUB
    out_base = small_base + small.shape[0]
    return pl.pallas_call(
        functools.partial(flatten_kernel, rows_in, rows_out, in_base, small_base, out_base),
        name="flatten",
        grid=(steps,),
        in_specs=[
            pl.BlockSpec((rows_in, half), lambda t: (t, 0)),
            pl.BlockSpec((rows_in, half), lambda t: (t, 0)),
            pl.BlockSpec((rows_out, out_w.shape[1]), lambda t: (t, 0)),
            pl.BlockSpec(memory_space=pl.ANY),
            pl.BlockSpec(memory_space=pl.ANY),
        ],
        out_specs=pl.BlockSpec(memory_space=pl.ANY),
        out_shape=jax.ShapeDtypeStruct((total, SUB, LANE), f32),
        scratch_shapes=[
            pltpu.VMEM((2, rows_in * wide // SUB, SUB, LANE), f32),
            pltpu.VMEM((2, rows_out, SUB, LANE), f32),
            pltpu.SemaphoreType.DMA((6,)),
        ],
        compiler_params=pltpu.CompilerParams(vmem_limit_bytes=VMEM_BYTES),
    )(stream, gate, out_w, gain, small)


def reduce_kernel(
    depth,
    bits,
    phases,
    half,
    span,
    flat_ref,
    out_ref,
    norm_ref,
    acc,
    first_recv,
    *rest,
):
    n = bits - 1
    bit_recvs = rest[:n]
    down_recv, up_recv, ring, sums, square_ref = rest[n : n + 5]
    local_sem, core_send, core_recv, bit_send, bit_recv, z_send, z_recv, ring_send, ring_recv = rest[n + 5 :]
    blk = lax.axis_index("blk")
    z = lax.axis_index("batch")
    mine = [(blk // 2**b) % 2 for b in range(bits)]
    partner = [blk + (1 - 2 * mine[b]) * 2**b for b in range(bits)]
    below, above = (z + depth - 1) % depth, (z + 1) % depth
    barrier = pltpu.get_barrier_semaphore()
    for b in range(bits):
        pl.semaphore_signal(barrier, inc=1, device_id={"blk": partner[b]}, device_id_type=MESH)
    for other in (below, above):
        pl.semaphore_signal(barrier, inc=1, device_id={"batch": other}, device_id_type=MESH)
    pl.semaphore_wait(barrier, bits + 2)

    def digits(r):
        return tuple((r // 2**i) % 2 for i in reversed(range(n)))

    def window(r, core, zz, p):
        owner = zz * 2**bits + 2 * r + core
        return pl.ds((owner * span) // ROW + p * 2 * half, 2 * half)

    def core_copies(p, own_too=True):
        remote, own = [], []
        for r in range(2**n):
            for zz in range(depth):
                at_slot = (p,) + digits(r) + (zz,)
                spot = (p * 2**n + r) * depth + zz
                remote.append(
                    pltpu.make_async_remote_copy(
                        src_ref=flat_ref.at[window(r, 1 - mine[0], zz, p)],
                        dst_ref=first_recv.at[at_slot],
                        send_sem=core_send.at[spot],
                        recv_sem=core_recv.at[spot],
                        device_id={"blk": partner[0]},
                        device_id_type=MESH,
                    )
                )
                if own_too:
                    own.append(
                        pltpu.make_async_copy(
                            flat_ref.at[window(r, mine[0], zz, p)], acc.at[at_slot], local_sem.at[spot]
                        )
                    )
        return remote, own

    def order(part):
        return list(range(n)) if part == 0 else list(reversed(range(n)))

    def place(p, part, done, pick):
        spots = [slice(None)] * n
        for i in order(part)[:done]:
            spots[i] = mine[i + 1]
        if pick is not None:
            spots[order(part)[done]] = pick
        return (p,) + tuple(reversed(spots)) + (slice(None), slice(part * half, (part + 1) * half))

    def bit_copies(p, s):
        copies = []
        for part in range(2):
            i = order(part)[s]
            spot = (p * n + s) * 2 + part
            copies.append(
                pltpu.make_async_remote_copy(
                    src_ref=acc.at[place(p, part, s, 1 - mine[i + 1])],
                    dst_ref=bit_recvs[s].at[p, part],
                    send_sem=bit_send.at[spot],
                    recv_sem=bit_recv.at[spot],
                    device_id={"blk": partner[i + 1]},
                    device_id_type=MESH,
                )
            )
        return copies

    settled = tuple(reversed([mine[i + 1] for i in range(n)]))

    def z_moves(p, u):
        down = u - (depth - 1 - z)
        up = depth - 1 - (u - z)
        spot = (p * (depth - 1) + u) * 2
        return (
            (
                (down >= 0) & (down < z),
                lax.max(down, 0),
                z < depth - 1,
                down_recv,
                below,
                spot,
            ),
            (
                (u >= z) & (up > z),
                lax.min(up, depth - 1),
                z > 0,
                up_recv,
                above,
                spot + 1,
            ),
        )

    def z_copy(p, goal, recv, to, spot):
        return pltpu.make_async_remote_copy(
            src_ref=acc.at[(p,) + settled + (goal,)],
            dst_ref=recv.at[p, goal],
            send_sem=z_send.at[spot],
            recv_sem=z_recv.at[0 if recv is down_recv else 1, p, goal],
            device_id={"batch": to},
            device_id_type=MESH,
        )

    def z_wait(p, goal, recv):
        z_copy(p, goal, recv, below if recv is down_recv else above, 0).wait_recv()

    def add_windows(p):
        remote, own = core_copies(p)
        for copy in own:
            copy.wait()
        for copy in remote:
            copy.wait_recv()
        for r in range(2**n):

            def one(zz, carry):
                at_slot = (p,) + digits(r) + (zz,)
                acc[at_slot] += first_recv[at_slot]
                return carry

            lax.fori_loop(0, depth, one, 0)

    def add_bits(p, s):
        for part, copy in enumerate(bit_copies(p, s)):
            copy.wait_recv()
            kept = place(p, part, s, mine[order(part)[s] + 1])
            free = [i for i, v in enumerate(kept[1 : 1 + n]) if isinstance(v, slice)]
            for r in range(2 ** len(free)):
                chosen = [(r // 2**j) % 2 for j in reversed(range(len(free)))]
                to = list(kept)
                for i, v in zip(free, chosen):
                    to[1 + i] = v

                def one(zz, carry):
                    dst = tuple(to[: 1 + n]) + (zz, to[-1])
                    acc[dst] += bit_recvs[s][(p, part) + tuple(chosen) + (zz,)]
                    return carry

                lax.fori_loop(0, depth, one, 0)

    last = n + depth - 1
    for t in range(phases + last + 1):
        for stage in reversed(range(last + 1)):
            p = t - stage
            if not 0 <= p < phases:
                continue
            if stage == 0:
                remote, own = core_copies(p)
                for copy in remote + own:
                    copy.start()
            elif stage <= n:
                if stage == 1:
                    add_windows(p)
                else:
                    add_bits(p, stage - 2)
                for copy in bit_copies(p, stage - 1):
                    copy.start()
            else:
                u = stage - n - 1
                if u == 0:
                    if n == 0:
                        add_windows(p)
                    else:
                        add_bits(p, n - 1)
                for cond, goal, relays, recv, to, spot in z_moves(p, u):

                    @pl.when(cond)
                    def _():
                        @pl.when(relays)
                        def _():
                            z_wait(p, goal, recv)
                            acc[(p,) + settled + (goal,)] += recv[p, goal]

                        z_copy(p, goal, recv, to, spot).start()

    square_ref[...] = jnp.zeros_like(square_ref)
    index = blk + z * 2**bits
    low = (index * span) % ROW
    inside = lax.broadcasted_iota(jnp.int32, (SUB, LANE), 0) * LANE + lax.broadcasted_iota(
        jnp.int32, (SUB, LANE), 1
    )
    for p in range(phases):
        for recv, here in ((down_recv, z < depth - 1), (up_recv, z > 0)):

            @pl.when(here)
            def _():
                z_wait(p, z, recv)
                acc[(p,) + settled + (z,)] += recv[p, z]

        def one(i, carry):
            value = acc[(p,) + settled + (z, i)]
            out_ref[p * 2 * half + i] = value
            spot = inside + (p * 2 * half + i) * ROW
            held = jnp.where((spot >= low) & (spot < low + span), value, 0.0)
            square_ref[...] += held * held
            return carry

        lax.fori_loop(0, 2 * half, one, 0)

    sums[0] = square_ref[...]
    for b in range(bits):
        copy = pltpu.make_async_remote_copy(
            src_ref=sums.at[b],
            dst_ref=sums.at[bits + 1 + b],
            send_sem=ring_send.at[b],
            recv_sem=ring_recv.at[b],
            device_id={"blk": partner[b]},
            device_id_type=MESH,
        )
        copy.start()
        copy.wait()
        sums[b + 1] = sums[b] + sums[bits + 1 + b]
    ring[z] = sums[bits]
    for u in range(depth - 1):
        moves = (
            ((z + u < depth) & (z > 0), lax.min(z + u, depth - 1), below, 0, (z < depth - 1) & (z + 1 + u < depth), lax.min(z + 1 + u, depth - 1)),
            ((z - u >= 0) & (z < depth - 1), lax.max(z - u, 0), above, 1, (z > 0) & (z - 1 - u >= 0), lax.max(z - 1 - u, 0)),
        )

        def hop(origin, to, way):
            return pltpu.make_async_remote_copy(
                src_ref=ring.at[origin],
                dst_ref=ring.at[origin],
                send_sem=ring_send.at[bits + u * 2 + way],
                recv_sem=ring_recv.at[bits + u * 2 + way],
                device_id={"batch": to},
                device_id_type=MESH,
            )

        for cond, origin, to, way, gets, source in moves:

            @pl.when(cond)
            def _():
                hop(origin, to, way).start()

        for cond, origin, to, way, gets, source in moves:

            @pl.when(gets)
            def _():
                hop(source, to, way).wait_recv()

            @pl.when(cond)
            def _():
                hop(origin, to, way).wait_send()

    total = ring[0]
    for zz in range(1, depth):
        total = total + ring[zz]
    norm_ref[...] = jnp.broadcast_to(jnp.sqrt(jnp.sum(total, keepdims=True)), (SUB, LANE))

    for p in range(phases):
        for copy in core_copies(p, False)[0]:
            copy.wait_send()
        for s in range(n):
            for copy in bit_copies(p, s):
                copy.wait_send()
        for u in range(depth - 1):
            for cond, goal, relays, recv, to, spot in z_moves(p, u):

                @pl.when(cond)
                def _():
                    z_copy(p, goal, recv, to, spot).wait_send()


def window_tiles(span, phases):
    need = (span - 1) // ROW + 2
    return -(-need // (2 * phases)) * 2 * phases


def reduce_call(flat, span, phases):
    depth, count = lax.axis_size("batch"), lax.axis_size("blk")
    bits = count.bit_length() - 1
    n = bits - 1
    half = window_tiles(span, phases) // (2 * phases)
    tile = (SUB, LANE)
    dma = pltpu.SemaphoreType.DMA
    spots = phases * 2**n * depth
    return pl.pallas_call(
        functools.partial(reduce_kernel, depth, bits, phases, half, span),
        name="reduce_gradients",
        in_specs=[pl.BlockSpec(memory_space=pl.ANY)],
        out_specs=[pl.BlockSpec(memory_space=pltpu.VMEM)] * 2,
        out_shape=[
            jax.ShapeDtypeStruct((phases * 2 * half,) + tile, f32),
            jax.ShapeDtypeStruct(tile, f32),
        ],
        scratch_shapes=[
            pltpu.VMEM((phases,) + (2,) * n + (depth, 2 * half) + tile, f32),
            pltpu.VMEM((phases,) + (2,) * n + (depth, 2 * half) + tile, f32),
        ]
        + [pltpu.VMEM((phases, 2) + (2,) * (n - 1 - s) + (depth, half) + tile, f32) for s in range(n)]
        + [pltpu.VMEM((phases, depth, 2 * half) + tile, f32)] * 2
        + [
            pltpu.VMEM((depth,) + tile, f32),
            pltpu.VMEM((2 * bits + 1,) + tile, f32),
            pltpu.VMEM(tile, f32),
            dma((spots,)),
            dma((spots,)),
            dma((spots,)),
            dma((phases * n * 2,)),
            dma((phases * n * 2,)),
            dma((phases * (depth - 1) * 2,)),
            dma((2, phases, depth)),
            dma((bits + 2 * (depth - 1),)),
            dma((bits + 2 * (depth - 1),)),
        ],
        compiler_params=pltpu.CompilerParams(
            vmem_limit_bytes=VMEM_BYTES, collective_id=1, has_side_effects=True
        ),
    )(flat)


def owned_params(params, counts, base, high):
    norm_gain, in_weight, out_weight = params[0], params[1], params[-1]
    per = in_weight.shape[1] // ROW
    small = jnp.concatenate([v.reshape(-1, ROW).astype(f32) for v in params[2:-1]], 0)
    starts = [0, norm_gain.size // ROW]
    starts.append(starts[1] + in_weight.size // ROW)
    starts.append(starts[2] + small.shape[0])
    rows = min(high // per + 2, in_weight.shape[0])
    first = jnp.clip((base - starts[1]) // per, 0, in_weight.shape[0] - rows)
    in_part = lax.dynamic_slice_in_dim(in_weight, first, rows).astype(f32).reshape(rows * per, ROW)
    deep = min(high, out_weight.shape[0])
    begin = jnp.clip(base - starts[3], 0, out_weight.shape[0] - deep)
    out_part = lax.dynamic_slice_in_dim(out_weight, begin, deep).astype(f32)
    place = base + lax.iota(jnp.int32, high)[:, None]
    total = jnp.broadcast_to(norm_gain.reshape(1, -1), (high, ROW))
    for part, origin, low in (
        (in_part, starts[1] + first * per, starts[1]),
        (small, starts[2], starts[2]),
        (out_part, starts[3] + begin, starts[3]),
    ):
        padded = jnp.pad(part, ((high, high), (0, 0)))
        offset = jnp.clip(base - origin + high, 0, part.shape[0] + high)
        total = jnp.where(place >= low, lax.dynamic_slice_in_dim(padded, offset, high), total)
    return total


def exchange(totals, state):
    count = lax.axis_size("blk")
    index = lax.axis_index("blk")
    decay, end, leave = totals[:state], totals[state : 2 * state], totals[2 * state :]
    pre_decay, pre_state = jnp.ones_like(decay), jnp.zeros_like(end)
    post_decay, post_state = jnp.ones_like(decay), jnp.zeros_like(end)
    bit = 1
    while bit < count:
        pairs = [(i, i ^ bit) for i in range(count)]
        far = lax.ppermute(jnp.concatenate([decay, end, leave], 0), "blk", pairs)
        far_decay, far_end, far_leave = far[:state], far[state : 2 * state], far[2 * state :]
        upper = (index & bit) != 0
        pre_state = jnp.where(upper, pre_state + pre_decay * far_end, pre_state)
        pre_decay = jnp.where(upper, pre_decay * far_decay, pre_decay)
        post_state = jnp.where(upper, post_state, post_state + post_decay * far_leave)
        post_decay = jnp.where(upper, post_decay, post_decay * far_decay)
        end = jnp.where(upper, end + decay * far_end, far_end + far_decay * end)
        leave = jnp.where(upper, far_leave + far_decay * leave, leave + decay * far_leave)
        decay = decay * far_decay
        bit *= 2
    return pre_state, post_state


def local(
    tokens,
    out_cot,
    norm_gain,
    in_weight,
    conv_weight,
    conv_bias,
    xproj_weight,
    dt_weight,
    dt_bias,
    a_log,
    d_skip,
    out_weight,
    moment_one,
    moment_two,
):
    contract = (((0,), (0,)), ((), ()))
    backward = (((1,), (1,)), ((), ()))
    token_rows = interleave(tokens[0])
    cot_low = interleave(out_cot[0])
    source = token_rows.astype(f32)
    length = source.shape[0]
    inner = dt_bias.shape[0]
    state = a_log.shape[0]
    rank = dt_weight.shape[0]
    width = conv_weight.shape[0]
    halo = (width - 1) * SUB
    scale = lax.rsqrt(jnp.mean(source * source, axis=-1, keepdims=True) + EPS)
    normed = (source * scale * norm_gain).astype(bf16)
    stream = jnp.dot(normed, in_weight[:, :inner], preferred_element_type=f32)
    ends = stream[length - halo :].reshape(width - 1, SUB, inner)
    tail = shifted(ends[:, SUB - 1], "blk", 1)
    gating = jnp.dot(normed, in_weight[:, inner:], preferred_element_type=f32)
    grad_gated = lax.dot_general(cot_low, out_weight, backward, preferred_element_type=f32)
    head = jnp.concatenate([tail[:, None], ends[:, : SUB - 1]], 1).reshape(halo, inner)
    longer = jnp.concatenate([head, stream], 0)

    def delayed(lag):
        return longer[halo - lag * SUB : halo - lag * SUB + length]

    conv_sum = conv_bias + conv_weight[width - 1] * stream
    for offset in range(width - 1):
        conv_sum = conv_sum + conv_weight[offset] * delayed(width - 1 - offset)
    conv_low = (conv_sum * jax.nn.sigmoid(conv_sum)).astype(bf16)
    conv_val = conv_low.astype(f32)
    selectors = jnp.dot(conv_low, xproj_weight, preferred_element_type=f32)
    step_low = selectors[:, :rank].astype(bf16)
    step_pre = jnp.dot(step_low, dt_weight, preferred_element_type=f32) + dt_bias
    step_size = jax.nn.softplus(step_pre)
    drive = step_size * conv_val
    gate_sig = jax.nn.sigmoid(gating)
    gate_val = gating * gate_sig
    grad_scanned = grad_gated * gate_val
    rates = -jnp.exp(a_log)
    rates_wide = jnp.repeat(rates * LOG2E, SUB, axis=0)

    pre_decay, pre_state, post_decay, post_state, totals = summary_call(
        step_size, drive, grad_scanned, selectors, rates_wide, rank
    )
    entry, arriving = exchange(totals, state)
    scan_out, prior, readout_grads = forward_call(
        step_size, drive, grad_scanned, selectors, rates_wide, pre_decay, pre_state, entry, rank
    )
    scanned = scan_out + d_skip * conv_val
    gated = (scanned * gate_val).astype(bf16)
    output = jnp.dot(gated, out_weight, preferred_element_type=f32)
    result = restore((source + output).astype(bf16))[None]
    grad_out_weight = lax.dot_general(gated, cot_low, contract, preferred_element_type=f32)
    grad_gating = (grad_gated * scanned * (gate_sig * (1.0 + gating * (1.0 - gate_sig)))).astype(bf16)
    grad_in_gate = lax.dot_general(normed, grad_gating, contract, preferred_element_type=f32)
    grad_d_skip = jnp.sum(grad_scanned * conv_val, 0)

    through, feed, inject_grads, rate_grads = backward_call(
        step_size, drive, grad_scanned, selectors, rates_wide, post_decay, post_state, arriving, prior, rank
    )
    grad_a_log = LN2 * jnp.sum(rate_grads.reshape(state, SUB, inner), 1)
    step_sig = jax.nn.sigmoid(step_pre)
    tiny = step_size < 1e-30
    ratio = jnp.where(tiny, 1.0, step_sig / jnp.where(tiny, 1.0, step_size))
    grad_pre = LN2 * through * ratio + conv_val * feed * step_sig
    grad_dt_bias = jnp.sum(grad_pre, 0)
    grad_pre_low = grad_pre.astype(bf16)
    grad_dt_weight = lax.dot_general(step_low, grad_pre_low, contract, preferred_element_type=f32)
    grad_step_low = lax.dot_general(grad_pre_low, dt_weight, backward, preferred_element_type=f32)
    grad_selectors = jnp.concatenate(
        [grad_step_low, inject_grads[:, :state], readout_grads[:, :state]], 1
    ).astype(bf16)
    grad_xproj = lax.dot_general(conv_low, grad_selectors, contract, preferred_element_type=f32)
    grad_conv_out = (
        grad_scanned * d_skip
        + step_size * feed
        + lax.dot_general(grad_selectors, xproj_weight, backward, preferred_element_type=f32)
    )
    grad_conv = grad_conv_out * silu_slope(conv_sum)
    begins = grad_conv[:halo].reshape(width - 1, SUB, inner)
    ahead = shifted(begins[:, 0], "blk", -1)
    foot = jnp.concatenate([begins[:, 1:], ahead[:, None]], 1).reshape(halo, inner)
    further = jnp.concatenate([grad_conv, foot], 0)
    grad_stream = conv_weight[width - 1] * grad_conv
    tap_grads = []
    for offset in range(width - 1):
        lead = width - 1 - offset
        grad_stream = grad_stream + conv_weight[offset] * further[lead * SUB : lead * SUB + length]
        tap_grads.append(jnp.sum(grad_conv * delayed(lead), 0))
    tap_grads.append(jnp.sum(grad_conv * stream, 0))
    grad_conv_weight = jnp.stack(tap_grads, 0)
    grad_conv_bias = jnp.sum(grad_conv, 0)
    grad_stream_low = grad_stream.astype(bf16)
    grad_in_stream = lax.dot_general(normed, grad_stream_low, contract, preferred_element_type=f32)
    grad_normed = lax.dot_general(
        jnp.concatenate([grad_stream_low, grad_gating], 1), in_weight, backward, preferred_element_type=f32
    )
    grad_gain = jnp.sum(grad_normed * source * scale, 0)
    weighted = grad_normed * norm_gain
    grad_source = (
        scale * weighted
        - source * scale**3 * jnp.mean(weighted * source, axis=-1, keepdims=True)
        + cot_low.astype(f32)
    )
    grad_tokens = restore(grad_source.astype(bf16))[None]
    span = moment_one.shape[0]
    small = jnp.concatenate(
        [
            value.reshape(-1, ROW)
            for value in (
                grad_conv_weight,
                grad_conv_bias,
                grad_xproj,
                grad_dt_weight,
                grad_dt_bias,
                grad_a_log,
                grad_d_skip,
            )
        ],
        0,
    ).reshape(-1, SUB, LANE)
    params = (
        norm_gain,
        in_weight,
        conv_weight,
        conv_bias,
        xproj_weight,
        dt_weight,
        dt_bias,
        a_log,
        d_skip,
        out_weight,
    )
    counts = [value.size for value in params]
    lower = sum(counts[:6])
    upper = sum(counts[:9])
    phases = 4 if span >= 16 * ROW * 4 else 1
    high = window_tiles(span, phases)
    flat = flatten_call(
        grad_in_stream, grad_in_gate, grad_out_weight, grad_gain.reshape(1, SUB, LANE), small, sum(counts) // ROW + high
    )
    reduced, norm = reduce_call(flat, span, phases)
    grad_norm = norm[0, 0]
    begin = lax.axis_index(("batch", "blk")) * span
    shard = lax.dynamic_slice_in_dim(reduced.reshape(-1), begin % ROW, span)
    owned = owned_params(params, counts, begin // ROW, high)
    owned = lax.dynamic_slice_in_dim(owned.reshape(-1), begin % ROW, span)
    place = begin + lax.iota(jnp.int32, span)
    keep = jnp.where((place >= lower) & (place < upper), 0.0, 1.0).astype(f32)
    clipped = shard * jnp.minimum(1.0, CLIP / (grad_norm + 1e-06))
    new_one = BETA_ONE * moment_one + (1.0 - BETA_ONE) * clipped
    new_two = BETA_TWO * moment_two + (1.0 - BETA_TWO) * clipped * clipped
    first = new_one / (1.0 - BETA_ONE**ADAM_STEP)
    second = new_two / (1.0 - BETA_TWO**ADAM_STEP)
    param_step = -RATE * (first / (jnp.sqrt(second) + ADAM_EPS) + DECAY * keep * owned)
    return (result, grad_tokens, shard, grad_norm, param_step, new_one, new_two)


def solution(mesh):
    return jax.shard_map(
        local,
        mesh=mesh,
        in_specs=(P("batch", "blk", None),) * 2 + (P(),) * 10 + (P(("batch", "blk")),) * 2,
        out_specs=(P("batch", "blk", None),) * 2
        + (P(("batch", "blk")), P(), P(("batch", "blk")), P(("batch", "blk")), P(("batch", "blk"))),
        check_vma=False,
    )
```

time: 3170 us -> 777 us (0.25)
  local copies, waits for them, and re-layouts: 1420 us -> 29 us
  other arithmetic: 890 us -> 79.8 us
  Pallas kernels: 0 us -> 514 us
  waiting for transfers between devices: 451 us -> 10.3 us
  loops' own time: 127 us -> 0 us
  blocking collectives: 40 us -> 0 us
  starting transfers between devices: 46.8 us -> 9.88 us
    dynamic_update_slice x128 -> x0, local copies, waits for them, and re-layouts: 661 us -> none  [the longest x112 536 us: place_row(): return lax.dynamic_update_index_in_dim(buffer, row[:, None], index, 1)]
    pallas_call x0 -> x5, Pallas kernels: none -> 514 us  [the longest x1 165 us: reduce_call(): pl.pallas_call(functools.partial(reduce_kernel, depth, bits, phases, half...]
    unnamed x2 -> x0, waiting for transfers between devices: 404 us -> none
    reduce_sum x33 -> x2, other arithmetic: 348 us -> 26 us  [the longest x1 25.7 us: local(): tap_grads.append(jnp.sum(grad_conv * delayed(lead), 0))]
    pad x40 -> x0, local copies, waits for them, and re-layouts: 314 us -> none  [sub_prefix(): inc_decay, inc_state = lax.associative_scan(link, (totals, ends))]
    add x88 -> x0, other arithmetic: 278 us -> none  [the longest x16 105 us: local_step(): jnp.exp(pick(step_rows, index)[:, None, :] * rates) * carry]
    unnamed x226 -> x97, local copies, waits for them, and re-layouts: 180 us -> 7.63 us
    mul x34 -> x3, other arithmetic: 154 us -> 0.1 us  [the longest x1 0.06 us: exchange(): decay = decay * far_decay]
  transfers between devices with their start and end apart: 17 -> 5, of which waited for: 15 -> 2; matrix products, arithmetic and copies ran while one was open for 4% -> 5% of each run, Pallas kernels for 0% -> 0%
where the time goes in v1:
time: 777 us; the launch traced here: 771 us
  Pallas kernels  514 us (66%)
  matrix products  126 us (16%)
  other arithmetic  79.8 us (10%)
  local copies, waits for them, and re-layouts  29 us (4%)
  waiting for transfers between devices  10.3 us (1%)
  starting transfers between devices  9.88 us (1%)
    pallas_call x1, Pallas kernels, reduce_call(): pl.pallas_call(functools.partial(reduce_kernel, depth, bits, phases, half...  165 us
    pallas_call x1, Pallas kernels, backward_call(): pl.pallas_call(functools.partial(backward_kernel, shape), name='scan_back...  118 us
    pallas_call x1, Pallas kernels, forward_call(): pl.pallas_call(functools.partial(forward_kernel, shape), name='scan_forwa...  98.1 us
    pallas_call x1, Pallas kernels, summary_call(): pl.pallas_call(functools.partial(summary_kernel, shape), name='scan_summa...  83.9 us
    pallas_call x1, Pallas kernels, flatten_call(): pl.pallas_call(functools.partial(flatten_kernel, rows_in, rows_out, in_ba...  48.3 us
    reduce_sum x1, other arithmetic, local(): tap_grads.append(jnp.sum(grad_conv * delayed(lead), 0))  25.7 us
    reduce_sum x1, other arithmetic, local(): grad_dt_bias = jnp.sum(grad_pre, 0)  22.4 us
    dot_general x1, matrix products, local(): lax.dot_general(cot_low, out_weight, backward, preferred_element_type=f32)  20.4 us
  transfers between devices with their start and end apart: 5, of which 2 were waited for; matrix products, arithmetic and copies ran while one was open for 5% of the time, Pallas kernels for 0%

profile of v1, /device:TPU:0, one launch (start us, length us, event | category | flops | bytes accessed | tf_op | source)
XLA Modules:
  0.0 771.4 jit_solution(1350927904322519388)
XLA Ops:
  0.6 2.1 multiply_reduce_fusion.4
  2.7 4.1 convert.34
  7.6 4.9 fusion.24
  12.5 7.1 fusion.35
  19.7 2.7 collective-permute-start
  22.5 6.8 fusion.33
  31.2 20.4 %fusion.16 = (f32[2048]{0:T(1024)}, f32[1024,2048]{1,0:T(8,128)}, bf16[1024,2048]{1,0:T(8,128)(2,1)S(1)}, f32[1024,2048]{1,0:T(8,128)}, f32[1024,2048]{1,0:T(8,128)}) fusion(f32[1024,2048]{1,0:T(8,128)} %fusion.33, f32[1024,2048]{1,0:T(8,128)S(1)} %fusion.35, f32[24,2048]{1,0:T(8,128)S(1)} %maximum_bitcast_fusion, f32[2048]{0:T(1024)} %bitcast.133, ...), kind=kOutput, calls=%fused_computation.27 | convolution fusion | flops 4345296896 | bytes 52674560 | tf_op jit(solution)/shard_map/dot_general | solution.py:955
  51.6 2.0 copy-done
  53.5 2.4 fusion.75
  57.0 12.7 %convert_multiply_fusion.3 = (f32[1024,2048]{1,0:T(8,128)}, f32[1024,2048]{1,0:T(8,128)}, f32[1024,2048]{1,0:T(8,128)}) fusion(bf16[1024,2048]{1,0:T(8,128)(2,1)} %copy-done, f32[2048]{0:T(1024)} %param.22, bf16[64,2048]{1,0:T(8,128)(2,1)S(1)} %copy-done.9, f32[1024,96]{0,1:T(8,128)S(1)} %fusion.75), kind=kOutput, calls=%fused_computation.4 | convolution fusion | flops 287309824 | bytes 29761536 | tf_op jit(solution)/shard_map/dot_general | solution.py:969
  69.7 83.9 %scan_summary.1 = (f32[128,2048]{1,0:T(8,128)}, f32[128,2048]{1,0:T(8,128)}, f32[128,2048]{1,0:T(8,128)}, f32[128,2048]{1,0:T(8,128)}, f32[48,2048]{1,0:T(8,128)}) custom-call(f32[1024,2048]{1,0:T(8,128)} %get-tuple-element.55.step_ref, f32[1024,2048]{1,0:T(8,128)} %get-tuple-element.54.drive_ref, f32[1024,2048]{1,0:T(8,128)} %get-tuple-element.47.grad_ref, ...), custom_call_target="tpu_custom_call" | custom-call | tf_op jit(solution)/shard_map/scan_summary/pallas_call | solution.py:371
  153.6 2.7 collective-permute-start.1
  161.9 8.7 %collective-permute-done.2 = f32[48,2048]{1,0:T(8,128)S(1)} collective-permute-done((f32[48,2048]{1,0:T(8,128)S(1)}, f32[48,2048]{1,0:T(8,128)S(1)}, u32[]{:S(2)}, u32[]{:S(2)}) %collective-permute-start.2) | collective-permute-done | bytes 393248 | tf_op jit(solution)/shard_map/ppermute | solution.py:908
  176.8 2.8 concatenate.61
  183.4 2.1 add_select_fusion
  185.5 98.1 %scan_forward.1 = (f32[1024,2048]{1,0:T(8,128)}, bf16[16384,2048]{1,0:T(8,128)(2,1)}, f32[1024,128]{1,0:T(8,128)}) custom-call(f32[1024,2048]{1,0:T(8,128)} %get-tuple-element.55.step_ref, f32[1024,2048]{1,0:T(8,128)} %get-tuple-element.54.drive_ref, f32[1024,2048]{1,0:T(8,128)} %get-tuple-element.47.grad_ref, f32[1024,96]{1,0:T(8,128)} %copy.52.sel_ref, ...), custom_call_target="tpu_custom_call" | custom-call | tf_op jit(solution)/shard_map/scan_forward/pallas_call | solution.py:393
  283.6 118.4 %scan_backward.1 = (f32[1024,2048]{1,0:T(8,128)}, f32[1024,2048]{1,0:T(8,128)}, f32[1024,128]{1,0:T(8,128)}, f32[128,2048]{1,0:T(8,128)}) custom-call(f32[1024,2048]{1,0:T(8,128)} %get-tuple-element.55.step_ref, f32[1024,2048]{1,0:T(8,128)} %get-tuple-element.54.drive_ref, f32[1024,2048]{1,0:T(8,128)} %get-tuple-element.47.grad_ref, ...), custom_call_target="tpu_custom_call" | custom-call | tf_op jit(solution)/shard_map/scan_backward/pallas_call | solution.py:427
  402.0 22.4 %fusion.72 = (f32[2048]{0:T(1024)}, bf16[1024,2048]{1,0:T(8,128)(2,1)S(1)}, bf16[1024,2048]{1,0:T(8,128)(2,1)S(1)}, bf16[1024,2048]{1,0:T(8,128)(2,1)}) fusion(f32[1024,2048]{1,0:T(8,128)} %get-tuple-element.28, bf16[1024,2048]{1,0:T(8,128)(2,1)S(1)} %copy-done.1, f32[1024,2048]{1,0:T(8,128)} %get-tuple-element.72, f32[2048]{0:T(1024)S(1)} %copy-done.29, ...), kind=kLoop, calls=%fused_computation.147 | loop fusion | flops 79689728 | bytes 67133440 | tf_op jit(solution)/shard_map/reduce_sum | solution.py:1002
  424.5 7.3 fusion.39.out_w_ref
  431.7 7.8 %fusion.38 = bf16[8,128,1024]{2,0,1:T(8,128)(2,1)} fusion(f32[8,128,1024]{2,1,0:T(8,128)S(1)} %copy-done.4, bf16[1024,2048]{1,0:T(8,128)(2,1)S(1)} %get-tuple-element.57, bf16[2048,1024]{1,0:T(8,128)(2,1)S(1)} %copy-done.32), kind=kOutput, calls=%fused_computation.69 | convolution fusion | flops 4297064448 | bytes 14680064 | tf_op jit(solution)/shard_map/dot_general | solution.py:987
  441.3 3.5 fusion.62
  444.8 15.0 %multiply_multiply_fusion = f32[1024,2048]{1,0:T(8,128)S(1)} fusion(f32[1024,2048]{1,0:T(8,128)} %get-tuple-element.49, f32[1024,2048]{1,0:T(8,128)} %get-tuple-element.28, f32[1024,2048]{1,0:T(8,128)} %get-tuple-element.47.grad_ref, bf16[2048,96]{0,1:T(8,128)(2,1)S(1)} %copy-done.14, f32[2048]{0:T(1024)S(1)} %copy-done.40, bf16[1024,16]{0,1:T(8,128)(2,1)S(1)} %copy.56, ...), kind=kOutput, calls=%fused_computation.40 | convolution fusion | flops 443088896 | bytes 42549248 | tf_op jit(solution)/shard_map/dot_general | solution.py:1013
  461.6 12.2 %fusion.77.gate_ref = f32[1024,2048]{1,0:T(8,128)} fusion(bf16[1024,1024]{1,0:T(8,128)(2,1)} %copy-done.10, bf16[1024,2048]{1,0:T(8,128)(2,1)} %get-tuple-element.58), kind=kOutput, calls=%fused_computation.151 | convolution fusion | flops 4294967296 | bytes 14680064 | tf_op jit(solution)/shard_map/dot_general | solution.py:991
  476.2 4.1 copy.53
  480.4 25.7 %multiply_reduce_fusion.3 = (f32[2048]{0:T(1024)S(1)}, f32[2048]{0:T(1024)}, f32[2048]{0:T(1024)}, f32[2048]{0:T(1024)}, f32[2048]{0:T(1024)S(1)}, /*index=5*/bf16[1024,2048]{1,0:T(8,128)(2,1)}) fusion(f32[1024,2048]{1,0:T(8,128)} %copy-done.7, f32[1024,2048]{1,0:T(8,128)} %copy-done.6, f32[24,2048]{1,0:T(8,128)S(1)} %copy-done.23, ...), kind=kLoop, calls=%fused_computation.38 | loop fusion | flops 48224256 | bytes 21438464 | tf_op jit(solution)/shard_map/reduce_sum | solution.py:1025
  506.1 10.9 %fusion.76.stream_ref = f32[1024,2048]{1,0:T(8,128)} fusion(bf16[1024,1024]{1,0:T(8,128)(2,1)} %copy-done.10, bf16[1024,2048]{1,0:T(8,128)(2,1)} %get-tuple-element.56), kind=kOutput, calls=%fused_computation.150 | convolution fusion | flops 4294967296 | bytes 14680064 | tf_op jit(solution)/shard_map/dot_general | solution.py:1030
  517.0 17.9 %fusion.32 = (f32[1024]{0:T(1024)}, f32[1024]{0:T(1024)S(1)}, f32[1024,1024]{1,0:T(8,128)}) fusion(f32[8,128,1024]{2,1,0:T(8,128)S(1)} %copy-done.5, f32[1024]{0:T(1024)S(1)} %copy-done.31, f32[1024]{0:T(1024)S(1)} %copy-done.35, bf16[1024,4096]{1,0:T(8,128)(2,1)} %param.17, bf16[1024,2048]{1,0:T(8,128)(2,1)} %get-tuple-element.58, ...), kind=kOutput, calls=%fused_computation.61 | convolution fusion | flops 8613001216 | bytes 25182208 | tf_op jit(solution)/shard_map/dot_general | solution.py:1031
  539.5 48.3 %flatten.1.flat_ref = f32[6719,8,128]{2,1,0:T(8,128)} custom-call(f32[1024,2048]{1,0:T(8,128)} %fusion.76.stream_ref, f32[1024,2048]{1,0:T(8,128)} %fusion.77.gate_ref, f32[2048,1024]{1,0:T(8,128)} %fusion.39.out_w_ref, f32[1,8,128]{2,1,0:T(8,128)} %bitcast.144, f32[366,8,128]{2,1,0:T(8,128)} %copy-done.17), custom_call_target="tpu_custom_call" | custom-call | tf_op jit(solution)/shard_map/flatten/pallas_call | solution.py:520
  587.8 165.1 %reduce_gradients.1 = (f32[208,8,128]{2,1,0:T(8,128)}, f32[8,128]{1,0:T(8,128)}) custom-call(f32[6719,8,128]{2,1,0:T(8,128)} %flatten.1.flat_ref), custom_call_target="tpu_custom_call" | custom-call | tf_op jit(solution)/shard_map/reduce_gradients/pallas_call | solution.py:838
  754.8 11.1 %fusion.37 = bf16[8,128,1024]{2,0,1:T(8,128)(2,1)S(1)} fusion(f32[8,128,1024]{2,1,0:T(8,128)} %convert.34, f32[1024,1024]{1,0:T(8,128)} %get-tuple-element.73, f32[1024]{0:T(1024)S(1)} %get-tuple-element.75, f32[1024]{0:T(1024)S(1)} %get-tuple-element.74, f32[1024]{0:T(1024)S(1)} %copy-done.35, f32[1024]{0:T(1024)S(1)} %copy-done.31, ...), kind=kLoop, calls=%fused_computation.68 | loop fusion | flops 8388608 | bytes 12599296 | tf_op jit(solution)/shard_map/transpose | solution.py:51
  766.0 2.5 copy.58
  768.4 2.7 add_multiply_fusion
  (154 shorter events, 30.8 us)
Async XLA Ops:
  7.6 14.8 %slice-start = ((s8[8388608]{0:T(1024)(128)(4,1)}), s8[4194304]{0:T(1024)(128)(4,1)S(1)}, s32[]{:S(2)}) async-start(s8[8388608]{0:T(1024)(128)(4,1)} %bitcast.142), calls=%async_computation | async-start | bytes 8388608
  12.5 10.0 %slice-start.1 = ((s8[8388608]{0:T(1024)(128)(4,1)}), s8[4194304]{0:T(1024)(128)(4,1)S(1)}, s32[]{:S(2)}) async-start(s8[8388608]{0:T(1024)(128)(4,1)} %bitcast.142), calls=%async_computation.1 | async-start | bytes 8388608
  19.6 11.5 %copy-start.6 = (f32[1024,2048]{1,0:T(8,128)}, f32[1024,2048]{1,0:T(8,128)S(1)}, u32[]{:S(2)}) copy-start(f32[1024,2048]{1,0:T(8,128)S(1)} %fusion.35) | copy-start | bytes 25165828
  19.7 10.7 %copy-start.28 = (f32[4,2048]{1,0:T(4,128)S(1)}, f32[4,2048]{1,0:T(4,128)}, u32[]{:S(2)}) copy-start(f32[4,2048]{1,0:T(4,128)} %param.18) | copy-start | bytes 98308
  19.7 11.3 %collective-permute-start = (f32[3,2048]{1,0:T(4,128)S(1)}, f32[3,2048]{1,0:T(4,128)S(1)}, u32[]{:S(2)}, u32[]{:S(2)}) collective-permute-start(f32[3,2048]{1,0:T(4,128)S(1)} %bitcast.140), channel_id=1, source_target_pairs={{0,1},{1,2},{2,3},{3,4},{4,5},{5,6},{6,7},{8,9},{9,10},{10,11},{11... | collective-permute-start | bytes 73736 | tf_op jit(solution)/shard_map/ppermute | solution.py:36
  31.1 20.4 %copy-start.22 = (f32[24,2048]{1,0:T(8,128)}, f32[24,2048]{1,0:T(8,128)S(1)}, u32[]{:S(2)}) copy-start(f32[24,2048]{1,0:T(8,128)S(1)} %maximum_bitcast_fusion) | copy-start | bytes 589828
  31.1 25.8 %copy-start.9 = (bf16[64,2048]{1,0:T(8,128)(2,1)S(1)}, bf16[64,2048]{1,0:T(8,128)(2,1)}, u32[]{:S(2)}) copy-start(bf16[64,2048]{1,0:T(8,128)(2,1)} %param.21) | copy-start | bytes 786436
  69.7 104.1 %copy-start.13 = (bf16[2048,96]{0,1:T(8,128)(2,1)S(1)}, bf16[2048,96]{0,1:T(8,128)(2,1)}, u32[]{:S(2)}) copy-start(bf16[2048,96]{0,1:T(8,128)(2,1)} %param.20) | copy-start | bytes 1179652
  69.7 105.1 %copy-start.25 = (f32[16,2048]{1,0:T(8,128)S(1)}, f32[16,2048]{1,0:T(8,128)}, u32[]{:S(2)}) copy-start(f32[16,2048]{1,0:T(8,128)} %param.23) | copy-start | bytes 393220
  69.7 105.2 %copy-start.41 = (f32[2048]{0:T(1024)S(1)}, f32[2048]{0:T(1024)}, u32[]{:S(2)}) copy-start(f32[2048]{0:T(1024)} %param.19) | copy-start | bytes 24580
  69.7 105.2 %copy-start.29 = (f32[2048]{0:T(1024)S(1)}, f32[2048]{0:T(1024)}, u32[]{:S(2)}) copy-start(f32[2048]{0:T(1024)} %param.22) | copy-start | bytes 24580
  153.6 23.2 %copy-start.40 = (f32[2048]{0:T(1024)S(1)}, f32[2048]{0:T(1024)}, u32[]{:S(2)}) copy-start(f32[2048]{0:T(1024)} %param.24) | copy-start | bytes 24580
  153.6 27.2 %copy-start.34 = (f32[1024]{0:T(1024)S(1)}, f32[1024]{0:T(1024)}, u32[]{:S(2)}) copy-start(f32[1024]{0:T(1024)} %param.16) | copy-start | bytes 12292
  153.6 4.2 collective-permute-start.1
  157.9 18.1 %copy-start.15 = (f32[48,2048]{1,0:T(8,128)}, f32[48,2048]{1,0:T(8,128)S(1)}, u32[]{:S(2)}) copy-start(f32[48,2048]{1,0:T(8,128)S(1)} %collective-permute-done.1) | copy-start | bytes 1179652
  159.1 11.5 %collective-permute-start.2 = (f32[48,2048]{1,0:T(8,128)S(1)}, f32[48,2048]{1,0:T(8,128)S(1)}, u32[]{:S(2)}, u32[]{:S(2)}) collective-permute-start(f32[48,2048]{1,0:T(8,128)S(1)} %pad_maximum_fusion.2), channel_id=1, source_target_pairs={{0,2},{1,3},{2,0},{3,1},{4,6},{5,7},{6,4},{7,5},{8,10},{9,11},{10,... | collective-permute-start | bytes 1179656 | tf_op jit(solution)/shard_map/ppermute | solution.py:908
  172.2 11.2 %collective-permute-start.3 = (f32[48,2048]{1,0:T(8,128)}, f32[48,2048]{1,0:T(8,128)}, u32[]{:S(2)}, u32[]{:S(2)}) collective-permute-start(f32[48,2048]{1,0:T(8,128)} %pad_maximum_fusion.3), channel_id=1, source_target_pairs={{0,4},{1,5},{2,6},{3,7},{4,0},{5,1},{6,2},{7,3},{8,12},{9,13},{10,... | collective-permute-start | bytes 1179656 | tf_op jit(solution)/shard_map/ppermute | solution.py:908
  283.6 118.4 %copy-start.1 = (bf16[1024,2048]{1,0:T(8,128)(2,1)S(1)}, bf16[1024,2048]{1,0:T(8,128)(2,1)}, u32[]{:S(2)}) copy-start(bf16[1024,2048]{1,0:T(8,128)(2,1)} %copy-done) | copy-start | bytes 12582916
  402.0 22.4 %copy-start.11 = (bf16[1,1024,1024]{2,1,0:T(8,128)(2,1)S(1)}, bf16[1,1024,1024]{2,1,0:T(8,128)(2,1)}, u32[]{:S(2)}) copy-start(bf16[1,1024,1024]{2,1,0:T(8,128)(2,1)} %param.15) | copy-start | bytes 6291460
  424.5 15.1 %copy-start.2 = (bf16[1024,2048]{1,0:T(8,128)(2,1)}, bf16[1024,2048]{1,0:T(8,128)(2,1)S(1)}, u32[]{:S(2)}) copy-start(bf16[1024,2048]{1,0:T(8,128)(2,1)S(1)} %get-tuple-element.51) | copy-start | bytes 12582916
  444.8 16.5 %copy-start.18 = (f32[128,2048]{1,0:T(8,128)S(1)}, f32[128,2048]{1,0:T(8,128)}, u32[]{:S(2)}) copy-start(f32[128,2048]{1,0:T(8,128)} %get-tuple-element.32) | copy-start | bytes 3145732
  459.8 14.0 %copy-start.7 = (f32[1024,2048]{1,0:T(8,128)}, f32[1024,2048]{1,0:T(8,128)S(1)}, u32[]{:S(2)}) copy-start(f32[1024,2048]{1,0:T(8,128)S(1)} %multiply_multiply_fusion) | copy-start | bytes 25165828
  459.8 20.5 %collective-permute-start.4 = (f32[3,2048]{1,0:T(4,128)S(1)}, f32[3,2048]{1,0:T(4,128)S(1)}, u32[]{:S(2)}, u32[]{:S(2)}) collective-permute-start(f32[3,2048]{1,0:T(4,128)S(1)} %bitcast.139), channel_id=1, source_target_pairs={{1,0},{2,1},{3,2},{4,3},{5,4},{6,5},{7,6},{9,8},{10,9},{11,10},{12... | collective-permute-start | bytes 73736 | tf_op jit(solution)/shard_map/ppermute | solution.py:36
  461.3 12.5 %copy-start.3 = (bf16[1024,2048]{1,0:T(8,128)(2,1)S(1)}, bf16[1024,2048]{1,0:T(8,128)(2,1)}, u32[]{:S(2)}) copy-start(bf16[1024,2048]{1,0:T(8,128)(2,1)} %copy-done.2) | copy-start | bytes 12582916
  506.1 10.9 %copy-start.5 = (f32[8,128,1024]{2,1,0:T(8,128)S(1)}, f32[8,128,1024]{2,1,0:T(8,128)}, u32[]{:S(2)}) copy-start(f32[8,128,1024]{2,1,0:T(8,128)} %convert.34) | copy-start | bytes 12582916
  506.1 10.9 %copy-start.31 = (f32[1024]{0:T(1024)S(1)}, f32[1024]{0:T(1024)}, u32[]{:S(2)}) copy-start(f32[1024]{0:T(1024)} %copy-done.30) | copy-start | bytes 12292
  506.1 10.9 %copy-start.35 = (f32[1024]{0:T(1024)S(1)}, f32[1024]{0:T(1024)}, u32[]{:S(2)}) copy-start(f32[1024]{0:T(1024)} %param.16) | copy-start | bytes 12292
  587.8 167.0 %copy-start.12 = (bf16[1,1024,1024]{2,1,0:T(8,128)(2,1)S(1)}, bf16[1,1024,1024]{2,1,0:T(8,128)(2,1)}, u32[]{:S(2)}) copy-start(bf16[1,1024,1024]{2,1,0:T(8,128)(2,1)} %param.15) | copy-start | bytes 6291460
  754.8 13.6 %copy-start.8 = (f32[26,8,8,128]{3,1,2,0:T(8,128)S(1)}, f32[26,8,8,128]{3,1,2,0:T(8,128)}, u32[]{:S(2)}) copy-start(f32[26,8,8,128]{3,1,2,0:T(8,128)} %copy.64) | copy-start | bytes 2555908
  754.8 13.6 %copy-start.19 = (f32[208352]{0:T(1024)S(1)}, f32[208352]{0:T(1024)}, u32[]{:S(2)}) copy-start(f32[208352]{0:T(1024)} %param.26) | copy-start | bytes 2500228
  754.8 13.6 %copy-start.20 = (f32[208352]{0:T(1024)S(1)}, f32[208352]{0:T(1024)}, u32[]{:S(2)}) copy-start(f32[208352]{0:T(1024)} %param.27) | copy-start | bytes 2500228
  754.8 13.6 %copy-start.21 = (f32[208,8,128]{2,1,0:T(8,128)S(1)}, f32[208,8,128]{2,1,0:T(8,128)}, u32[]{:S(2)}) copy-start(f32[208,8,128]{2,1,0:T(8,128)} %get-tuple-element.33) | copy-start | bytes 2555908
  (17 other events, 102.3 us)

commit v2 on v1

--- a/solution.py
+++ b/solution.py
@@ -55,30 +55,31 @@
     return pl.ds(pl.multiple_of(start, size), size)
 
 
-def spread(sel_ref, base, state, tiles, out_ref):
-    def one(i, carry):
-        tile = sel_ref[at(i * SUB, SUB), :]
-        for n in range(state):
-            out_ref[at((i * state + n) * SUB, SUB), :] = jnp.broadcast_to(
-                tile[:, base + n : base + n + 1], (SUB, LANE)
-            )
-        return carry
-
-    lax.fori_loop(0, tiles, one, 0)
-
-
-def gather_lanes(src_ref, state, tiles, out_ref):
-    lane = lax.broadcasted_iota(jnp.int32, (SUB, LANE), 1)
-
-    def one(i, carry):
-        total = jnp.zeros((SUB, LANE), f32)
-        for n in range(state):
-            part = jnp.sum(src_ref[at((i * state + n) * SUB, SUB), :], axis=1, keepdims=True)
-            total = jnp.where(lane == n, part, total)
-        out_ref[at(i * SUB, SUB), :] = total
-        return carry
-
-    lax.fori_loop(0, tiles, one, 0)
+def spread(sel_ref, spots_ref, out_ref):
+    out_ref[...] = jnp.dot(sel_ref[...], spots_ref[...], preferred_element_type=f32)
+
+
+def gather_lanes(src_ref, spots_ref, out_ref):
+    value = src_ref[...]
+    high = value.astype(bf16)
+    low = (value - high.astype(f32)).astype(bf16)
+    spots = spots_ref[0:LANE, 0 : value.shape[1]]
+    back = (((1,), (1,)), ((), ()))
+    out_ref[...] = lax.dot_general(high, spots, back, preferred_element_type=f32) + lax.dot_general(
+        low, spots, back, preferred_element_type=f32
+    )
+
+
+def split_selectors(values):
+    high = lax.reduce_precision(values, 8, 7)
+    middle = lax.reduce_precision(values - high, 8, 7)
+    terms = jnp.concatenate([high, middle, values - high - middle], 1)
+    count = values.shape[1]
+    terms = jnp.pad(terms, ((0, 0), (0, LANE - 3 * count))).astype(bf16)
+    row = lax.broadcasted_iota(jnp.int32, (LANE, count * LANE), 0)
+    col = lax.broadcasted_iota(jnp.int32, (LANE, count * LANE), 1) // LANE
+    spots = ((row % count == col) & (row < 3 * count)).astype(bf16)
+    return terms, spots
 
 
 def summary_kernel(
@@ -87,6 +88,7 @@
     drive_ref,
     grad_ref,
     sel_ref,
+    spots_ref,
     rates_ref,
     pre_decay_ref,
     pre_state_ref,
@@ -96,10 +98,9 @@
     end_ref,
     exit_ref,
     prod_ref,
-    inject_ref,
-    readout_ref,
+    select_ref,
 ):
-    tiles, state, inner, rank, cols, group = shape
+    tiles, state, inner, cols, group = shape
     turn = pl.program_id(0)
 
     @pl.when(turn == 0)
@@ -108,8 +109,7 @@
         exit_ref[...] = jnp.zeros_like(exit_ref)
         prod_ref[...] = jnp.ones_like(prod_ref)
 
-    spread(sel_ref, rank, state, tiles, inject_ref)
-    spread(sel_ref, rank + state, state, tiles, readout_ref)
+    spread(sel_ref, spots_ref, select_ref)
 
     def columns(c, carry):
         lanes = [at((c * cols + k) * LANE, LANE) for k in range(cols)]
@@ -124,8 +124,10 @@
                 step = [step_ref[here, l] for l in lanes]
                 drive = [drive_ref[here, l] for l in lanes]
                 grad = [grad_ref[here, l] for l in lanes]
-                inject = [inject_ref[at((i * state + first + n) * SUB, SUB), :] for n in range(group)]
-                readout = [readout_ref[at((i * state + first + n) * SUB, SUB), :] for n in range(group)]
+                inject = [select_ref[here, (first + n) * LANE : (first + n + 1) * LANE] for n in range(group)]
+                readout = [
+                    select_ref[here, (state + first + n) * LANE : (state + first + n + 1) * LANE] for n in range(group)
+                ]
                 new = ([], [], [])
                 for s, (n, k) in enumerate(spots):
                     decay = jnp.exp2(step[k] * rates[s])
@@ -136,7 +138,7 @@
                 return tuple(tuple(x) for x in new)
 
             start = tuple(tuple(ref[w] for w in where) for ref in (end_ref, exit_ref, prod_ref))
-            ends, exits, prods = lax.fori_loop(0, tiles, advance, start, unroll=8)
+            ends, exits, prods = lax.fori_loop(0, tiles, advance, start, unroll=16)
             for s, w in enumerate(where):
                 end_ref[w] = ends[s]
                 exit_ref[w] = exits[s]
@@ -184,28 +186,35 @@
     drive_ref,
     grad_ref,
     sel_ref,
+    spots_ref,
     rates_ref,
     pre_decay_ref,
     pre_state_ref,
     entry_ref,
-    scanned_ref,
+    conv_ref,
+    gating_ref,
+    grad_gated_ref,
+    skip_ref,
     prior_ref,
     readout_grad_ref,
+    gated_ref,
+    grad_gating_ref,
+    skip_grad_ref,
     state_ref,
-    inject_ref,
-    readout_ref,
+    select_ref,
     sums_ref,
+    scanned_ref,
 ):
-    tiles, state, inner, rank, cols, group = shape
+    tiles, state, inner, cols, group = shape
 
     @pl.when(pl.program_id(0) == 0)
     def _():
+        skip_grad_ref[...] = jnp.zeros_like(skip_grad_ref)
         for n in range(state):
             here = slice(n * SUB, (n + 1) * SUB)
             state_ref[here, :] = pre_state_ref[here, :] + pre_decay_ref[here, :] * entry_ref[n : n + 1, :]
 
-    spread(sel_ref, rank, state, tiles, inject_ref)
-    spread(sel_ref, rank + state, state, tiles, readout_ref)
+    spread(sel_ref, spots_ref, select_ref)
     sums_ref[...] = jnp.zeros_like(sums_ref)
 
     def columns(c, carry):
@@ -223,9 +232,9 @@
                 outs = [None] * cols
                 new = []
                 for n in range(group):
-                    spot = at((i * state + first + n) * SUB, SUB)
-                    inject = inject_ref[spot, :]
-                    readout = readout_ref[spot, :]
+                    spot = slice((first + n) * LANE, (first + n + 1) * LANE)
+                    inject = select_ref[here, spot]
+                    readout = select_ref[here, (state + first + n) * LANE : (state + first + n + 1) * LANE]
                     total = None
                     for k in range(cols):
                         s = n * cols + k
@@ -236,7 +245,7 @@
                         outs[k] = part if outs[k] is None else outs[k] + part
                         part = grad[k] * fresh
                         total = part if total is None else total + part
-                    sums_ref[spot, :] += total
+                    sums_ref[here, spot] += total
                     if n % 2 == 1:
                         pair = pl.ds(pl.multiple_of((i * state + first + n - 1) * SUB, 2 * SUB), 2 * SUB)
                         for k in range(cols):
@@ -250,13 +259,36 @@
                         scanned_ref[here, lanes[k]] += outs[k]
                 return tuple(new)
 
-            states = lax.fori_loop(0, tiles, advance, tuple(state_ref[w] for w in where), unroll=4)
+            states = lax.fori_loop(0, tiles, advance, tuple(state_ref[w] for w in where), unroll=16)
             for s, w in enumerate(where):
                 state_ref[w] = states[s]
         return carry
 
     lax.fori_loop(0, inner // (LANE * cols), columns, 0)
-    gather_lanes(sums_ref, state, tiles, readout_grad_ref)
+    gather_lanes(sums_ref, spots_ref, readout_grad_ref)
+
+    def finish(c, carry):
+        lanes = at(c * 2 * LANE, 2 * LANE)
+        skip = skip_ref[:, lanes]
+
+        def pair(i, total):
+            here = at(i * 2 * SUB, 2 * SUB)
+            conv = conv_ref[here, lanes].astype(f32)
+            gating = gating_ref[here, lanes]
+            sig = jax.nn.sigmoid(gating)
+            gate = gating * sig
+            scanned = scanned_ref[here, lanes] + skip * conv
+            gated_ref[here, lanes] = (scanned * gate).astype(bf16)
+            slope = sig + gate * (1.0 - sig)
+            grad_gating_ref[here, lanes] = (grad_gated_ref[here, lanes] * scanned * slope).astype(bf16)
+            product = grad_ref[here, lanes] * conv
+            return total + product[:SUB] + product[SUB:]
+
+        zero = jnp.zeros((SUB, 2 * LANE), f32)
+        skip_grad_ref[:, lanes] += lax.fori_loop(0, tiles // 2, pair, zero, unroll=4)
+        return carry
+
+    lax.fori_loop(0, inner // (2 * LANE), finish, 0)
 
 
 def backward_kernel(
@@ -265,31 +297,75 @@
     drive_ref,
     grad_ref,
     sel_ref,
+    spots_ref,
     rates_ref,
     post_decay_ref,
     post_state_ref,
     arriving_ref,
     prior_ref,
+    conv_sum_ref,
+    stream_ref,
+    readout_grad_ref,
+    step_back_ref,
+    select_back_ref,
+    taps_ref,
+    skip_ref,
+    grad_stream_ref,
+    grad_pre_ref,
+    grad_select_ref,
+    rate_grad_ref,
+    taps_grad_ref,
+    edge_ref,
+    carry_ref,
+    select_ref,
+    sums_ref,
     through_ref,
     feed_ref,
+    grad_conv_ref,
     inject_grad_ref,
-    rate_grad_ref,
-    carry_ref,
-    inject_ref,
-    readout_ref,
-    sums_ref,
+    probe_ref,
+    probe_sems,
 ):
-    tiles, state, inner, rank, cols, group = shape
+    tiles, state, inner, cols, group = shape
+    blk = lax.axis_index("blk")
+    other = blk + 1 - 2 * (blk % 2)
+
+    def probe():
+        return pltpu.make_async_remote_copy(
+            src_ref=probe_ref.at[0],
+            dst_ref=probe_ref.at[1],
+            send_sem=probe_sems.at[0],
+            recv_sem=probe_sems.at[1],
+            device_id={"blk": other},
+            device_id_type=MESH,
+        )
+
+    @pl.when(pl.program_id(0) == 0)
+    def _():
+        barrier = pltpu.get_barrier_semaphore()
+        pl.semaphore_signal(barrier, inc=1, device_id={"blk": other}, device_id_type=MESH)
+        pl.semaphore_wait(barrier, 1)
+        probe_ref[0] = jnp.ones((SUB, LANE), f32)
+        probe().start()
+
+    @pl.when(pl.program_id(0) == pl.num_programs(0) - 1)
+    def _():
+        probe().wait()
+
+    block = tiles * SUB
+    width = taps_ref.shape[0]
+    halo = (width - 1) * SUB
 
     @pl.when(pl.program_id(0) == 0)
     def _():
         rate_grad_ref[...] = jnp.zeros_like(rate_grad_ref)
+        taps_grad_ref[...] = jnp.zeros_like(taps_grad_ref)
+        grad_conv_ref[tiles * SUB :, :] = jnp.zeros((grad_conv_ref.shape[0] - tiles * SUB, inner), f32)
         for n in range(state):
             here = slice(n * SUB, (n + 1) * SUB)
             carry_ref[here, :] = post_state_ref[here, :] + post_decay_ref[here, :] * arriving_ref[n : n + 1, :]
 
-    spread(sel_ref, rank, state, tiles, inject_ref)
-    spread(sel_ref, rank + state, state, tiles, readout_ref)
+    spread(sel_ref, spots_ref, select_ref)
     sums_ref[...] = jnp.zeros_like(sums_ref)
 
     def columns(c, carry):
@@ -310,9 +386,9 @@
                 feeds = [None] * cols
                 new = ([], [])
                 for n in range(group):
-                    spot = at((i * state + first + n) * SUB, SUB)
-                    inject = inject_ref[spot, :]
-                    readout = readout_ref[spot, :]
+                    spot = slice((first + n) * LANE, (first + n + 1) * LANE)
+                    inject = select_ref[here, spot]
+                    readout = select_ref[here, (state + first + n) * LANE : (state + first + n + 1) * LANE]
                     if n % 2 == 0:
                         pair = pl.ds(pl.multiple_of((i * state + first + n) * SUB, 2 * SUB), 2 * SUB)
                         pairs = [prior_ref[pair, lanes[k]].astype(f32) for k in range(cols)]
@@ -331,7 +407,7 @@
                         feeds[k] = part if feeds[k] is None else feeds[k] + part
                         part = adjoint * drive[k]
                         total = part if total is None else total + part
-                    sums_ref[spot, :] += total
+                    sums_ref[here, spot] += total
                 for k in range(cols):
                     if first == 0:
                         through_ref[here, lanes[k]] = throughs[k]
@@ -342,14 +418,95 @@
                 return tuple(tuple(x) for x in new)
 
             start = tuple(tuple(ref[w] for w in where) for ref in (carry_ref, rate_grad_ref))
-            carries, rate_grads = lax.fori_loop(0, tiles, retreat, start, unroll=4)
+            carries, rate_grads = lax.fori_loop(0, tiles, retreat, start, unroll=16)
             for s, w in enumerate(where):
                 carry_ref[w] = carries[s]
                 rate_grad_ref[w] = rate_grads[s]
         return carry
 
     lax.fori_loop(0, inner // (LANE * cols), columns, 0)
-    gather_lanes(sums_ref, state, tiles, inject_grad_ref)
+    gather_lanes(sums_ref, spots_ref, inject_grad_ref)
+
+    def steps(c, carry):
+        lanes = at(c * 2 * LANE, 2 * LANE)
+
+        def pair(i, total):
+            here = at(i * 2 * SUB, 2 * SUB)
+            step = step_ref[here, lanes]
+            series = 1.0 + step * (-1.0 / 2 + step * (1.0 / 6 + step * (-1.0 / 24 + step * (1.0 / 120))))
+            near = step < 0.06
+            exact = (1.0 - jnp.exp2(step * -LOG2E)) / jnp.where(near, 1.0, step)
+            ratio = jnp.where(near, series, exact)
+            pre = ratio * (LN2 * through_ref[here, lanes] + drive_ref[here, lanes] * feed_ref[here, lanes])
+            grad_pre_ref[here, lanes] = pre.astype(bf16)
+            return total + pre[:SUB] + pre[SUB:]
+
+        zero = jnp.zeros((SUB, 2 * LANE), f32)
+        taps_grad_ref[(width + 1) * SUB :, lanes] += lax.fori_loop(0, tiles // 2, pair, zero, unroll=4)
+        return carry
+
+    lax.fori_loop(0, inner // (2 * LANE), steps, 0)
+    lane = lax.broadcasted_iota(jnp.int32, (block, LANE), 1)
+    rank = LANE - 2 * state
+    grads = jnp.dot(grad_pre_ref[...], step_back_ref[...], preferred_element_type=f32)
+    grads = jnp.where(
+        lane < state,
+        inject_grad_ref[...],
+        jnp.where(lane < 2 * state, pltpu.roll(readout_grad_ref[...], state, 1), grads),
+    )
+    grads = grads.astype(bf16)
+    grad_select_ref[...] = grads
+
+    def convs(c, carry):
+        lanes = at(c * 2 * LANE, 2 * LANE)
+        skip = skip_ref[:, lanes]
+        feeds = jnp.dot(grads, select_back_ref[:, lanes], preferred_element_type=f32)
+        through_ref[:, lanes] = feeds
+
+        def conv(i, carry):
+            here = at(i * SUB, SUB)
+            value = conv_sum_ref[here, lanes]
+            sig = jax.nn.sigmoid(value)
+            slope = sig * (1.0 + value * (1.0 - sig))
+            out = grad_ref[here, lanes] * skip + step_ref[here, lanes] * feed_ref[here, lanes] + through_ref[here, lanes]
+            grad_conv_ref[here, lanes] = out * slope
+            return carry
+
+        lax.fori_loop(0, tiles, conv, 0, unroll=8)
+        taps = [jnp.broadcast_to(taps_ref[k : k + 1, lanes], (SUB, 2 * LANE)) for k in range(width)]
+
+        def tap(i, totals):
+            totals = list(totals)
+            done = []
+            for q in range(2):
+                parts = [
+                    grad_conv_ref[pl.ds(pl.multiple_of((2 * i + q + m) * SUB, SUB), SUB), lanes] for m in range(width)
+                ]
+                stream = stream_ref[pl.ds(pl.multiple_of((2 * i + q) * SUB, SUB), SUB), lanes]
+                grad = taps[width - 1] * parts[0]
+                totals[width - 1] = totals[width - 1] + parts[0] * stream
+                totals[width] = totals[width] + parts[0]
+                for m in range(1, width):
+                    grad = grad + taps[width - 1 - m] * parts[m]
+                    totals[width - 1 - m] = totals[width - 1 - m] + parts[m] * stream
+                done.append(grad)
+            grad_stream_ref[at(i * 2 * SUB, 2 * SUB), lanes] = jnp.concatenate(done, 0).astype(bf16)
+            return tuple(totals)
+
+        zero = jnp.zeros((SUB, 2 * LANE), f32)
+        totals = lax.fori_loop(0, tiles // 2, tap, (zero,) * (width + 1), unroll=4)
+        for k in range(width + 1):
+            taps_grad_ref[k * SUB : (k + 1) * SUB, lanes] += totals[k]
+        return carry
+
+    lax.fori_loop(0, inner // (2 * LANE), convs, 0)
+
+    @pl.when(pl.program_id(0) == 0)
+    def _():
+        edge_ref[halo:, :] = grad_conv_ref[block - halo : block, :]
+
+    edge_ref[:halo, :] = grad_conv_ref[:halo, :]
+    grad_conv_ref[block:, :] = grad_conv_ref[:halo, :]
 
 
 def scan_shapes(rows, state, inner):
@@ -358,60 +515,71 @@
     return tiles, count
 
 
-def summary_call(step, drive, grad, sel, rates, rank):
+def summary_call(step, drive, grad, sel, spots, rates):
     rows, inner = step.shape
     state = rates.shape[0] // SUB
     tiles, count = scan_shapes(rows, state, inner)
     wide = pl.BlockSpec((tiles * SUB, inner), lambda t: (t, 0))
+    table = pl.BlockSpec(spots.shape, lambda t: (0, 0))
     thin = pl.BlockSpec((tiles * SUB, sel.shape[1]), lambda t: (t, 0))
     whole = pl.BlockSpec((state * SUB, inner), lambda t: (0, 0))
     total = pl.BlockSpec((3 * state, inner), lambda t: (0, 0))
-    shape = (tiles, state, inner, rank, 2, 4)
+    shape = (tiles, state, inner, 2, 4)
     big = jax.ShapeDtypeStruct((state * SUB, inner), f32)
     return pl.pallas_call(
         functools.partial(summary_kernel, shape),
         name="scan_summary",
         grid=(count,),
-        in_specs=[wide, wide, wide, thin, whole],
+        in_specs=[wide, wide, wide, thin, table, whole],
         out_specs=[whole] * 4 + [total],
         out_shape=[big] * 4 + [jax.ShapeDtypeStruct((3 * state, inner), f32)],
         scratch_shapes=[pltpu.VMEM((state * SUB, inner), f32)] * 3
-        + [pltpu.VMEM((tiles * state * SUB, LANE), f32)] * 2,
+        + [pltpu.VMEM((tiles * SUB, 2 * state * LANE), f32)],
         compiler_params=pltpu.CompilerParams(vmem_limit_bytes=VMEM_BYTES),
-    )(step, drive, grad, sel, rates)
-
-
-def forward_call(step, drive, grad, sel, rates, pre_decay, pre_state, entry, rank):
+    )(step, drive, grad, sel, spots, rates)
+
+
+def forward_call(step, drive, grad, sel, spots, rates, pre_decay, pre_state, entry, conv, gating, grad_gated, skip):
     rows, inner = step.shape
     state = rates.shape[0] // SUB
     tiles, count = scan_shapes(rows, state, inner)
     wide = pl.BlockSpec((tiles * SUB, inner), lambda t: (t, 0))
+    table = pl.BlockSpec(spots.shape, lambda t: (0, 0))
     thin = pl.BlockSpec((tiles * SUB, sel.shape[1]), lambda t: (t, 0))
     whole = pl.BlockSpec((state * SUB, inner), lambda t: (0, 0), pipeline_mode=pl.Buffered(1))
+    line = pl.BlockSpec((1, inner), lambda t: (0, 0))
     short = pl.BlockSpec((state, inner), lambda t: (0, 0))
-    shape = (tiles, state, inner, rank, 2, 8)
+    shape = (tiles, state, inner, 2, 8)
     return pl.pallas_call(
         functools.partial(forward_kernel, shape),
         name="scan_forward",
         grid=(count,),
-        in_specs=[wide, wide, wide, thin, whole, whole, whole, short],
+        in_specs=[wide, wide, wide, thin, table, whole, whole, whole, short, wide, wide, wide, line],
         out_specs=[
-            wide,
             pl.BlockSpec((tiles * state * SUB, inner), lambda t: (t, 0)),
             pl.BlockSpec((tiles * SUB, LANE), lambda t: (t, 0)),
+            wide,
+            wide,
+            pl.BlockSpec((SUB, inner), lambda t: (0, 0)),
         ],
         out_shape=[
-            jax.ShapeDtypeStruct((rows, inner), f32),
             jax.ShapeDtypeStruct((rows * state, inner), bf16),
             jax.ShapeDtypeStruct((rows, LANE), f32),
+            jax.ShapeDtypeStruct((rows, inner), bf16),
+            jax.ShapeDtypeStruct((rows, inner), bf16),
+            jax.ShapeDtypeStruct((SUB, inner), f32),
         ],
         scratch_shapes=[pltpu.VMEM((state * SUB, inner), f32)]
-        + [pltpu.VMEM((tiles * state * SUB, LANE), f32)] * 3,
+        + [
+            pltpu.VMEM((tiles * SUB, 2 * state * LANE), f32),
+            pltpu.VMEM((tiles * SUB, state * LANE), f32),
+            pltpu.VMEM((tiles * SUB, inner), f32),
+        ],
         compiler_params=pltpu.CompilerParams(vmem_limit_bytes=VMEM_BYTES),
-    )(step, drive, grad, sel, rates, pre_decay, pre_state, entry)
-
-
-def backward_call(step, drive, grad, sel, rates, post_decay, post_state, arriving, prior, rank):
+    )(step, drive, grad, sel, spots, rates, pre_decay, pre_state, entry, conv, gating, grad_gated, skip)
+
+
+def backward_call(step, drive, grad, sel, spots, rates, post_decay, post_state, arriving, prior, conv_sum, stream, readout_grad, step_back, select_back, taps, skip):
     rows, inner = step.shape
     state = rates.shape[0] // SUB
     tiles, count = scan_shapes(rows, state, inner)
@@ -420,32 +588,68 @@
         return (count - 1 - t, 0)
 
     wide = pl.BlockSpec((tiles * SUB, inner), back)
+    table = pl.BlockSpec(spots.shape, lambda t: (0, 0))
     thin = pl.BlockSpec((tiles * SUB, sel.shape[1]), back)
     whole = pl.BlockSpec((state * SUB, inner), lambda t: (0, 0), pipeline_mode=pl.Buffered(1))
     short = pl.BlockSpec((state, inner), lambda t: (0, 0))
-    shape = (tiles, state, inner, rank, 2, 4)
+    narrow = pl.BlockSpec((tiles * SUB, LANE), back)
+    width = taps.shape[0]
+    halo = (width - 1) * SUB
+
+    def fixed(x):
+        return pl.BlockSpec(x.shape, lambda t: (0, 0), pipeline_mode=pl.Buffered(1))
+
+    shape = (tiles, state, inner, 2, 4)
     return pl.pallas_call(
         functools.partial(backward_kernel, shape),
         name="scan_backward",
         grid=(count,),
-        in_specs=[wide, wide, wide, thin, whole, whole, whole, short]
-        + [pl.BlockSpec((tiles * state * SUB, inner), back)],
+        in_specs=[wide, wide, wide, thin, table, whole, whole, whole, short]
+        + [pl.BlockSpec((tiles * state * SUB, inner), back), wide, wide, narrow]
+        + [fixed(step_back), fixed(select_back), fixed(taps), fixed(skip)],
         out_specs=[
             wide,
             wide,
-            pl.BlockSpec((tiles * SUB, LANE), back),
+            narrow,
             pl.BlockSpec((state * SUB, inner), lambda t: (0, 0)),
+            pl.BlockSpec(((width + 2) * SUB, inner), lambda t: (0, 0)),
+            pl.BlockSpec((2 * halo, inner), lambda t: (0, 0)),
         ],
         out_shape=[
-            jax.ShapeDtypeStruct((rows, inner), f32),
-            jax.ShapeDtypeStruct((rows, inner), f32),
-            jax.ShapeDtypeStruct((rows, LANE), f32),
+            jax.ShapeDtypeStruct((rows, inner), bf16),
+            jax.ShapeDtypeStruct((rows, inner), bf16),
+            jax.ShapeDtypeStruct((rows, LANE), bf16),
             jax.ShapeDtypeStruct((state * SUB, inner), f32),
+            jax.ShapeDtypeStruct(((width + 2) * SUB, inner), f32),
+            jax.ShapeDtypeStruct((2 * halo, inner), f32),
         ],
         scratch_shapes=[pltpu.VMEM((state * SUB, inner), f32)]
-        + [pltpu.VMEM((tiles * state * SUB, LANE), f32)] * 3,
-        compiler_params=pltpu.CompilerParams(vmem_limit_bytes=VMEM_BYTES),
-    )(step, drive, grad, sel, rates, post_decay, post_state, arriving, prior)
+        + [
+            pltpu.VMEM((tiles * SUB, 2 * state * LANE), f32),
+            pltpu.VMEM((tiles * SUB, state * LANE), f32),
+            pltpu.VMEM((tiles * SUB, inner), f32),
+            pltpu.VMEM((tiles * SUB, inner), f32),
+            pltpu.VMEM((tiles * SUB + halo, inner), f32),
+            pltpu.VMEM((tiles * SUB, LANE), f32),
+            pltpu.VMEM((2, SUB, LANE), f32),
+            pltpu.SemaphoreType.DMA((2,)),
+        ],
+        compiler_params=pltpu.CompilerParams(vmem_limit_bytes=VMEM_BYTES, collective_id=2, has_side_effects=True),
+    )(step, drive, grad, sel, spots, rates, post_decay, post_state, arriving, prior, conv_sum, stream, readout_grad, step_back, select_back, taps, skip)
+
+
+def turn_tiles(tiles):
+    row = lax.broadcasted_iota(jnp.int32, (SUB, LANE), 0)
+    for bit in (1, 2, 4):
+        upper = (row // bit) % 2 == 1
+        new = list(tiles)
+        for a in range(SUB):
+            if a & bit == 0:
+                b = a + bit
+                new[a] = jnp.where(upper, pltpu.roll(tiles[b], bit, 0), tiles[a])
+                new[b] = jnp.where(upper, tiles[b], pltpu.roll(tiles[a], SUB - bit, 0))
+        tiles = new
+    return tiles
 
 
 def flatten_kernel(rows_in, rows_out, in_base, small_base, out_base, stream_ref, gate_ref, out_w_ref, gain_ref, small_ref, flat_ref, in_buf, out_buf, sems):
@@ -484,18 +688,20 @@
         for copy in copies(turn - 2, slot):
             copy.wait()
 
+    def lay(src, rows, first, buf, base, stride):
+        tiles = [src[rows, (first + a) * LANE : (first + a + 1) * LANE] for a in range(SUB)]
+        for r, tile in enumerate(turn_tiles(tiles)):
+            buf[slot, base + r * stride] = tile
+
+    per = wide // SUB
     for r in range(rows_in // SUB):
         rows = slice(r * SUB, (r + 1) * SUB)
-        for a in range(wide):
-            src = stream_ref if a < half else gate_ref
-            tile = src[rows, (a % half) * LANE : (a % half + 1) * LANE]
-            for_tile = in_buf.at[slot, r * wide : (r + 1) * wide]
-            for_tile[pl.ds(a // SUB, SUB, stride=wide // SUB), a % SUB, :] = tile
-    deep = out_w_ref.shape[1] // LANE
+        for q in range(per):
+            src = stream_ref if q < per // 2 else gate_ref
+            lay(src, rows, (q % (per // 2)) * SUB, in_buf, r * wide + q, per)
     for r in range(rows_out // SUB):
         rows = slice(r * SUB, (r + 1) * SUB)
-        for a in range(deep):
-            out_buf[slot, rows, a, :] = out_w_ref[rows, a * LANE : (a + 1) * LANE]
+        lay(out_w_ref, rows, 0, out_buf, r * SUB, 1)
     for copy in copies(turn, slot):
         copy.start()
 
@@ -966,6 +1172,7 @@
     conv_val = conv_low.astype(f32)
     selectors = jnp.dot(conv_low, xproj_weight, preferred_element_type=f32)
     step_low = selectors[:, :rank].astype(bf16)
+    terms, spots = split_selectors(selectors[:, rank:])
     step_pre = jnp.dot(step_low, dt_weight, preferred_element_type=f32) + dt_bias
     step_size = jax.nn.softplus(step_pre)
     drive = step_size * conv_val
@@ -976,57 +1183,77 @@
     rates_wide = jnp.repeat(rates * LOG2E, SUB, axis=0)
 
     pre_decay, pre_state, post_decay, post_state, totals = summary_call(
-        step_size, drive, grad_scanned, selectors, rates_wide, rank
+        step_size, drive, grad_scanned, terms, spots, rates_wide
     )
     entry, arriving = exchange(totals, state)
-    scan_out, prior, readout_grads = forward_call(
-        step_size, drive, grad_scanned, selectors, rates_wide, pre_decay, pre_state, entry, rank
+    prior, readout_grads, gated, grad_gating, skip_grads = forward_call(
+        step_size,
+        drive,
+        grad_scanned,
+        terms,
+        spots,
+        rates_wide,
+        pre_decay,
+        pre_state,
+        entry,
+        conv_low,
+        gating,
+        grad_gated,
+        d_skip[None],
     )
-    scanned = scan_out + d_skip * conv_val
-    gated = (scanned * gate_val).astype(bf16)
     output = jnp.dot(gated, out_weight, preferred_element_type=f32)
     result = restore((source + output).astype(bf16))[None]
     grad_out_weight = lax.dot_general(gated, cot_low, contract, preferred_element_type=f32)
-    grad_gating = (grad_gated * scanned * (gate_sig * (1.0 + gating * (1.0 - gate_sig)))).astype(bf16)
     grad_in_gate = lax.dot_general(normed, grad_gating, contract, preferred_element_type=f32)
-    grad_d_skip = jnp.sum(grad_scanned * conv_val, 0)
-
-    through, feed, inject_grads, rate_grads = backward_call(
-        step_size, drive, grad_scanned, selectors, rates_wide, post_decay, post_state, arriving, prior, rank
+    grad_d_skip = jnp.sum(skip_grads, 0)
+
+    spare = LANE - rank - 2 * state
+    step_back = jnp.pad(dt_weight, ((2 * state, spare), (0, 0))).T
+    select_back = jnp.pad(jnp.roll(xproj_weight, 2 * state, 1), ((0, 0), (0, spare))).T
+    grad_stream_low, grad_pre_low, grad_selectors, rate_grads, taps_grads, edges = backward_call(
+        step_size,
+        drive,
+        grad_scanned,
+        terms,
+        spots,
+        rates_wide,
+        post_decay,
+        post_state,
+        arriving,
+        prior,
+        conv_sum,
+        stream,
+        readout_grads,
+        step_back,
+        select_back,
+        conv_weight,
+        d_skip[None],
     )
     grad_a_log = LN2 * jnp.sum(rate_grads.reshape(state, SUB, inner), 1)
-    step_sig = jax.nn.sigmoid(step_pre)
-    tiny = step_size < 1e-30
-    ratio = jnp.where(tiny, 1.0, step_sig / jnp.where(tiny, 1.0, step_size))
-    grad_pre = LN2 * through * ratio + conv_val * feed * step_sig
-    grad_dt_bias = jnp.sum(grad_pre, 0)
-    grad_pre_low = grad_pre.astype(bf16)
+    begins = edges[:halo].reshape(width - 1, SUB, inner)
+    ahead = shifted(begins[:, 0], "blk", -1)
     grad_dt_weight = lax.dot_general(step_low, grad_pre_low, contract, preferred_element_type=f32)
-    grad_step_low = lax.dot_general(grad_pre_low, dt_weight, backward, preferred_element_type=f32)
-    grad_selectors = jnp.concatenate(
-        [grad_step_low, inject_grads[:, :state], readout_grads[:, :state]], 1
-    ).astype(bf16)
     grad_xproj = lax.dot_general(conv_low, grad_selectors, contract, preferred_element_type=f32)
-    grad_conv_out = (
-        grad_scanned * d_skip
-        + step_size * feed
-        + lax.dot_general(grad_selectors, xproj_weight, backward, preferred_element_type=f32)
-    )
-    grad_conv = grad_conv_out * silu_slope(conv_sum)
-    begins = grad_conv[:halo].reshape(width - 1, SUB, inner)
-    ahead = shifted(begins[:, 0], "blk", -1)
-    foot = jnp.concatenate([begins[:, 1:], ahead[:, None]], 1).reshape(halo, inner)
-    further = jnp.concatenate([grad_conv, foot], 0)
-    grad_stream = conv_weight[width - 1] * grad_conv
+    grad_xproj = jnp.roll(grad_xproj[:, : rank + 2 * state], rank, 1)
+    foot = jnp.concatenate([begins[:, 1:], ahead[:, None]], 1)
+    lasts = edges[halo:].reshape(width - 1, SUB, inner)
+    further = jnp.concatenate([lasts, foot], 0)
+    last_stream = stream[length - halo :].reshape(width - 1, SUB, inner)
+    grad_last = conv_weight[width - 1] * lasts
+    taps_grads = jnp.sum(taps_grads.reshape(width + 2, SUB, inner), 1)
     tap_grads = []
     for offset in range(width - 1):
         lead = width - 1 - offset
-        grad_stream = grad_stream + conv_weight[offset] * further[lead * SUB : lead * SUB + length]
-        tap_grads.append(jnp.sum(grad_conv * delayed(lead), 0))
-    tap_grads.append(jnp.sum(grad_conv * stream, 0))
+        grad_last = grad_last + conv_weight[offset] * further[lead : lead + width - 1]
+        over = jnp.sum(last_stream[width - 1 - lead :] * foot[:lead], (0, 1))
+        tap_grads.append(taps_grads[offset] + over)
+    tap_grads.append(taps_grads[width - 1])
     grad_conv_weight = jnp.stack(tap_grads, 0)
-    grad_conv_bias = jnp.sum(grad_conv, 0)
-    grad_stream_low = grad_stream.astype(bf16)
+    grad_conv_bias = taps_grads[width]
+    grad_dt_bias = taps_grads[width + 1]
+    grad_stream_low = lax.dynamic_update_slice_in_dim(
+        grad_stream_low, grad_last.reshape(halo, inner).astype(bf16), length - halo, 0
+    )
     grad_in_stream = lax.dot_general(normed, grad_stream_low, contract, preferred_element_type=f32)
     grad_normed = lax.dot_general(
         jnp.concatenate([grad_stream_low, grad_gating], 1), in_weight, backward, preferred_element_type=f32

time: 777 us -> 680 us (0.88)
  Pallas kernels: 514 us -> 461 us
  matrix products: 126 us -> 91.3 us
  other arithmetic: 79.8 us -> 61.6 us
    reduce_sum x2 -> x5, other arithmetic: 48.1 us -> 5.33 us  [the longest x3 4.6 us: local(): over = jnp.sum(last_stream[width - 1 - lead:] * foot[:lead], (0, 1))]
    pallas_call x1, Pallas kernels: 98.1 us -> 71.2 us  [forward_call(): pl.pallas_call(functools.partial(forward_kernel, shape), name='scan_forwa...]
    pallas_call x1, Pallas kernels: 83.9 us -> 57.6 us  [summary_call(): pl.pallas_call(functools.partial(summary_kernel, shape), name='scan_summa...]
    convert_element_type x0 -> x2, other arithmetic: none -> 20.6 us  [the longest x1 19.2 us: local(): conv_low = (conv_sum * jax.nn.sigmoid(conv_sum)).astype(bf16)]
    dot_general x2 -> x0, matrix products: 16.4 us -> none  [the longest x1 15 us: local(): lax.dot_general(grad_selectors, xproj_weight, backward, preferred_element...]
  transfers between devices with their start and end apart: 5 -> 5, of which waited for: 2 -> 2; matrix products, arithmetic and copies ran while one was open for 5% -> 7% of each run, Pallas kernels for 0% -> 0%
where the time goes in v2:
time: 680 us; the launch traced here: 672 us
  Pallas kernels  461 us (68%)
  matrix products  91.3 us (13%)
  other arithmetic  61.6 us (9%)
  local copies, waits for them, and re-layouts  30 us (4%)
  waiting for transfers between devices  15.4 us (2%)
  starting transfers between devices  9.79 us (1%)
    pallas_call x1, Pallas kernels, reduce_call(): pl.pallas_call(functools.partial(reduce_kernel, depth, bits, phases, half...  168 us
    pallas_call x1, Pallas kernels, backward_call(): pl.pallas_call(functools.partial(backward_kernel, shape), name='scan_back...  116 us
    pallas_call x1, Pallas kernels, forward_call(): pl.pallas_call(functools.partial(forward_kernel, shape), name='scan_forwa...  71.2 us
    pallas_call x1, Pallas kernels, summary_call(): pl.pallas_call(functools.partial(summary_kernel, shape), name='scan_summa...  57.6 us
    pallas_call x1, Pallas kernels, flatten_call(): pl.pallas_call(functools.partial(flatten_kernel, rows_in, rows_out, in_ba...  48 us
    convert_element_type x1, other arithmetic, local(): conv_low = (conv_sum * jax.nn.sigmoid(conv_sum)).astype(bf16)  19.2 us
    dot_general x1, matrix products, local(): lax.dot_general(jnp.concatenate([grad_stream_low, grad_gating], 1), in_we...  18.1 us
    ppermute x3, waiting for transfers between devices, exchange(): far = lax.ppermute(jnp.concatenate([decay, end, leave], 0), 'blk', pairs)  15.4 us
  transfers between devices with their start and end apart: 5, of which 2 were waited for; matrix products, arithmetic and copies ran while one was open for 7% of the time, Pallas kernels for 0%

profile of v2, /device:TPU:0, one launch (start us, length us, event | category | flops | bytes accessed | tf_op | source)
XLA Modules:
  0.0 672.0 jit_solution(13479482367908495488)
XLA Ops:
  0.6 2.1 multiply_reduce_fusion
  2.7 4.0 convert.34
  7.0 4.9 fusion.13
  11.9 7.1 %fusion.24.stream_ref = f32[1024,2048]{1,0:T(8,128)S(1)} fusion(bf16[1024,1024]{1,0:T(8,128)(2,1)S(1)} %fusion.13, bf16[1024,4096]{1,0:T(8,128)(2,1)} %param.17), kind=kOutput, calls=%fused_computation.36 | convolution fusion | flops 4294967296 | bytes 14680064 | tf_op jit(solution)/shard_map/dot_general | solution.py:1157
  19.1 2.8 collective-permute-start
  21.9 4.5 fusion.22.gating_ref
  27.9 14.4 %multiply_multiply_fusion = (f32[1024,2048]{1,0:T(8,128)}, f32[1024,2048]{1,0:T(8,128)}) fusion(f32[1024,2048]{1,0:T(8,128)S(1)} %fusion.22.gating_ref, bf16[2048,1024]{1,0:T(8,128)(2,1)} %param.25, bf16[8,128,1024]{2,1,0:T(8,128)(2,1)S(1)} %bitcast.140), kind=kOutput, calls=%fused_computation.16 | convolution fusion | flops 4305453056 | bytes 31457280 | tf_op jit(solution)/shard_map/dot_general | solution.py:1161
  43.8 19.2 %multiply_convert_fusion = (bf16[1024,2048]{1,0:T(8,128)(2,1)S(1)}, f32[1024,2048]{1,0:T(8,128)}) fusion(f32[1024,2048]{1,0:T(8,128)} %copy-done.4, f32[24,2048]{1,0:T(8,128)S(1)} %maximum_bitcast_fusion, f32[2048]{0:T(1024)S(1)} %bitcast.147, f32[2048]{0:T(1024)S(1)} %bitcast.149, f32[2048]{0:T(1024)S(1)} %bitcast.151, f32[2048]{0:T(1024)S(1)} %bitcast.145, ...), kind=kLoop, calls=%fused_computation.18 | loop fusion | flops 33554432 | bytes 21209088 | tf_op jit(solution)/shard_map/convert_element_type | solution.py:1171
  63.1 2.0 copy-done
  66.9 10.5 %convert_multiply_fusion = (f32[1024,2048]{1,0:T(8,128)}, f32[1024,2048]{1,0:T(8,128)}) fusion(bf16[1024,2048]{1,0:T(8,128)(2,1)} %copy-done, f32[2048]{0:T(1024)S(1)} %copy-done.42, bf16[64,2048]{1,0:T(8,128)(2,1)S(1)} %copy-done.20, f32[1024,96]{0,1:T(8,128)S(1)} %fusion.77), kind=kOutput, calls=%fused_computation.17 | convolution fusion | flops 287309824 | bytes 21372928 | tf_op jit(solution)/shard_map/dot_general | solution.py:1176
  78.4 57.6 %scan_summary.1 = (f32[128,2048]{1,0:T(8,128)}, f32[128,2048]{1,0:T(8,128)}, f32[128,2048]{1,0:T(8,128)}, f32[128,2048]{1,0:T(8,128)}, f32[48,2048]{1,0:T(8,128)}) custom-call(f32[1024,2048]{1,0:T(8,128)} %get-tuple-element.75.step_ref, f32[1024,2048]{1,0:T(8,128)} %get-tuple-element.74.drive_ref, f32[1024,2048]{1,0:T(8,128)} %get-tuple-element.76.grad_ref, ...), custom_call_target="tpu_custom_call" | custom-call | tf_op jit(solution)/shard_map/scan_summary/pallas_call | solution.py:529
  136.0 2.5 collective-permute-start.1
  150.0 8.1 %collective-permute-done.2 = f32[48,2048]{1,0:T(8,128)} collective-permute-done((f32[48,2048]{1,0:T(8,128)}, f32[48,2048]{1,0:T(8,128)}, u32[]{:S(2)}, u32[]{:S(2)}) %collective-permute-start.2) | collective-permute-done | bytes 393248 | tf_op jit(solution)/shard_map/ppermute | solution.py:1114
  159.4 1.6 collective-permute-start.3
  162.4 7.2 %collective-permute-done.3 = f32[48,2048]{1,0:T(8,128)S(1)} collective-permute-done((f32[48,2048]{1,0:T(8,128)S(1)}, f32[48,2048]{1,0:T(8,128)S(1)}, u32[]{:S(2)}, u32[]{:S(2)}) %collective-permute-start.3) | collective-permute-done | bytes 393248 | tf_op jit(solution)/shard_map/ppermute | solution.py:1114
  169.6 2.0 add_select_fusion
  171.6 71.2 %scan_forward.1 = (bf16[16384,2048]{1,0:T(8,128)(2,1)}, f32[1024,128]{1,0:T(8,128)}, bf16[1024,2048]{1,0:T(8,128)(2,1)}, bf16[1024,2048]{1,0:T(8,128)(2,1)}, f32[8,2048]{1,0:T(8,128)}) custom-call(f32[1024,2048]{1,0:T(8,128)} %get-tuple-element.75.step_ref, f32[1024,2048]{1,0:T(8,128)} %get-tuple-element.74.drive_ref, ...), custom_call_target="tpu_custom_call" | custom-call | tf_op jit(solution)/shard_map/scan_forward/pallas_call | solution.py:553
  242.9 116.0 %scan_backward.1 = (bf16[1024,2048]{1,0:T(8,128)(2,1)}, bf16[1024,2048]{1,0:T(8,128)(2,1)}, bf16[1024,128]{1,0:T(8,128)(2,1)}, f32[128,2048]{1,0:T(8,128)}, f32[48,2048]{1,0:T(8,128)}, /*index=5*/f32[48,2048]{1,0:T(8,128)}) custom-call(f32[1024,2048]{1,0:T(8,128)} %get-tuple-element.75.step_ref, f32[1024,2048]{1,0:T(8,128)} %get-tuple-element.74.drive_ref, ...), custom_call_target="tpu_custom_call" | custom-call | tf_op jit(solution)/shard_map/scan_backward/pallas_call | solution.py:603
  359.0 1.9 fusion.80
  361.9 7.4 %fusion.28.out_w_ref = f32[2048,1024]{1,0:T(8,128)} fusion(bf16[1024,2048]{1,0:T(8,128)(2,1)S(1)} %copy-done.44, bf16[8,128,1024]{2,1,0:T(8,128)(2,1)S(1)} %bitcast.141), kind=kOutput, calls=%fused_computation.42 | convolution fusion | flops 4294967296 | bytes 14680064 | tf_op jit(solution)/shard_map/dot_general | solution.py:1206
  369.3 7.4 %fusion.27 = bf16[8,128,1024]{2,0,1:T(8,128)(2,1)} fusion(f32[8,128,1024]{2,1,0:T(8,128)S(1)} %copy-done.2, bf16[1024,2048]{1,0:T(8,128)(2,1)S(1)} %copy-done.44, bf16[2048,1024]{1,0:T(8,128)(2,1)S(1)} %copy-done.35), kind=kOutput, calls=%fused_computation.41 | convolution fusion | flops 4297064448 | bytes 14680064 | tf_op jit(solution)/shard_map/dot_general | solution.py:1204
  380.7 6.9 %fusion.79.gate_ref = f32[1024,2048]{1,0:T(8,128)} fusion(bf16[1024,1024]{1,0:T(8,128)(2,1)S(1)} %copy-done.10, bf16[1024,2048]{1,0:T(8,128)(2,1)S(1)} %copy-done.43), kind=kOutput, calls=%fused_computation.169 | convolution fusion | flops 4294967296 | bytes 14680064 | tf_op jit(solution)/shard_map/dot_general | solution.py:1207
  390.6 1.6 mul.333
  392.2 4.1 copy.57
  397.7 1.6 fusion.56
  403.1 10.8 %fusion.78.stream_ref = f32[1024,2048]{1,0:T(8,128)} fusion(bf16[1024,1024]{1,0:T(8,128)(2,1)} %copy-done.9, bf16[1024,2048]{1,0:T(8,128)(2,1)} %bitcast_dynamic-update-slice_fusion), kind=kOutput, calls=%fused_computation.168 | convolution fusion | flops 4294967296 | bytes 14680064 | tf_op jit(solution)/shard_map/dot_general | solution.py:1257
  413.9 18.1 %fusion.21 = (f32[1024]{0:T(1024)}, f32[1024]{0:T(1024)S(1)}, f32[1024,1024]{1,0:T(8,128)}) fusion(f32[8,128,1024]{2,1,0:T(8,128)S(1)} %copy-done.3, f32[1024]{0:T(1024)S(1)} %rsqrt.15, f32[1024]{0:T(1024)S(1)} %copy-done.37, bf16[1024,4096]{1,0:T(8,128)(2,1)} %param.17, bf16[1024,2048]{1,0:T(8,128)(2,1)} %get-tuple-element.35, ...), kind=kOutput, calls=%fused_computation.33 | convolution fusion | flops 8613001216 | bytes 25182208 | tf_op jit(solution)/shard_map/dot_general | solution.py:1258
  437.3 48.0 %flatten.1.flat_ref = f32[6719,8,128]{2,1,0:T(8,128)} custom-call(f32[1024,2048]{1,0:T(8,128)} %fusion.78.stream_ref, f32[1024,2048]{1,0:T(8,128)} %fusion.79.gate_ref, f32[2048,1024]{1,0:T(8,128)} %fusion.28.out_w_ref, f32[1,8,128]{2,1,0:T(8,128)} %bitcast.165, f32[366,8,128]{2,1,0:T(8,128)} %copy-done.17), custom_call_target="tpu_custom_call" | custom-call | tf_op jit(solution)/shard_map/flatten/pallas_call | solution.py:726
  485.3 168.2 %reduce_gradients.1 = (f32[208,8,128]{2,1,0:T(8,128)}, f32[8,128]{1,0:T(8,128)}) custom-call(f32[6719,8,128]{2,1,0:T(8,128)} %flatten.1.flat_ref), custom_call_target="tpu_custom_call" | custom-call | tf_op jit(solution)/shard_map/reduce_gradients/pallas_call | solution.py:1044
  655.4 11.0 %fusion.26 = bf16[8,128,1024]{2,0,1:T(8,128)(2,1)S(1)} fusion(f32[8,128,1024]{2,1,0:T(8,128)} %convert.34, f32[1024,1024]{1,0:T(8,128)} %get-tuple-element.78, f32[1024]{0:T(1024)S(1)} %broadcast_multiply_fusion.1, f32[1024]{0:T(1024)S(1)} %copy-done.41, f32[1024]{0:T(1024)S(1)} %copy-done.37, f32[1024]{0:T(1024)S(1)} %rsqrt.15, ...), kind=kLoop, calls=%fused_computation.40 | loop fusion | flops 8388608 | bytes 12599296 | tf_op jit(solution)/shard_map/transpose | solution.py:51
  666.4 2.5 copy.60
  668.9 2.7 add_multiply_fusion
  (182 shorter events, 39.2 us)
Async XLA Ops:
  7.0 14.9 %slice-start.4 = ((s8[8388608]{0:T(1024)(128)(4,1)}), s8[4194304]{0:T(1024)(128)(4,1)S(1)}, s32[]{:S(2)}) async-start(s8[8388608]{0:T(1024)(128)(4,1)} %bitcast.163), calls=%async_computation.4 | async-start | bytes 8388608
  11.9 10.0 %copy-start.9 = (bf16[1024,1024]{1,0:T(8,128)(2,1)}, bf16[1024,1024]{1,0:T(8,128)(2,1)S(1)}, u32[]{:S(2)}) copy-start(bf16[1024,1024]{1,0:T(8,128)(2,1)S(1)} %fusion.13) | copy-start | bytes 6291460
  11.9 10.0 %slice-start.5 = ((s8[8388608]{0:T(1024)(128)(4,1)}), s8[4194304]{0:T(1024)(128)(4,1)S(1)}, s32[]{:S(2)}) async-start(s8[8388608]{0:T(1024)(128)(4,1)} %bitcast.163), calls=%async_computation.5 | async-start | bytes 8388608
  19.1 8.7 %copy-start.12 = (bf16[1,1024,1024]{2,1,0:T(8,128)(2,1)S(1)}, bf16[1,1024,1024]{2,1,0:T(8,128)(2,1)}, u32[]{:S(2)}) copy-start(bf16[1,1024,1024]{2,1,0:T(8,128)(2,1)} %param.15) | copy-start | bytes 6291460
  19.1 24.6 %collective-permute-start = (f32[3,2048]{1,0:T(4,128)S(1)}, f32[3,2048]{1,0:T(4,128)S(1)}, u32[]{:S(2)}, u32[]{:S(2)}) collective-permute-start(f32[3,2048]{1,0:T(4,128)S(1)} %bitcast.155), channel_id=1, source_target_pairs={{0,1},{1,2},{2,3},{3,4},{4,5},{5,6},{6,7},{8,9},{9,10},{10,11},{11... | collective-permute-start | bytes 73736 | tf_op jit(solution)/shard_map/ppermute | solution.py:36
  26.5 15.8 %copy-start.5 = (f32[1024,2048]{1,0:T(8,128)}, f32[1024,2048]{1,0:T(8,128)S(1)}, u32[]{:S(2)}) copy-start(f32[1024,2048]{1,0:T(8,128)S(1)} %fusion.22.gating_ref) | copy-start | bytes 25165828
  27.8 15.8 %copy-start.30 = (f32[4,2048]{1,0:T(4,128)S(1)}, f32[4,2048]{1,0:T(4,128)}, u32[]{:S(2)}) copy-start(f32[4,2048]{1,0:T(4,128)} %taps_ref.1) | copy-start | bytes 98308
  27.9 16.0 %copy-start.38 = (f32[2048]{0:T(1024)S(1)}, f32[2048]{0:T(1024)}, u32[]{:S(2)}) copy-start(f32[2048]{0:T(1024)} %param.19) | copy-start | bytes 24580
  43.6 19.4 %copy-start.31 = (f32[1,2048]{1,0:T(1,128)}, f32[1,2048]{1,0:T(1,128)S(1)}, u32[]{:S(2)}) copy-start(f32[1,2048]{1,0:T(1,128)S(1)} %get-tuple-element.73) | copy-start | bytes 24580
  43.8 21.2 %copy-start.8 = (bf16[2048,96]{0,1:T(8,128)(2,1)S(1)}, bf16[2048,96]{0,1:T(8,128)(2,1)}, u32[]{:S(2)}) copy-start(bf16[2048,96]{0,1:T(8,128)(2,1)} %param.20) | copy-start | bytes 1179652
  66.5 10.9 %copy-start.15 = (f32[1024,96]{0,1:T(8,128)}, f32[1024,96]{0,1:T(8,128)S(1)}, u32[]{:S(2)}) copy-start(f32[1024,96]{0,1:T(8,128)S(1)} %fusion.77) | copy-start | bytes 1179652
  136.0 8.7 %collective-permute-start.1 = (f32[48,2048]{1,0:T(8,128)}, f32[48,2048]{1,0:T(8,128)}, u32[]{:S(2)}, u32[]{:S(2)}) collective-permute-start(f32[48,2048]{1,0:T(8,128)} %get-tuple-element.27), channel_id=1, source_target_pairs={{0,1},{1,0},{2,3},{3,2},{4,5},{5,4},{6,7},{7,6},{8,9},{9,8},{10,11... | collective-permute-start | bytes 1179656 | tf_op jit(solution)/shard_map/ppermute | solution.py:1114
  146.0 15.6 %slice-start.2 = ((bf16[2048,96]{0,1:T(8,128)(2,1)}), bf16[2048,64]{0,1:T(8,128)(2,1)S(1)}, s32[]{:S(2)}) async-start(bf16[2048,96]{0,1:T(8,128)(2,1)} %param.20), calls=%async_computation.2 | async-start | bytes 524288 | tf_op jit(solution)/shard_map/jit(_roll_static)/slice | solution.py:1212
  146.0 15.6 %slice-start.3 = ((bf16[2048,96]{0,1:T(8,128)(2,1)}), bf16[2048,32]{0,1:T(8,128)(2,1)S(1)}, s32[]{:S(2)}) async-start(bf16[2048,96]{0,1:T(8,128)(2,1)} %param.20), calls=%async_computation.3 | async-start | bytes 262144 | tf_op jit(solution)/shard_map/jit(_roll_static)/slice | solution.py:1212
  146.8 11.4 %collective-permute-start.2 = (f32[48,2048]{1,0:T(8,128)}, f32[48,2048]{1,0:T(8,128)}, u32[]{:S(2)}, u32[]{:S(2)}) collective-permute-start(f32[48,2048]{1,0:T(8,128)} %pad_maximum_fusion.2), channel_id=1, source_target_pairs={{0,2},{1,3},{2,0},{3,1},{4,6},{5,7},{6,4},{7,5},{8,10},{9,11},{10,... | collective-permute-start | bytes 1179656 | tf_op jit(solution)/shard_map/ppermute | solution.py:1114
  159.4 10.3 %collective-permute-start.3 = (f32[48,2048]{1,0:T(8,128)S(1)}, f32[48,2048]{1,0:T(8,128)S(1)}, u32[]{:S(2)}, u32[]{:S(2)}) collective-permute-start(f32[48,2048]{1,0:T(8,128)S(1)} %pad_maximum_fusion.3), channel_id=1, source_target_pairs={{0,4},{1,5},{2,6},{3,7},{4,0},{5,1},{6,2},{7,3},{8,12},{9,13},{10,... | collective-permute-start | bytes 1179656 | tf_op jit(solution)/shard_map/ppermute | solution.py:1114
  242.9 116.1 %copy-start.1 = (bf16[1024,2048]{1,0:T(8,128)(2,1)S(1)}, bf16[1024,2048]{1,0:T(8,128)(2,1)}, u32[]{:S(2)}) copy-start(bf16[1024,2048]{1,0:T(8,128)(2,1)} %copy-done) | copy-start | bytes 12582916
  360.8 8.4 %copy-start.7 = (f32[2048,128]{0,1:T(8,128)}, f32[2048,128]{0,1:T(8,128)S(1)}, u32[]{:S(2)}) copy-start(f32[2048,128]{0,1:T(8,128)S(1)} %fusion.80) | copy-start | bytes 3145732
  369.3 9.6 %copy-start.6 = (bf16[1024,2048]{1,0:T(8,128)(2,1)S(1)}, bf16[1024,2048]{1,0:T(8,128)(2,1)}, u32[]{:S(2)}) copy-start(bf16[1024,2048]{1,0:T(8,128)(2,1)} %get-tuple-element.38) | copy-start | bytes 12582916
  369.3 9.6 %copy-start.16 = (f32[1024,96]{0,1:T(8,128)S(1)}, f32[1024,96]{0,1:T(8,128)}, u32[]{:S(2)}) copy-start(f32[1024,96]{0,1:T(8,128)} %copy-done.15) | copy-start | bytes 1179652
  369.3 11.4 %copy-start.43 = (bf16[1024,2048]{1,0:T(8,128)(2,1)S(1)}, bf16[1024,2048]{1,0:T(8,128)(2,1)}, u32[]{:S(2)}) copy-start(bf16[1024,2048]{1,0:T(8,128)(2,1)} %get-tuple-element.35) | copy-start | bytes 12582916
  377.5 19.4 %collective-permute-start.4 = (f32[3,2048]{1,0:T(4,128)S(1)}, f32[3,2048]{1,0:T(4,128)}, u32[]{:S(2)}, u32[]{:S(2)}) collective-permute-start(f32[3,2048]{1,0:T(4,128)S(1)} %bitcast.157), channel_id=1, source_target_pairs={{1,0},{2,1},{3,2},{4,3},{5,4},{6,5},{7,6},{9,8},{10,9},{11,10},{12... | collective-permute-start | bytes 73736 | tf_op jit(solution)/shard_map/ppermute | solution.py:36
  388.2 8.0 %copy-start.34 = (f32[8,2048]{1,0:T(8,128)S(1)}, f32[8,2048]{1,0:T(8,128)}, u32[]{:S(2)}) copy-start(f32[8,2048]{1,0:T(8,128)} %get-tuple-element.40) | copy-start | bytes 196612
  388.2 14.0 %copy-start.27 = (f32[3,8,2048]{2,1,0:T(8,128)S(1)}, f32[3,8,2048]{2,1,0:T(8,128)}, u32[]{:S(2)}) copy-start(f32[3,8,2048]{2,1,0:T(8,128)} %get-tuple-element.62) | copy-start | bytes 589828
  389.7 12.6 %copy-start.23 = (f32[48,2048]{1,0:T(8,128)S(1)}, f32[48,2048]{1,0:T(8,128)}, u32[]{:S(2)}) copy-start(f32[48,2048]{1,0:T(8,128)} %get-tuple-element.34) | copy-start | bytes 1179652
  389.7 12.6 %copy-start.32 = (f32[1,2048]{1,0:T(1,128)S(1)}, f32[1,2048]{1,0:T(1,128)}, u32[]{:S(2)}) copy-start(f32[1,2048]{1,0:T(1,128)} %copy-done.31) | copy-start | bytes 24580
  403.1 10.8 %copy-start.3 = (f32[8,128,1024]{2,1,0:T(8,128)S(1)}, f32[8,128,1024]{2,1,0:T(8,128)}, u32[]{:S(2)}) copy-start(f32[8,128,1024]{2,1,0:T(8,128)} %convert.34) | copy-start | bytes 12582916
  403.1 10.8 %copy-start.37 = (f32[1024]{0:T(1024)S(1)}, f32[1024]{0:T(1024)}, u32[]{:S(2)}) copy-start(f32[1024]{0:T(1024)} %param.16) | copy-start | bytes 12292
  413.9 18.1 %copy-start.40 = (f32[2048]{0:T(1024)S(1)}, f32[2048]{0:T(1024)}, u32[]{:S(2)}) copy-start(f32[2048]{0:T(1024)} %fusion.59) | copy-start | bytes 24580
  413.9 22.2 %copy-start.39 = (f32[2048]{0:T(1024)S(1)}, f32[2048]{0:T(1024)}, u32[]{:S(2)}) copy-start(f32[2048]{0:T(1024)} %reduce_sum.101) | copy-start | bytes 24580
  485.3 170.1 %copy-start.14 = (bf16[1,1024,1024]{2,1,0:T(8,128)(2,1)S(1)}, bf16[1,1024,1024]{2,1,0:T(8,128)(2,1)}, u32[]{:S(2)}) copy-start(bf16[1,1024,1024]{2,1,0:T(8,128)(2,1)} %param.15) | copy-start | bytes 6291460
  485.3 170.1 %copy-start.41 = (f32[1024]{0:T(1024)S(1)}, f32[1024]{0:T(1024)}, u32[]{:S(2)}) copy-start(f32[1024]{0:T(1024)} %multiply_multiply_fusion.2) | copy-start | bytes 12292
  (24 other events, 110.8 us)

commit v3 on v2

v3 whole, which is shorter than its diff:
```python
import functools
import math

import jax
import jax.numpy as jnp
from jax import lax
from jax.experimental import pallas as pl
from jax.experimental.pallas import tpu as pltpu
from jax.sharding import PartitionSpec as P

ADAM_STEP = 100
EPS = 1e-05
RATE = 0.002
BETA_ONE = 0.9
BETA_TWO = 0.95
ADAM_EPS = 1e-08
DECAY = 0.1
CLIP = 1.0

LOG2E = 1.0 / math.log(2.0)
LN2 = math.log(2.0)
SUB = 8
LANE = 128
ROW = 1024
VMEM_BYTES = 56 * 2**20

MESH = pl.DeviceIdType.MESH

f32 = jnp.float32
bf16 = jnp.bfloat16


def shifted(x, axis, by):
    count = lax.axis_size(axis)
    pairs = [(i, i + by) for i in range(count) if 0 <= i + by < count]
    return lax.ppermute(x, axis, pairs)


def silu_slope(value):
    sig = jax.nn.sigmoid(value)
    return sig * (1.0 + value * (1.0 - sig))


def interleave(x):
    rows, width = x.shape
    return x.reshape(SUB, rows // SUB, width).transpose(1, 0, 2).reshape(rows, width)


def restore(x):
    rows, width = x.shape
    return x.reshape(rows // SUB, SUB, width).transpose(1, 0, 2).reshape(rows, width)


def at(start, size):
    return pl.ds(pl.multiple_of(start, size), size)


def spread(sel_ref, spots_ref, out_ref):
    out_ref[...] = jnp.dot(sel_ref[...], spots_ref[...], preferred_element_type=f32)


def gather_lanes(src_ref, spots_ref, out_ref):
    value = src_ref[...]
    high = value.astype(bf16)
    low = (value - high.astype(f32)).astype(bf16)
    spots = spots_ref[0:LANE, 0 : value.shape[1]]
    back = (((1,), (1,)), ((), ()))
    out_ref[...] = lax.dot_general(high, spots, back, preferred_element_type=f32) + lax.dot_general(
        low, spots, back, preferred_element_type=f32
    )


def spread_table(count):
    row = lax.broadcasted_iota(jnp.int32, (LANE, count * LANE), 0)
    col = lax.broadcasted_iota(jnp.int32, (LANE, count * LANE), 1) // LANE
    return ((row % count == col) & (row < 3 * count)).astype(bf16)


def summary_kernel(
    shape,
    stream_ref,
    gating_ref,
    grad_gated_ref,
    head_ref,
    taps_ref,
    bias_ref,
    select_in_ref,
    step_in_ref,
    step_bias_ref,
    spots_ref,
    rates_ref,
    conv_sum_ref,
    conv_ref,
    step_ref,
    drive_ref,
    grad_ref,
    low_ref,
    sel_ref,
    pre_decay_ref,
    pre_state_ref,
    post_decay_ref,
    post_state_ref,
    totals_ref,
    end_ref,
    exit_ref,
    prod_ref,
    select_ref,
    longer_ref,
):
    tiles, state, inner, cols, group = shape
    turn = pl.program_id(0)
    block = tiles * SUB
    width = taps_ref.shape[0]
    halo = (width - 1) * SUB

    @pl.when(turn == 0)
    def _():
        end_ref[...] = jnp.zeros_like(end_ref)
        exit_ref[...] = jnp.zeros_like(exit_ref)
        prod_ref[...] = jnp.ones_like(prod_ref)
        longer_ref[:halo, :] = head_ref[...]

    @pl.when(turn > 0)
    def _():
        longer_ref[:halo, :] = longer_ref[block:, :]

    longer_ref[halo:, :] = stream_ref[...]

    def convs(c, carry):
        lanes = at(c * 2 * LANE, 2 * LANE)
        taps = [jnp.broadcast_to(taps_ref[k : k + 1, lanes], (2 * SUB, 2 * LANE)) for k in range(width)]
        bias = bias_ref[:, lanes]

        def pair(i, carry):
            here = at(i * 2 * SUB, 2 * SUB)
            total = bias + taps[width - 1] * stream_ref[here, lanes]
            for k in range(width - 1):
                total = total + taps[k] * longer_ref[pl.ds(pl.multiple_of((2 * i + k) * SUB, SUB), 2 * SUB), lanes]
            conv_sum_ref[here, lanes] = total
            conv_ref[here, lanes] = (total * jax.nn.sigmoid(total)).astype(bf16)
            gating = gating_ref[here, lanes]
            grad_ref[here, lanes] = grad_gated_ref[here, lanes] * (gating * jax.nn.sigmoid(gating))
            return carry

        lax.fori_loop(0, tiles // 2, pair, 0, unroll=4)
        return carry

    lax.fori_loop(0, inner // (2 * LANE), convs, 0)
    lane = lax.broadcasted_iota(jnp.int32, (block, LANE), 1)
    selectors = jnp.dot(conv_ref[...], select_in_ref[...], preferred_element_type=f32)
    low = selectors.astype(bf16)
    low_ref[...] = low
    value = jnp.where(lane < 2 * state, selectors, 0.0)
    high = value.astype(bf16).astype(f32)
    middle = (value - high).astype(bf16).astype(f32)
    rest = value - high - middle
    sel_ref[...] = (high + pltpu.roll(middle, 2 * state, 1) + pltpu.roll(rest, 4 * state, 1)).astype(bf16)

    def steps(c, carry):
        lanes = at(c * 2 * LANE, 2 * LANE)
        bias = step_bias_ref[:, lanes]
        step_ref[:, lanes] = jnp.dot(low, step_in_ref[:, lanes], preferred_element_type=f32)

        def pair(i, carry):
            here = at(i * 2 * SUB, 2 * SUB)
            pre = step_ref[here, lanes] + bias
            step = jnp.maximum(pre, 0.0) + jnp.log1p(jnp.exp(-jnp.abs(pre)))
            step_ref[here, lanes] = step
            drive_ref[here, lanes] = step * conv_ref[here, lanes].astype(f32)
            return carry

        lax.fori_loop(0, tiles // 2, pair, 0, unroll=4)
        return carry

    lax.fori_loop(0, inner // (2 * LANE), steps, 0)
    spread(sel_ref, spots_ref, select_ref)

    def columns(c, carry):
        lanes = [at((c * cols + k) * LANE, LANE) for k in range(cols)]
        for first in range(0, state, group):
            spots = [(n, k) for n in range(group) for k in range(cols)]
            where = [(slice((first + n) * SUB, (first + n + 1) * SUB), lanes[k]) for n, k in spots]
            rates = [rates_ref[w] for w in where]

            def advance(i, carry):
                ends, exits, prods = carry
                here = at(i * SUB, SUB)
                step = [step_ref[here, l] for l in lanes]
                drive = [drive_ref[here, l] for l in lanes]
                grad = [grad_ref[here, l] for l in lanes]
                inject = [select_ref[here, (first + n) * LANE : (first + n + 1) * LANE] for n in range(group)]
                readout = [
                    select_ref[here, (state + first + n) * LANE : (state + first + n + 1) * LANE] for n in range(group)
                ]
                new = ([], [], [])
                for s, (n, k) in enumerate(spots):
                    decay = jnp.exp2(step[k] * rates[s])
                    prod = prods[s] * decay
                    new[0].append(ends[s] * decay + drive[k] * inject[n])
                    new[1].append(exits[s] + prod * (grad[k] * readout[n]))
                    new[2].append(prod)
                return tuple(tuple(x) for x in new)

            start = tuple(tuple(ref[w] for w in where) for ref in (end_ref, exit_ref, prod_ref))
            ends, exits, prods = lax.fori_loop(0, tiles, advance, start, unroll=16)
            for s, w in enumerate(where):
                end_ref[w] = ends[s]
                exit_ref[w] = exits[s]
                prod_ref[w] = prods[s]
        return carry

    lax.fori_loop(0, inner // (LANE * cols), columns, 0)

    @pl.when(turn == pl.num_programs(0) - 1)
    def _():
        row = lax.broadcasted_iota(jnp.int32, (SUB, LANE), 0)

        def columns(c, carry):
            lanes = at(c * LANE, LANE)
            for n in range(state):
                here = (slice(n * SUB, (n + 1) * SUB), lanes)
                for way, src, decay_out, state_out, total_row in (
                    (1, end_ref, pre_decay_ref, pre_state_ref, 1),
                    (-1, exit_ref, post_decay_ref, post_state_ref, 2),
                ):
                    decay, value = prod_ref[here], src[here]

                    def seen(by):
                        return row >= by if way > 0 else row < SUB - by

                    for by in (1, 2, 4):
                        far_decay = pltpu.roll(decay, by if way > 0 else SUB - by, 0)
                        far_value = pltpu.roll(value, by if way > 0 else SUB - by, 0)
                        value = jnp.where(seen(by), value + decay * far_value, value)
                        decay = jnp.where(seen(by), decay * far_decay, decay)
                    last = SUB - 1 if way > 0 else 0
                    totals_ref[pl.ds(n, 1), lanes] = decay[last : last + 1]
                    totals_ref[pl.ds(total_row * state + n, 1), lanes] = value[last : last + 1]
                    turn_by = 1 if way > 0 else SUB - 1
                    decay_out[here] = jnp.where(seen(1), pltpu.roll(decay, turn_by, 0), 1.0)
                    state_out[here] = jnp.where(seen(1), pltpu.roll(value, turn_by, 0), 0.0)
            return carry

        lax.fori_loop(0, inner // LANE, columns, 0)


def forward_kernel(
    shape,
    step_ref,
    drive_ref,
    grad_ref,
    sel_ref,
    spots_ref,
    rates_ref,
    pre_decay_ref,
    pre_state_ref,
    entry_ref,
    conv_ref,
    gating_ref,
    grad_gated_ref,
    skip_ref,
    prior_ref,
    readout_grad_ref,
    gated_ref,
    grad_gating_ref,
    skip_grad_ref,
    state_ref,
    select_ref,
    sums_ref,
    scanned_ref,
):
    tiles, state, inner, cols, group = shape

    @pl.when(pl.program_id(0) == 0)
    def _():
        skip_grad_ref[...] = jnp.zeros_like(skip_grad_ref)
        for n in range(state):
            here = slice(n * SUB, (n + 1) * SUB)
            state_ref[here, :] = pre_state_ref[here, :] + pre_decay_ref[here, :] * entry_ref[n : n + 1, :]

    spread(sel_ref, spots_ref, select_ref)
    sums_ref[...] = jnp.zeros_like(sums_ref)

    def columns(c, carry):
        lanes = [at((c * cols + k) * LANE, LANE) for k in range(cols)]
        for first in range(0, state, group):
            spots = [(n, k) for n in range(group) for k in range(cols)]
            where = [(slice((first + n) * SUB, (first + n + 1) * SUB), lanes[k]) for n, k in spots]
            rates = [rates_ref[w] for w in where]

            def advance(i, states):
                here = at(i * SUB, SUB)
                step = [step_ref[here, l] for l in lanes]
                drive = [drive_ref[here, l] for l in lanes]
                grad = [grad_ref[here, l] for l in lanes]
                outs = [None] * cols
                new = []
                for n in range(group):
                    spot = slice((first + n) * LANE, (first + n + 1) * LANE)
                    inject = select_ref[here, spot]
                    readout = select_ref[here, (state + first + n) * LANE : (state + first + n + 1) * LANE]
                    total = None
                    for k in range(cols):
                        s = n * cols + k
                        decay = jnp.exp2(step[k] * rates[s])
                        fresh = decay * states[s] + drive[k] * inject
                        new.append(fresh)
                        part = readout * fresh
                        outs[k] = part if outs[k] is None else outs[k] + part
                        part = grad[k] * fresh
                        total = part if total is None else total + part
                    sums_ref[here, spot] += total
                    if n % 2 == 1:
                        pair = pl.ds(pl.multiple_of((i * state + first + n - 1) * SUB, 2 * SUB), 2 * SUB)
                        for k in range(cols):
                            prior_ref[pair, lanes[k]] = jnp.concatenate(
                                [states[(n - 1) * cols + k], states[n * cols + k]], 0
                            ).astype(bf16)
                for k in range(cols):
                    if first == 0:
                        scanned_ref[here, lanes[k]] = outs[k]
                    else:
                        scanned_ref[here, lanes[k]] += outs[k]
                return tuple(new)

            states = lax.fori_loop(0, tiles, advance, tuple(state_ref[w] for w in where), unroll=16)
            for s, w in enumerate(where):
                state_ref[w] = states[s]
        return carry

    lax.fori_loop(0, inner // (LANE * cols), columns, 0)
    gather_lanes(sums_ref, spots_ref, readout_grad_ref)

    def finish(c, carry):
        lanes = at(c * 2 * LANE, 2 * LANE)
        skip = skip_ref[:, lanes]

        def pair(i, total):
            here = at(i * 2 * SUB, 2 * SUB)
            conv = conv_ref[here, lanes].astype(f32)
            gating = gating_ref[here, lanes]
            sig = jax.nn.sigmoid(gating)
            gate = gating * sig
            scanned = scanned_ref[here, lanes] + skip * conv
            gated_ref[here, lanes] = (scanned * gate).astype(bf16)
            slope = sig + gate * (1.0 - sig)
            grad_gating_ref[here, lanes] = (grad_gated_ref[here, lanes] * scanned * slope).astype(bf16)
            product = grad_ref[here, lanes] * conv
            return total + product[:SUB] + product[SUB:]

        zero = jnp.zeros((SUB, 2 * LANE), f32)
        skip_grad_ref[:, lanes] += lax.fori_loop(0, tiles // 2, pair, zero, unroll=4)
        return carry

    lax.fori_loop(0, inner // (2 * LANE), finish, 0)


def backward_kernel(
    shape,
    scan_turns,
    regions,
    bits,
    phases,
    stride,
    step_ref,
    drive_ref,
    grad_ref,
    sel_ref,
    spots_ref,
    rates_ref,
    begin_ref,
    prior_ref,
    conv_sum_ref,
    stream_ref,
    readout_grad_ref,
    step_back_ref,
    select_back_ref,
    taps_ref,
    skip_ref,
    flat_ref,
    grad_stream_ref,
    grad_pre_ref,
    grad_select_ref,
    rate_grad_ref,
    taps_grad_ref,
    edge_ref,
    early_ref,
    carry_ref,
    select_ref,
    sums_ref,
    through_ref,
    feed_ref,
    grad_conv_ref,
    inject_grad_ref,
    *refs,
):
    tiles, state, inner, cols, group = shape
    block = tiles * SUB
    width = taps_ref.shape[0]
    halo = (width - 1) * SUB
    turn = pl.program_id(0)
    work = Reducer(regions.depth, bits, phases, stride, regions.early_start, flat_ref, refs)
    turns = scan_turns
    early = max(work.slots - turns, 0)
    for g in range(turns):

        @pl.when(turn == g)
        def _():
            if g == 0:
                work.greet()
            for t in range(0 if g == 0 else g + early, min(g + early + 1, work.slots)):
                work.run(t)

    @pl.when(pl.program_id(0) == 0)
    def _():
        rate_grad_ref[...] = jnp.zeros_like(rate_grad_ref)
        taps_grad_ref[...] = jnp.zeros_like(taps_grad_ref)
        grad_conv_ref[tiles * SUB :, :] = jnp.zeros((grad_conv_ref.shape[0] - tiles * SUB, inner), f32)
        carry_ref[...] = begin_ref[...]

    spread(sel_ref, spots_ref, select_ref)
    sums_ref[...] = jnp.zeros_like(sums_ref)

    def columns(c, carry):
        lanes = [at((c * cols + k) * LANE, LANE) for k in range(cols)]
        for first in range(0, state, group):
            spots = [(n, k) for n in range(group) for k in range(cols)]
            where = [(slice((first + n) * SUB, (first + n + 1) * SUB), lanes[k]) for n, k in spots]
            rates = [rates_ref[w] for w in where]

            def retreat(turn, carry):
                carries, rate_grads = carry
                i = tiles - 1 - turn
                here = at(i * SUB, SUB)
                step = [step_ref[here, l] for l in lanes]
                drive = [drive_ref[here, l] for l in lanes]
                grad = [grad_ref[here, l] for l in lanes]
                throughs = [None] * cols
                feeds = [None] * cols
                new = ([], [])
                for n in range(group):
                    spot = slice((first + n) * LANE, (first + n + 1) * LANE)
                    inject = select_ref[here, spot]
                    readout = select_ref[here, (state + first + n) * LANE : (state + first + n + 1) * LANE]
                    if n % 2 == 0:
                        pair = pl.ds(pl.multiple_of((i * state + first + n) * SUB, 2 * SUB), 2 * SUB)
                        pairs = [prior_ref[pair, lanes[k]].astype(f32) for k in range(cols)]
                    total = None
                    for k in range(cols):
                        s = n * cols + k
                        prior = pairs[k][(n % 2) * SUB : (n % 2 + 1) * SUB]
                        power = step[k] * rates[s]
                        adjoint = grad[k] * readout + carries[s]
                        back = jnp.exp2(power) * adjoint
                        through = back * prior * power
                        new[0].append(back)
                        new[1].append(rate_grads[s] + through)
                        throughs[k] = through if throughs[k] is None else throughs[k] + through
                        part = adjoint * inject
                        feeds[k] = part if feeds[k] is None else feeds[k] + part
                        part = adjoint * drive[k]
                        total = part if total is None else total + part
                    sums_ref[here, spot] += total
                for k in range(cols):
                    if first == 0:
                        through_ref[here, lanes[k]] = throughs[k]
                        feed_ref[here, lanes[k]] = feeds[k]
                    else:
                        through_ref[here, lanes[k]] += throughs[k]
                        feed_ref[here, lanes[k]] += feeds[k]
                return tuple(tuple(x) for x in new)

            start = tuple(tuple(ref[w] for w in where) for ref in (carry_ref, rate_grad_ref))
            carries, rate_grads = lax.fori_loop(0, tiles, retreat, start, unroll=8)
            for s, w in enumerate(where):
                carry_ref[w] = carries[s]
                rate_grad_ref[w] = rate_grads[s]
        return carry

    lax.fori_loop(0, inner // (LANE * cols), columns, 0)
    gather_lanes(sums_ref, spots_ref, inject_grad_ref)

    def steps(c, carry):
        lanes = at(c * 2 * LANE, 2 * LANE)

        def pair(i, total):
            here = at(i * 2 * SUB, 2 * SUB)
            step = step_ref[here, lanes]
            series = 1.0 + step * (-1.0 / 2 + step * (1.0 / 6 + step * (-1.0 / 24 + step * (1.0 / 120))))
            near = step < 0.06
            exact = (1.0 - jnp.exp2(step * -LOG2E)) / jnp.where(near, 1.0, step)
            ratio = jnp.where(near, series, exact)
            pre = ratio * (LN2 * through_ref[here, lanes] + drive_ref[here, lanes] * feed_ref[here, lanes])
            grad_pre_ref[here, lanes] = pre.astype(bf16)
            return total + pre[:SUB] + pre[SUB:]

        zero = jnp.zeros((SUB, 2 * LANE), f32)
        taps_grad_ref[(width + 1) * SUB :, lanes] += lax.fori_loop(0, tiles // 2, pair, zero, unroll=4)
        return carry

    lax.fori_loop(0, inner // (2 * LANE), steps, 0)
    lane = lax.broadcasted_iota(jnp.int32, (block, LANE), 1)
    rank = LANE - 2 * state
    grads = jnp.dot(grad_pre_ref[...], step_back_ref[...], preferred_element_type=f32)
    grads = jnp.where(
        lane < state,
        inject_grad_ref[...],
        jnp.where(lane < 2 * state, pltpu.roll(readout_grad_ref[...], state, 1), grads),
    )
    grads = grads.astype(bf16)
    grad_select_ref[...] = grads

    def convs(c, carry):
        lanes = at(c * 2 * LANE, 2 * LANE)
        skip = skip_ref[:, lanes]
        feeds = jnp.dot(grads, select_back_ref[:, lanes], preferred_element_type=f32)
        through_ref[:, lanes] = feeds

        def conv(i, carry):
            here = at(i * SUB, SUB)
            value = conv_sum_ref[here, lanes]
            sig = jax.nn.sigmoid(value)
            slope = sig * (1.0 + value * (1.0 - sig))
            out = grad_ref[here, lanes] * skip + step_ref[here, lanes] * feed_ref[here, lanes] + through_ref[here, lanes]
            grad_conv_ref[here, lanes] = out * slope
            return carry

        lax.fori_loop(0, tiles, conv, 0, unroll=8)
        taps = [jnp.broadcast_to(taps_ref[k : k + 1, lanes], (SUB, 2 * LANE)) for k in range(width)]

        def tap(i, totals):
            totals = list(totals)
            done = []
            for q in range(2):
                parts = [
                    grad_conv_ref[pl.ds(pl.multiple_of((2 * i + q + m) * SUB, SUB), SUB), lanes] for m in range(width)
                ]
                stream = stream_ref[pl.ds(pl.multiple_of((2 * i + q) * SUB, SUB), SUB), lanes]
                grad = taps[width - 1] * parts[0]
                totals[width - 1] = totals[width - 1] + parts[0] * stream
                totals[width] = totals[width] + parts[0]
                for m in range(1, width):
                    grad = grad + taps[width - 1 - m] * parts[m]
                    totals[width - 1 - m] = totals[width - 1 - m] + parts[m] * stream
                done.append(grad)
            grad_stream_ref[at(i * 2 * SUB, 2 * SUB), lanes] = jnp.concatenate(done, 0).astype(bf16)
            return tuple(totals)

        zero = jnp.zeros((SUB, 2 * LANE), f32)
        totals = lax.fori_loop(0, tiles // 2, tap, (zero,) * (width + 1), unroll=4)
        for k in range(width + 1):
            taps_grad_ref[k * SUB : (k + 1) * SUB, lanes] += totals[k]
        return carry

    lax.fori_loop(0, inner // (2 * LANE), convs, 0)

    @pl.when(pl.program_id(0) == 0)
    def _():
        edge_ref[halo:, :] = grad_conv_ref[block - halo : block, :]

    edge_ref[:halo, :] = grad_conv_ref[:halo, :]
    grad_conv_ref[block:, :] = grad_conv_ref[:halo, :]

    @pl.when(turn == turns - 1)
    def _():
        work.collect(early_ref)


def scan_shapes(rows, state, inner, tiles=16):
    tiles = min(tiles, rows // SUB)
    count = rows // (SUB * tiles)
    return tiles, count


def summary_call(stream, gating, grad_gated, head, taps, bias, select_in, step_in, step_bias, spots, rates):
    rows, inner = stream.shape
    state = rates.shape[0] // SUB
    tiles, count = scan_shapes(rows, state, inner)
    halo = head.shape[0]
    wide = pl.BlockSpec((tiles * SUB, inner), lambda t: (t, 0))
    thin = pl.BlockSpec((tiles * SUB, LANE), lambda t: (t, 0))
    whole = pl.BlockSpec((state * SUB, inner), lambda t: (0, 0))
    total = pl.BlockSpec((3 * state, inner), lambda t: (0, 0))
    shape = (tiles, state, inner, 2, 4)
    big = jax.ShapeDtypeStruct((state * SUB, inner), f32)
    full = jax.ShapeDtypeStruct((rows, inner), f32)
    slim = jax.ShapeDtypeStruct((rows, LANE), bf16)

    def fixed(x):
        return pl.BlockSpec(x.shape, lambda t: (0, 0), pipeline_mode=pl.Buffered(1))

    constants = (head, taps, bias, select_in, step_in, step_bias, spots, rates)
    return pl.pallas_call(
        functools.partial(summary_kernel, shape),
        name="scan_summary",
        grid=(count,),
        in_specs=[wide, wide, wide] + [fixed(x) for x in constants],
        out_specs=[wide] * 5 + [thin] * 2 + [whole] * 4 + [total],
        out_shape=[full, jax.ShapeDtypeStruct((rows, inner), bf16), full, full, full, slim, slim]
        + [big] * 4
        + [jax.ShapeDtypeStruct((3 * state, inner), f32)],
        scratch_shapes=[pltpu.VMEM((state * SUB, inner), f32)] * 3
        + [
            pltpu.VMEM((tiles * SUB, 2 * state * LANE), f32),
            pltpu.VMEM((halo + tiles * SUB, inner), f32),
        ],
        compiler_params=pltpu.CompilerParams(vmem_limit_bytes=VMEM_BYTES),
    )(stream, gating, grad_gated, *constants)


def forward_call(step, drive, grad, sel, spots, rates, pre_decay, pre_state, entry, conv, gating, grad_gated, skip):
    rows, inner = step.shape
    state = rates.shape[0] // SUB
    tiles, count = scan_shapes(rows, state, inner)
    wide = pl.BlockSpec((tiles * SUB, inner), lambda t: (t, 0))
    table = pl.BlockSpec(spots.shape, lambda t: (0, 0))
    thin = pl.BlockSpec((tiles * SUB, sel.shape[1]), lambda t: (t, 0))
    whole = pl.BlockSpec((state * SUB, inner), lambda t: (0, 0), pipeline_mode=pl.Buffered(1))
    line = pl.BlockSpec((1, inner), lambda t: (0, 0))
    short = pl.BlockSpec((state, inner), lambda t: (0, 0))
    shape = (tiles, state, inner, 2, 8)
    return pl.pallas_call(
        functools.partial(forward_kernel, shape),
        name="scan_forward",
        grid=(count,),
        in_specs=[wide, wide, wide, thin, table, whole, whole, whole, short, wide, wide, wide, line],
        out_specs=[
            pl.BlockSpec((tiles * state * SUB, inner), lambda t: (t, 0)),
            pl.BlockSpec((tiles * SUB, LANE), lambda t: (t, 0)),
            wide,
            wide,
            pl.BlockSpec((SUB, inner), lambda t: (0, 0)),
        ],
        out_shape=[
            jax.ShapeDtypeStruct((rows * state, inner), bf16),
            jax.ShapeDtypeStruct((rows, LANE), f32),
            jax.ShapeDtypeStruct((rows, inner), bf16),
            jax.ShapeDtypeStruct((rows, inner), bf16),
            jax.ShapeDtypeStruct((SUB, inner), f32),
        ],
        scratch_shapes=[pltpu.VMEM((state * SUB, inner), f32)]
        + [
            pltpu.VMEM((tiles * SUB, 2 * state * LANE), f32),
            pltpu.VMEM((tiles * SUB, state * LANE), f32),
            pltpu.VMEM((tiles * SUB, inner), f32),
        ],
        compiler_params=pltpu.CompilerParams(vmem_limit_bytes=VMEM_BYTES),
    )(step, drive, grad, sel, spots, rates, pre_decay, pre_state, entry, conv, gating, grad_gated, skip)


def backward_call(step, drive, grad, sel, spots, rates, begin, prior, conv_sum, stream, readout_grad, step_back, select_back, taps, skip, flat, regions):
    rows, inner = step.shape
    state = rates.shape[0] // SUB
    tiles, count = scan_shapes(rows, state, inner, 8)
    bits = regions.count.bit_length() - 1
    phases = regions.early_phases()
    stride = 1

    def back(t):
        return (count - 1 - t, 0)

    wide = pl.BlockSpec((tiles * SUB, inner), back)
    table = pl.BlockSpec(spots.shape, lambda t: (0, 0), pipeline_mode=pl.Buffered(1))
    thin = pl.BlockSpec((tiles * SUB, sel.shape[1]), back)
    whole = pl.BlockSpec((state * SUB, inner), lambda t: (0, 0), pipeline_mode=pl.Buffered(1))
    narrow = pl.BlockSpec((tiles * SUB, LANE), back)
    width = taps.shape[0]
    halo = (width - 1) * SUB

    def fixed(x):
        return pl.BlockSpec(x.shape, lambda t: (0, 0), pipeline_mode=pl.Buffered(1))

    shape = (tiles, state, inner, 2, 4)
    return pl.pallas_call(
        functools.partial(backward_kernel, shape, count, regions, bits, phases, stride),
        name="scan_backward",
        grid=(count,),
        in_specs=[wide, wide, wide, thin, table, whole, whole]
        + [pl.BlockSpec((tiles * state * SUB, inner), back), wide, wide, narrow]
        + [fixed(step_back), fixed(select_back), fixed(taps), fixed(skip)]
        + [pl.BlockSpec(memory_space=pl.ANY)],
        out_specs=[
            wide,
            wide,
            narrow,
            pl.BlockSpec((state * SUB, inner), lambda t: (0, 0)),
            pl.BlockSpec(((width + 2) * SUB, inner), lambda t: (0, 0)),
            pl.BlockSpec((2 * halo, inner), lambda t: (0, 0)),
            pl.BlockSpec((regions.slot, SUB, LANE), lambda t: (0, 0, 0)),
        ],
        out_shape=[
            jax.ShapeDtypeStruct((rows, inner), bf16),
            jax.ShapeDtypeStruct((rows, inner), bf16),
            jax.ShapeDtypeStruct((rows, LANE), bf16),
            jax.ShapeDtypeStruct((state * SUB, inner), f32),
            jax.ShapeDtypeStruct(((width + 2) * SUB, inner), f32),
            jax.ShapeDtypeStruct((2 * halo, inner), f32),
            jax.ShapeDtypeStruct((regions.slot, SUB, LANE), f32),
        ],
        scratch_shapes=[pltpu.VMEM((state * SUB, inner), f32)]
        + [
            pltpu.VMEM((tiles * SUB, 2 * state * LANE), f32),
            pltpu.VMEM((tiles * SUB, state * LANE), f32),
            pltpu.VMEM((tiles * SUB, inner), f32),
            pltpu.VMEM((tiles * SUB, inner), f32),
            pltpu.VMEM((tiles * SUB + halo, inner), f32),
            pltpu.VMEM((tiles * SUB, LANE), f32),
        ]
        + Reducer.scratch(regions.depth, bits, phases),
        compiler_params=pltpu.CompilerParams(
            vmem_limit_bytes=62 * 2**20, collective_id=2, has_side_effects=True
        ),
    )(step, drive, grad, sel, spots, rates, begin, prior, conv_sum, stream, readout_grad, step_back, select_back, taps, skip, flat)


def turn_tiles(tiles):
    row = lax.broadcasted_iota(jnp.int32, (SUB, LANE), 0)
    for bit in (1, 2, 4):
        upper = (row // bit) % 2 == 1
        new = list(tiles)
        for a in range(SUB):
            if a & bit == 0:
                b = a + bit
                new[a] = jnp.where(upper, pltpu.roll(tiles[b], bit, 0), tiles[a])
                new[b] = jnp.where(upper, tiles[b], pltpu.roll(tiles[a], SUB - bit, 0))
        tiles = new
    return tiles


def product_kernel(steps, shapes, *refs):
    out_ref, held_ref = refs[-2:]
    contract = (((0,), (0,)), ((), ()))
    for turn, (rows, width) in enumerate(shapes):
        left_ref, right_ref = refs[2 * turn : 2 * turn + 2]
        per = width // ROW

        @pl.when(pl.program_id(0) // steps == turn)
        def _():
            for q in range(per):
                held_ref[:rows] = lax.dot_general(
                    left_ref[...], right_ref[:, q * ROW : (q + 1) * ROW], contract, preferred_element_type=f32
                )

                def one(r, carry):
                    tiles = [held_ref[at(r * SUB, SUB), a * LANE : (a + 1) * LANE] for a in range(SUB)]
                    for b, tile in enumerate(turn_tiles(tiles)):
                        out_ref[(r * SUB + b) * per + q] = tile
                    return carry

                lax.fori_loop(0, rows // SUB, one, 0, unroll=4)


def product_call(*pairs):
    steps = 8
    shapes = [(left.shape[1] // steps, right.shape[1]) for left, right in pairs]
    size = shapes[0][0] * shapes[0][1] // ROW

    def block(k):
        return lambda t: (0, jnp.clip(t - k * steps, 0, steps - 1))

    specs = []
    for k, (left, right) in enumerate(pairs):
        specs.append(pl.BlockSpec((left.shape[0], left.shape[1] // steps), block(k)))
        specs.append(pl.BlockSpec(right.shape, lambda t: (0, 0), pipeline_mode=pl.Buffered(1)))
    return pl.pallas_call(
        functools.partial(product_kernel, steps, shapes),
        name="flat_product",
        grid=(steps * len(pairs),),
        in_specs=specs,
        out_specs=pl.BlockSpec((size, SUB, LANE), lambda t: (t, 0, 0)),
        out_shape=jax.ShapeDtypeStruct((size * steps * len(pairs), SUB, LANE), f32),
        scratch_shapes=[pltpu.VMEM((max(rows for rows, _ in shapes), ROW), f32)],
        compiler_params=pltpu.CompilerParams(vmem_limit_bytes=VMEM_BYTES),
    )(*[x for pair in pairs for x in pair])


class Regions:
    def __init__(self, depth, count, span, gain, in_shape, small, out_shape):
        self.depth, self.count, self.span = depth, count, span
        self.per = in_shape[1] // ROW
        self.in_rows = in_shape[0]
        self.in_base = gain
        self.small_base = gain + in_shape[0] * self.per
        self.out_base = self.small_base + small
        self.out_rows = out_shape[0] * out_shape[1] // ROW
        self.need = (span - 1) // ROW + 2
        self.lines = min((self.need + self.per - 2) // self.per + 1, self.in_rows)
        self.half = self.lines * self.per // 2
        self.pieces = -(-self.need // self.half)
        self.slot = self.pieces * self.half

    def base(self, owner):
        return owner * self.span // ROW

    def in_first(self, owner):
        line = lax.max(self.base(owner) - self.in_base, 0) // self.per
        return lax.min(line, self.in_rows - self.lines)

    def out_first(self, owner):
        return lax.max(lax.min(self.base(owner) - self.out_base, self.out_rows - self.slot), 0)

    def meets_in(self, z):
        return z * self.count * self.span // ROW < self.small_base

    def meets_out(self, z):
        return ((z + 1) * self.count * self.span - 1) // ROW >= self.out_base

    def early_start(self, z, owner):
        if not self.meets_out(z):
            return self.in_first(owner) * (self.per // 2)
        out = self.in_rows * self.per // 2 + self.out_first(owner)
        if not self.meets_in(z):
            return out
        inside = self.base(owner) < self.small_base
        return jnp.where(inside, self.in_first(owner) * (self.per // 2), out)

    def early_phases(self):
        phases = []
        cut = 2 if self.half % 4 == 0 else 1
        size = self.half // cut
        for z in range(self.depth):
            for piece in range((self.pieces if self.meets_out(z) else 1) * cut):
                phases.append((z, piece * size, size))
        return phases

    def late_phases(self):
        cut = 2 if self.half % 4 == 0 else 1
        size = self.half // cut
        return [(z, piece * size, size) for z in range(self.depth) if self.meets_in(z) for piece in range(cut)]


class Reducer:
    def __init__(self, depth, bits, phases, stride, start, src_ref, refs):
        self.depth, self.bits, self.phases, self.stride = depth, bits, phases, stride
        self.start, self.src = start, src_ref
        self.n = bits - 1
        self.half = phases[0][2] // 2
        self.acc, self.first = refs[:2]
        self.bit_recvs = refs[2 : 2 + self.n]
        self.down, self.up = refs[2 + self.n : 4 + self.n]
        (
            self.local_sem,
            self.core_send,
            self.core_recv,
            self.bit_send,
            self.bit_recv,
            self.z_send,
            self.z_recv,
        ) = refs[4 + self.n : 11 + self.n]
        self.blk, self.z = lax.axis_index("blk"), lax.axis_index("batch")
        self.mine = [(self.blk // 2**b) % 2 for b in range(bits)]
        self.partner = [self.blk + (1 - 2 * self.mine[b]) * 2**b for b in range(bits)]
        self.last = self.n + depth - 1
        self.slots = stride * (len(phases) - 1) + self.last + 1

    @staticmethod
    def scratch(depth, bits, phases):
        n, count, size = bits - 1, len(phases), phases[0][2]
        tile = (SUB, LANE)
        dma = pltpu.SemaphoreType.DMA
        return (
            [pltpu.VMEM((count,) + (2,) * n + (size,) + tile, f32)] * 2
            + [pltpu.VMEM((count, 2) + (2,) * (n - 1 - s) + (size // 2,) + tile, f32) for s in range(n)]
            + [pltpu.VMEM((count, size) + tile, f32)] * 2
            + [dma((count * 2**n,))] * 3
            + [dma((max(count * n * 2, 1),))] * 2
            + [dma((count,)), dma((2 * count,))]
        )

    def greet(self):
        barrier = pltpu.get_barrier_semaphore()
        for other in self.partner:
            pl.semaphore_signal(barrier, inc=1, device_id={"blk": other}, device_id_type=MESH)
        for by in (1, self.depth - 1):
            other = lax.rem(self.z + by, self.depth)
            pl.semaphore_signal(barrier, inc=1, device_id={"batch": other}, device_id_type=MESH)
        pl.semaphore_wait(barrier, self.bits + 2)

    def digits(self, r):
        return tuple((r // 2**i) % 2 for i in reversed(range(self.n)))

    def window(self, p, r, core):
        goal, offset, size = self.phases[p]
        owner = goal * 2**self.bits + 2 * r + core
        return pl.ds(self.start(goal, owner) + offset, size)

    def core_copies(self, p, own=False):
        copies = []
        for r in range(2**self.n):
            spot = p * 2**self.n + r
            where = (p,) + self.digits(r)
            if own:
                copies.append(
                    pltpu.make_async_copy(
                        self.src.at[self.window(p, r, self.mine[0])], self.acc.at[where], self.local_sem.at[spot]
                    )
                )
            else:
                copies.append(
                    pltpu.make_async_remote_copy(
                        src_ref=self.src.at[self.window(p, r, 1 - self.mine[0])],
                        dst_ref=self.first.at[where],
                        send_sem=self.core_send.at[spot],
                        recv_sem=self.core_recv.at[spot],
                        device_id={"blk": self.partner[0]},
                        device_id_type=MESH,
                    )
                )
        return copies

    def order(self, part):
        return list(range(self.n)) if part == 0 else list(reversed(range(self.n)))

    def place(self, p, part, done, pick):
        spots = [slice(None)] * self.n
        for i in self.order(part)[:done]:
            spots[i] = self.mine[i + 1]
        spots[self.order(part)[done]] = pick
        return (p,) + tuple(reversed(spots)) + (slice(part * self.half, (part + 1) * self.half),)

    def bit_copies(self, p, s):
        copies = []
        for part in range(2):
            i = self.order(part)[s]
            spot = (p * self.n + s) * 2 + part
            copies.append(
                pltpu.make_async_remote_copy(
                    src_ref=self.acc.at[self.place(p, part, s, 1 - self.mine[i + 1])],
                    dst_ref=self.bit_recvs[s].at[p, part],
                    send_sem=self.bit_send.at[spot],
                    recv_sem=self.bit_recv.at[spot],
                    device_id={"blk": self.partner[i + 1]},
                    device_id_type=MESH,
                )
            )
        return copies

    def settled(self, p):
        return (p,) + tuple(reversed([self.mine[i + 1] for i in range(self.n)]))

    def z_copy(self, p, up):
        return pltpu.make_async_remote_copy(
            src_ref=self.acc.at[self.settled(p)],
            dst_ref=(self.up if up else self.down).at[p],
            send_sem=self.z_send.at[p],
            recv_sem=self.z_recv.at[2 * p + up],
            device_id={"batch": lax.rem(self.z + (1 if up else self.depth - 1), self.depth)},
            device_id_type=MESH,
        )

    def add(self, dst, dst_at, src, src_at):
        dst[dst_at] += src[src_at]

    def finish_core(self, p):
        for copy in self.core_copies(p, True):
            copy.wait()
        for copy in self.core_copies(p):
            copy.wait_recv()
        for r in range(2**self.n):
            where = (p,) + self.digits(r)
            self.add(self.acc, where, self.first, where)

    def finish_bit(self, p, s):
        for part, copy in enumerate(self.bit_copies(p, s)):
            copy.wait_recv()
            kept = self.place(p, part, s, self.mine[self.order(part)[s] + 1])
            free = [i for i in range(1, 1 + self.n) if isinstance(kept[i], slice)]
            for r in range(2 ** len(free)):
                chosen = tuple((r // 2**j) % 2 for j in reversed(range(len(free))))
                to = list(kept)
                for i, v in zip(free, chosen):
                    to[i] = v
                self.add(self.acc, tuple(to), self.bit_recvs[s], (p, part) + chosen)

    def take(self, p, up):
        self.z_copy(p, up).wait_recv()
        self.add(self.acc, self.settled(p), self.up if up else self.down, p)

    def z_moves(self, p, u):
        goal = self.phases[p][0]
        moves = []
        if self.depth - 1 - u > goal:
            moves.append((self.depth - 1 - u, False))
        if u < goal:
            moves.append((u, True))
        return moves

    def act(self, p, stage):
        n = self.n
        if stage == 0:
            for copy in self.core_copies(p) + self.core_copies(p, True):
                copy.start()
            return
        if stage == 1:
            self.finish_core(p)
        elif stage <= n + 1:
            self.finish_bit(p, stage - 2)
        if stage <= n:
            for copy in self.bit_copies(p, stage - 1):
                copy.start()
            return
        u = stage - n - 1
        for mover, up in self.z_moves(p, u):

            @pl.when(self.z == mover)
            def _():
                if u > 0:
                    self.take(p, up)
                self.z_copy(p, up).start()

    def run(self, t):
        for stage in reversed(range(self.last + 1)):
            p, odd = divmod(t - stage, self.stride)
            if odd == 0 and 0 <= p < len(self.phases):
                self.act(p, stage)

    def collect(self, out_ref):
        for p, (goal, offset, size) in enumerate(self.phases):

            @pl.when(self.z == goal)
            def _():
                if goal < self.depth - 1:
                    self.take(p, False)
                if goal > 0:
                    self.take(p, True)
                out_ref[offset : offset + size] = self.acc[self.settled(p)]

        for p in range(len(self.phases)):
            for copy in self.core_copies(p):
                copy.wait_send()
            for s in range(self.n):
                for copy in self.bit_copies(p, s):
                    copy.wait_send()
            for u in range(self.depth - 1):
                for mover, up in self.z_moves(p, u):

                    @pl.when(self.z == mover)
                    def _():
                        self.z_copy(p, up).wait_send()


def put_restored(value, turn_ref, out_ref, block):
    rows, width = value.shape
    tiles = rows // SUB
    step = out_ref.shape[0] // SUB
    for a in range(width // LANE):
        turn_ref[a] = value[:, a * LANE : (a + 1) * LANE]
    for j in range(SUB):
        here = pl.ds(pl.multiple_of(j * step + block * tiles, tiles), tiles)
        for a in range(width // LANE):
            part = turn_ref[a, pl.ds(j, tiles, stride=SUB), :]
            out_ref[here, a * LANE : (a + 1) * LANE] = part.astype(bf16)


def late_kernel(
    regions,
    bits,
    phases,
    blocks,
    flat_ref,
    early_ref,
    gain_ref,
    *refs,
):
    depth, span = regions.depth, regions.span
    sources, refs = refs[:7], refs[7:]
    window_ref, totals_ref, result_ref, grad_ref = refs[:4]
    held, refs = refs[4:11], refs[11:]
    gate_back, stream_back, in_w, token, cot, gated, out_w = held
    late_ref, turn_ref, gain_sum, sums, ring, load_sem, ring_send, ring_recv = refs[:8]
    work = Reducer(depth, bits, phases, 1, lambda z, owner: regions.in_first(owner) * (regions.per // 2), flat_ref, refs[8:])
    blk, z = work.blk, work.z
    inner = gated.shape[1]
    loads = [pltpu.make_async_copy(src, dst, load_sem.at[i]) for i, (src, dst) in enumerate(zip(sources, held))]
    for load in loads:
        load.start()
    work.greet()
    gain_sum[...] = jnp.zeros_like(gain_sum)
    size = token.shape[0] // blocks
    across = (((1,), (1,)), ((), ()))

    def slot(t, carry):
        for k in range(work.slots):

            @pl.when(t == k)
            def _():
                work.run(k)
                if k == 0:
                    for load in loads:
                        load.wait()

        @pl.when(t < blocks)
        def _():
            here = pl.ds(pl.multiple_of(t * size, size), size)
            source = token[here, :].astype(f32)
            output = jnp.dot(gated[here, :], out_w[...], preferred_element_type=f32)
            put_restored(source + output, turn_ref, result_ref, t)
            grad_normed = lax.dot_general(
                stream_back[here, :], in_w[:, :inner], across, preferred_element_type=f32
            ) + lax.dot_general(gate_back[here, :], in_w[:, inner:], across, preferred_element_type=f32)
            scale = lax.rsqrt(jnp.mean(source * source, axis=-1, keepdims=True) + EPS)
            scaled = source * scale
            part = grad_normed * scaled
            gain_sum[...] += jnp.sum(part.reshape(size // SUB, SUB, part.shape[1]), 0)
            weighted = grad_normed * gain_ref[...]
            mean = jnp.mean(weighted * source, axis=-1, keepdims=True)
            back = scale * weighted - source * (scale * scale * scale) * mean + cot[here, :].astype(f32)
            put_restored(back, turn_ref, grad_ref, t)

        return carry

    lax.fori_loop(0, max(work.slots, blocks), slot, 0)
    late_ref[...] = jnp.zeros_like(late_ref)
    work.collect(late_ref)

    owner = z * 2**bits + blk
    base = regions.base(owner)
    inside = lax.broadcasted_iota(jnp.int32, (SUB, LANE), 0) * LANE + lax.broadcasted_iota(
        jnp.int32, (SUB, LANE), 1
    )
    sums[0, 0] = jnp.zeros((SUB, LANE), f32)
    gain = jnp.sum(gain_sum[...], 0, keepdims=True)
    for a in range(SUB):
        sums[0, 1, a : a + 1, :] = gain[:, a * LANE : (a + 1) * LANE]
    half = regions.per // 2
    window_ref[...] = jnp.zeros_like(window_ref)

    def keep(value, row):
        place = row - base

        @pl.when((place >= 0) & (place < regions.need))
        def _():
            spot = inside + (row * ROW - owner * span)
            own = jnp.where((spot >= 0) & (spot < span), value, 0.0)
            sums[0, 0] += own * own
            window_ref[place] = value

    @pl.when(base < regions.small_base)
    def _():
        def line(d, carry):
            row = regions.in_base + (regions.in_first(owner) + d) * regions.per
            for q in range(half):
                keep(late_ref[d * half + q], row + q)
                keep(early_ref[d * half + q], row + half + q)
            return carry

        lax.fori_loop(0, regions.lines, line, 0)

    @pl.when(base >= regions.small_base)
    def _():
        def line(i, carry):
            keep(early_ref[i], regions.out_base + regions.out_first(owner) + i)
            return carry

        lax.fori_loop(0, regions.slot, line, 0)

    for b in range(bits):
        copy = pltpu.make_async_remote_copy(
            src_ref=sums.at[b],
            dst_ref=sums.at[bits + 1 + b],
            send_sem=ring_send.at[b],
            recv_sem=ring_recv.at[b],
            device_id={"blk": work.partner[b]},
            device_id_type=MESH,
        )
        copy.start()
        copy.wait()
        sums[b + 1] = sums[b] + sums[bits + 1 + b]
    ring[z] = sums[bits]
    for u in range(depth - 1):
        moves = (
            ((z + u < depth) & (z > 0), lax.min(z + u, depth - 1), depth - 1, 0),
            ((z - u >= 0) & (z < depth - 1), lax.max(z - u, 0), 1, 1),
        )
        gets = (
            ((z < depth - 1) & (z + 1 + u < depth), lax.min(z + 1 + u, depth - 1), depth - 1, 0),
            ((z > 0) & (z - 1 - u >= 0), lax.max(z - 1 - u, 0), 1, 1),
        )

        def hop(origin, by, way):
            return pltpu.make_async_remote_copy(
                src_ref=ring.at[origin],
                dst_ref=ring.at[origin],
                send_sem=ring_send.at[bits + u * 2 + way],
                recv_sem=ring_recv.at[bits + u * 2 + way],
                device_id={"batch": lax.rem(z + by, depth)},
                device_id_type=MESH,
            )

        for cond, origin, by, way in moves:

            @pl.when(cond)
            def _():
                hop(origin, by, way).start()

        for cond, origin, by, way in gets:

            @pl.when(cond)
            def _():
                hop(origin, by, way).wait_recv()

        for cond, origin, by, way in moves:

            @pl.when(cond)
            def _():
                hop(origin, by, way).wait_send()

    total = ring[0]
    for zz in range(1, depth):
        total = total + ring[zz]
    totals_ref[...] = total

    @pl.when(base < regions.in_base)
    def _():
        window_ref[0] = total[1]


def late_call(flat, early, gain, sources, regions):
    bits = regions.count.bit_length() - 1
    depth = regions.depth
    phases = regions.late_phases()
    tile = (SUB, LANE)
    dma = pltpu.SemaphoreType.DMA
    hops = bits + 2 * (depth - 1)
    vmem = pl.BlockSpec(memory_space=pltpu.VMEM)
    far = pl.BlockSpec(memory_space=pl.ANY)
    rows, model = sources[3].shape
    blocks = 8
    return pl.pallas_call(
        functools.partial(late_kernel, regions, bits, phases, blocks),
        name="reduce_late",
        in_specs=[far, vmem, vmem] + [far] * len(sources),
        out_specs=[vmem] * 4,
        out_shape=[
            jax.ShapeDtypeStruct((regions.need,) + tile, f32),
            jax.ShapeDtypeStruct((2,) + tile, f32),
            jax.ShapeDtypeStruct((rows, model), bf16),
            jax.ShapeDtypeStruct((rows, model), bf16),
        ],
        scratch_shapes=[pltpu.VMEM(x.shape, x.dtype) for x in sources]
        + [
            pltpu.VMEM((regions.half,) + tile, f32),
            pltpu.VMEM((model // LANE, rows // blocks, LANE), f32),
            pltpu.VMEM((SUB, model), f32),
            pltpu.VMEM((2 * bits + 1, 2) + tile, f32),
            pltpu.VMEM((depth, 2) + tile, f32),
            dma((len(sources),)),
            dma((hops,)),
            dma((hops,)),
        ]
        + Reducer.scratch(depth, bits, phases),
        compiler_params=pltpu.CompilerParams(
            vmem_limit_bytes=62 * 2**20, collective_id=1, has_side_effects=True
        ),
    )(flat, early, gain, *sources)


def share(regions, gain, in_part, small, out_part, owner):
    base, high = regions.base(owner), regions.need
    place = (base + lax.iota(jnp.int32, high))[:, None, None]
    total = jnp.broadcast_to(gain, (high, SUB, LANE))
    for part, origin, low in (
        (in_part, regions.in_base + regions.in_first(owner) * regions.per, regions.in_base),
        (small, regions.small_base, regions.small_base),
        (out_part, regions.out_base + regions.out_first(owner), regions.out_base),
    ):
        padded = jnp.pad(part, ((high, high), (0, 0), (0, 0)))
        offset = jnp.clip(base - origin + high, 0, part.shape[0] + high)
        total = jnp.where(place >= low, lax.dynamic_slice_in_dim(padded, offset, high), total)
    return lax.dynamic_slice_in_dim(total.reshape(-1), owner * regions.span % ROW, regions.span)


def exchange(totals, state):
    count = lax.axis_size("blk")
    index = lax.axis_index("blk")
    decay, end, leave = totals[:state], totals[state : 2 * state], totals[2 * state :]
    pre_decay, pre_state = jnp.ones_like(decay), jnp.zeros_like(end)
    post_decay, post_state = jnp.ones_like(decay), jnp.zeros_like(end)
    bit = 1
    while bit < count:
        pairs = [(i, i ^ bit) for i in range(count)]
        far = lax.ppermute(jnp.concatenate([decay, end, leave], 0), "blk", pairs)
        far_decay, far_end, far_leave = far[:state], far[state : 2 * state], far[2 * state :]
        upper = (index & bit) != 0
        pre_state = jnp.where(upper, pre_state + pre_decay * far_end, pre_state)
        pre_decay = jnp.where(upper, pre_decay * far_decay, pre_decay)
        post_state = jnp.where(upper, post_state, post_state + post_decay * far_leave)
        post_decay = jnp.where(upper, post_decay, post_decay * far_decay)
        end = jnp.where(upper, end + decay * far_end, far_end + far_decay * end)
        leave = jnp.where(upper, far_leave + far_decay * leave, leave + decay * far_leave)
        decay = decay * far_decay
        bit *= 2
    return pre_state, post_state


def local(
    tokens,
    out_cot,
    norm_gain,
    in_weight,
    conv_weight,
    conv_bias,
    xproj_weight,
    dt_weight,
    dt_bias,
    a_log,
    d_skip,
    out_weight,
    moment_one,
    moment_two,
):
    contract = (((0,), (0,)), ((), ()))
    backward = (((1,), (1,)), ((), ()))
    token_rows = interleave(tokens[0])
    cot_low = interleave(out_cot[0])
    source = token_rows.astype(f32)
    length = source.shape[0]
    inner = dt_bias.shape[0]
    state = a_log.shape[0]
    rank = dt_weight.shape[0]
    width = conv_weight.shape[0]
    halo = (width - 1) * SUB
    scale = lax.rsqrt(jnp.mean(source * source, axis=-1, keepdims=True) + EPS)
    normed = (source * scale * norm_gain).astype(bf16)
    stream = jnp.dot(normed, in_weight[:, :inner], preferred_element_type=f32)
    ends = stream[length - halo :].reshape(width - 1, SUB, inner)
    tail = shifted(ends[:, SUB - 1], "blk", 1)
    gating = jnp.dot(normed, in_weight[:, inner:], preferred_element_type=f32)
    grad_gated = lax.dot_general(cot_low, out_weight, backward, preferred_element_type=f32)
    head = jnp.concatenate([tail[:, None], ends[:, : SUB - 1]], 1).reshape(halo, inner)
    rates = -jnp.exp(a_log)
    rates_wide = jnp.repeat(rates * LOG2E, SUB, axis=0)
    spots = spread_table(2 * state)
    spare = LANE - rank - 2 * state
    select_in = jnp.pad(jnp.roll(xproj_weight, 2 * state, 1), ((0, 0), (0, spare)))
    step_in = jnp.pad(dt_weight, ((2 * state, spare), (0, 0)))
    (
        conv_sum,
        conv_low,
        step_size,
        drive,
        grad_scanned,
        sel_low,
        terms,
        pre_decay,
        pre_state,
        post_decay,
        post_state,
        totals,
    ) = summary_call(
        stream,
        gating,
        grad_gated,
        head,
        conv_weight,
        conv_bias[None],
        select_in,
        step_in,
        dt_bias[None],
        spots,
        rates_wide,
    )
    entry, arriving = exchange(totals, state)
    prior, readout_grads, gated, grad_gating, skip_grads = forward_call(
        step_size,
        drive,
        grad_scanned,
        terms,
        spots,
        rates_wide,
        pre_decay,
        pre_state,
        entry,
        conv_low,
        gating,
        grad_gated,
        d_skip[None],
    )
    grad_d_skip = jnp.sum(skip_grads, 0)

    span = moment_one.shape[0]
    small_rows = sum(
        value.size for value in (conv_weight, conv_bias, xproj_weight, dt_weight, dt_bias, a_log, d_skip)
    ) // ROW
    regions = Regions(
        lax.axis_size("batch"),
        lax.axis_size("blk"),
        span,
        norm_gain.size // ROW,
        in_weight.shape,
        small_rows,
        out_weight.shape,
    )
    flat_early = product_call((normed, grad_gating), (gated, cot_low))
    step_back = step_in.T
    select_back = select_in.T
    grad_stream_low, grad_pre_low, grad_selectors, rate_grads, taps_grads, edges, early = backward_call(
        step_size,
        drive,
        grad_scanned,
        terms,
        spots,
        rates_wide,
        post_state + post_decay * jnp.repeat(arriving, SUB, axis=0),
        prior,
        conv_sum,
        stream,
        readout_grads,
        step_back,
        select_back,
        conv_weight,
        d_skip[None],
        flat_early,
        regions,
    )
    grad_a_log = LN2 * jnp.sum(rate_grads.reshape(state, SUB, inner), 1)
    begins = edges[:halo].reshape(width - 1, SUB, inner)
    ahead = shifted(begins[:, 0], "blk", -1)
    grad_dt_weight = lax.dot_general(sel_low, grad_pre_low, contract, preferred_element_type=f32)[
        2 * state : 2 * state + rank
    ]
    grad_xproj = lax.dot_general(grad_selectors, conv_low, contract, preferred_element_type=f32)
    foot = jnp.concatenate([begins[:, 1:], ahead[:, None]], 1)
    lasts = edges[halo:].reshape(width - 1, SUB, inner)
    further = jnp.concatenate([lasts, foot], 0)
    last_stream = stream[length - halo :].reshape(width - 1, SUB, inner)
    grad_last = conv_weight[width - 1] * lasts
    taps_grads = jnp.sum(taps_grads.reshape(width + 2, SUB, inner), 1)
    tap_grads = []
    for offset in range(width - 1):
        lead = width - 1 - offset
        grad_last = grad_last + conv_weight[offset] * further[lead : lead + width - 1]
        over = jnp.sum(last_stream[width - 1 - lead :] * foot[:lead], (0, 1))
        tap_grads.append(taps_grads[offset] + over)
    tap_grads.append(taps_grads[width - 1])
    grad_conv_weight = jnp.stack(tap_grads, 0)
    grad_conv_bias = taps_grads[width]
    grad_dt_bias = taps_grads[width + 1]
    grad_stream_low = lax.dynamic_update_slice_in_dim(
        grad_stream_low, grad_last.reshape(halo, inner).astype(bf16), length - halo, 0
    )
    thin = (grad_xproj, grad_dt_weight, grad_a_log, grad_conv_weight, grad_conv_bias, grad_dt_bias, grad_d_skip)
    thin = jnp.concatenate([value.reshape(-1, inner) for value in thin], 0)
    grad_stream_low, thin = lax.optimization_barrier((grad_stream_low, thin))
    thin = lax.psum(jnp.pad(thin, ((0, -thin.shape[0] % SUB), (0, 0))), ("batch", "blk"))
    parts = []
    for value in (LANE, rank, state, width, 1, 1, 1):
        start = sum(part.shape[0] for part in parts)
        parts.append(thin[start : start + value])
    used = rank + 2 * state
    xproj = jnp.roll(parts[0][:used], rank, 0).T
    order = (parts[3], parts[4], xproj, parts[1], parts[5], parts[2], parts[6])
    small = jnp.concatenate([value.reshape(-1, ROW) for value in order], 0)
    window, totals, result, grad_tokens = late_call(
        product_call((normed, grad_stream_low)),
        early,
        norm_gain[None],
        (grad_gating, grad_stream_low, in_weight, token_rows, cot_low, gated, out_weight),
        regions,
    )
    result, grad_tokens = result[None], grad_tokens[None]
    grad_norm = jnp.sqrt(jnp.sum(totals[0]) + jnp.sum(totals[1] * totals[1]) + jnp.sum(small * small))
    owner = lax.axis_index(("batch", "blk"))
    begin = owner * span
    base, high = regions.base(owner), regions.need
    place = (base + lax.iota(jnp.int32, high))[:, None, None]
    padded = jnp.pad(small.reshape(-1, SUB, LANE), ((high, high), (0, 0), (0, 0)))
    offset = jnp.clip(base - regions.small_base + high, 0, small_rows + high)
    window = jnp.where(
        (place >= regions.small_base) & (place < regions.out_base),
        lax.dynamic_slice_in_dim(padded, offset, high),
        window,
    )
    shard = lax.dynamic_slice_in_dim(window.reshape(-1), begin % ROW, span)
    in_part = lax.dynamic_slice_in_dim(in_weight, regions.in_first(owner), regions.lines)
    out_part = lax.dynamic_slice_in_dim(out_weight, regions.out_first(owner), regions.slot)
    small_params = (conv_weight, conv_bias, xproj_weight, dt_weight, dt_bias, a_log, d_skip)
    small_params = jnp.concatenate([value.reshape(-1, ROW).astype(f32) for value in small_params], 0)
    owned = share(
        regions,
        norm_gain.reshape(-1, SUB, LANE),
        in_part.astype(f32).reshape(-1, SUB, LANE),
        small_params.reshape(-1, SUB, LANE),
        out_part.astype(f32).reshape(-1, SUB, LANE),
        owner,
    )
    lower = norm_gain.size + in_weight.size + sum(
        value.size for value in (conv_weight, conv_bias, xproj_weight, dt_weight)
    )
    upper = lower + dt_bias.size + a_log.size + d_skip.size
    place = begin + lax.iota(jnp.int32, span)
    keep = jnp.where((place >= lower) & (place < upper), 0.0, 1.0).astype(f32)
    clipped = shard * jnp.minimum(1.0, CLIP / (grad_norm + 1e-06))
    new_one = BETA_ONE * moment_one + (1.0 - BETA_ONE) * clipped
    new_two = BETA_TWO * moment_two + (1.0 - BETA_TWO) * clipped * clipped
    first = new_one / (1.0 - BETA_ONE**ADAM_STEP)
    second = new_two / (1.0 - BETA_TWO**ADAM_STEP)
    param_step = -RATE * (first / (jnp.sqrt(second) + ADAM_EPS) + DECAY * keep * owned)
    return (result, grad_tokens, shard, grad_norm, param_step, new_one, new_two)


def solution(mesh):
    return jax.shard_map(
        local,
        mesh=mesh,
        in_specs=(P("batch", "blk", None),) * 2 + (P(),) * 10 + (P(("batch", "blk")),) * 2,
        out_specs=(P("batch", "blk", None),) * 2
        + (P(("batch", "blk")), P(), P(("batch", "blk")), P(("batch", "blk")), P(("batch", "blk"))),
        check_vma=False,
    )
```

time: 680 us -> 612 us (0.900)
  matrix products: 91.3 us -> 29 us
  other arithmetic: 61.6 us -> 28.8 us
  local copies, waits for them, and re-layouts: 30 us -> 54.8 us
  Pallas kernels: 461 us -> 440 us
  between operations: 2.87 us -> 18.4 us
  waiting for transfers between devices: 15.4 us -> 26.4 us
    dot_general x9 -> x2, matrix products: 65.3 us -> 4.1 us  [the longest x1 3.16 us: local(): lax.dot_general(grad_selectors, conv_low, contract, preferred_element_typ...]
    pallas_call x3 -> x4, Pallas kernels: 332 us -> 278 us  [the longest x1 141 us: backward_call(): pl.pallas_call(functools.partial(backward_kernel, shape, count, regions,...]
    pallas_call x1, Pallas kernels: 57.6 us -> 90.4 us  [summary_call(): pl.pallas_call(functools.partial(summary_kernel, shape), name='scan_summa...]
    convert_element_type x3 -> x1, other arithmetic: 24.6 us -> 1.43 us  [spread_table(): return ((row % count == col) & (row < 3 * count)).astype(bf16)]
    psum x0 -> x1, waiting for transfers between devices: none -> 13.1 us  [local(): lax.psum(jnp.pad(thin, ((0, -thin.shape[0] % SUB), (0, 0))), ('batch', 'b...]
    unnamed x105 -> x118, local copies, waits for them, and re-layouts: 8.86 us -> 19.8 us
    transpose x2, other arithmetic: 11.8 us -> 0.97 us  [the longest x1 0.9 us: local(): select_back = select_in.T]
    reshape x6 -> x9, local copies, waits for them, and re-layouts: 0.34 us -> 7.91 us  [the longest x1 4.31 us: interleave(): x.reshape(SUB, rows // SUB, width).transpose(1, 0, 2).reshape(rows, width)]
  transfers between devices with their start and end apart: 5 -> 6, of which waited for: 2 -> 3; matrix products, arithmetic and copies ran while one was open for 7% -> 9% of each run, Pallas kernels for 0% -> 19%
where the time goes in v3:
time: 612 us; the launch traced here: 607 us
  Pallas kernels  440 us (72%)
  local copies, waits for them, and re-layouts  54.8 us (9%)
  matrix products  29 us (5%)
  other arithmetic  28.8 us (5%)
  waiting for transfers between devices  26.4 us (4%)
  between operations  18.4 us (3%)
  starting transfers between devices  9.77 us (2%)
    pallas_call x1, Pallas kernels, backward_call(): pl.pallas_call(functools.partial(backward_kernel, shape, count, regions,...  141 us
    pallas_call x1, Pallas kernels, late_call(): pl.pallas_call(functools.partial(late_kernel, regions, bits, phases, bloc...  99.3 us
    pallas_call x1, Pallas kernels, summary_call(): pl.pallas_call(functools.partial(summary_kernel, shape), name='scan_summa...  90.4 us
    pallas_call x1, Pallas kernels, forward_call(): pl.pallas_call(functools.partial(forward_kernel, shape), name='scan_forwa...  71.2 us
    pallas_call x2, Pallas kernels, product_call(): pl.pallas_call(functools.partial(product_kernel, steps, shapes), name='fl...  37.4 us
    unnamed x118, local copies, waits for them, and re-layouts  19.8 us
    ppermute x3, waiting for transfers between devices, exchange(): far = lax.ppermute(jnp.concatenate([decay, end, leave], 0), 'blk', pairs)  13.3 us
    psum x1, waiting for transfers between devices, local(): lax.psum(jnp.pad(thin, ((0, -thin.shape[0] % SUB), (0, 0))), ('batch', 'b...  13.1 us
  transfers between devices with their start and end apart: 6, of which 3 were waited for; matrix products, arithmetic and copies ran while one was open for 9% of the time, Pallas kernels for 19%

profile of v3, /device:TPU:0, one launch (start us, length us, event | category | flops | bytes accessed | tf_op | source)
XLA Modules:
  0.0 606.7 jit_solution(7681657204057446472)
XLA Ops:
  7.2 2.9 multiply_reduce_fusion
  10.3 1.5 multiply_convert_fusion.refs_0_
  11.9 7.1 %fusion.2.stream_ref = f32[1024,2048]{1,0:T(8,128)S(1)} fusion(bf16[1024,1024]{1,0:T(8,128)(2,1)S(1)} %multiply_convert_fusion.refs_0_, bf16[1024,4096]{1,0:T(8,128)(2,1)} %refs_2_.1), kind=kOutput, calls=%fused_computation.2 | convolution fusion | flops 4294967296 | bytes 14680064 | tf_op jit(solution)/shard_map/dot_general | solution.py:1325
  19.8 3.2 collective-permute-start
  23.1 6.8 %fusion.gating_ref = f32[1024,2048]{1,0:T(8,128)} fusion(bf16[1024,1024]{1,0:T(8,128)(2,1)S(1)} %multiply_convert_fusion.refs_0_, bf16[1024,4096]{1,0:T(8,128)(2,1)S(1)} %bitcast.103), kind=kOutput, calls=%fused_computation | convolution fusion | flops 4294967296 | bytes 14680064 | tf_op jit(solution)/shard_map/dot_general | solution.py:1328
  33.4 1.6 concatenate.86
  36.0 1.9 constant_dynamic-slice_fusion
  39.4 1.5 reshape.199
  41.0 11.0 %fusion.39.grad_gated_ref = f32[1024,2048]{1,0:T(8,128)} fusion(bf16[2048,1024]{1,0:T(8,128)(2,1)} %refs_6_.1, bf16[8,128,1024]{2,1,0:T(8,128)(2,1)} %bitcast.106), kind=kOutput, calls=%fused_computation.129 | convolution fusion | flops 4294967296 | bytes 14680064 | tf_op jit(solution)/shard_map/dot_general | solution.py:1329
  57.3 1.4 fusion.5.spots_ref
  58.7 1.9 dynamic-slice_bitcast_fusion
  64.4 90.4 %scan_summary.1 = (f32[1024,2048]{1,0:T(8,128)}, bf16[1024,2048]{1,0:T(8,128)(2,1)}, f32[1024,2048]{1,0:T(8,128)}, f32[1024,2048]{1,0:T(8,128)}, f32[1024,2048]{...) custom-call(f32[1024,2048]{1,0:T(8,128)} %copy-done, ...), custom_call_target="tpu_custom_call" | custom-call | tf_op jit(solution)/shard_map/scan_summary/pallas_call | solution.py:593
  154.9 2.1 collective-permute-start.1
  162.3 1.6 collective-permute-start.2
  164.4 8.9 %collective-permute-done.2 = f32[48,2048]{1,0:T(8,128)S(1)} collective-permute-done((f32[48,2048]{1,0:T(8,128)S(1)}, f32[48,2048]{1,0:T(8,128)S(1)}, u32[]{:S(2)}, u32[]{:S(2)}) %collective-permute-start.2) | collective-permute-done | bytes 393248 | tf_op jit(solution)/shard_map/ppermute | solution.py:1282
  173.5 1.6 collective-permute-start.3
  175.0 4.3 copy_bitcast_fusion
  179.4 4.4 collective-permute-done.3
  183.7 1.8 add_select_fusion
  185.5 71.2 %scan_forward.1 = (bf16[16384,2048]{1,0:T(8,128)(2,1)}, f32[1024,128]{1,0:T(8,128)}, bf16[1024,2048]{1,0:T(8,128)(2,1)}, bf16[1024,2048]{1,0:T(8,128)(2,1)}, f32[8,2048]{1,0:T(8,128)}) custom-call(f32[1024,2048]{1,0:T(8,128)} %get-tuple-element.37.step_ref, f32[1024,2048]{1,0:T(8,128)} %get-tuple-element.38.drive_ref, ...), custom_call_target="tpu_custom_call" | custom-call | tf_op jit(solution)/shard_map/scan_forward/pallas_call | solution.py:622
  256.8 24.1 %flat_product.2.flat_ref = f32[4096,8,128]{2,1,0:T(8,128)} custom-call(bf16[1024,1024]{1,0:T(8,128)(2,1)} %copy-done.1, bf16[1024,2048]{1,0:T(8,128)(2,1)} %get-tuple-element.50.refs_1_.refs_0_, bf16[1024,2048]{1,0:T(8,128)(2,1)} %get-tuple-element.51.refs_2_.refs_5_, bf16[1024,1024]{1,0:T(8,128)(2,1)} %get-tuple-element.106.refs_3_.refs_4_), custom_call_target="tpu_custom_call" | custom-call | tf_op jit(solution)/shard_map/flat_product/pallas_call | solution.py:765
  282.0 141.3 %scan_backward.1 = (bf16[1024,2048]{1,0:T(8,128)(2,1)}, bf16[1024,2048]{1,0:T(8,128)(2,1)}, bf16[1024,128]{1,0:T(8,128)(2,1)}, f32[128,2048]{1,0:T(8,128)}, f32[...) custom-call(f32[1024,2048]{1,0:T(8,128)} %get-tuple-element.37.step_ref, ...), custom_call_target="tpu_custom_call" | custom-call | tf_op jit(solution)/shard_map/scan_backward/pallas_call | solution.py:674
  426.3 3.2 fusion.44
  436.5 1.3 pad.34
  439.2 3.1 fusion.13
  442.3 13.3 %flat_product.3.flat_ref = f32[2048,8,128]{2,1,0:T(8,128)} custom-call(bf16[1024,1024]{1,0:T(8,128)(2,1)} %copy-done.1, bf16[1024,2048]{1,0:T(8,128)(2,1)} %bitcast_dynamic-update-slice_fusion.refs_1_), custom_call_target="tpu_custom_call" | custom-call | tf_op jit(solution)/shard_map/flat_product/pallas_call | solution.py:765
  455.5 99.3 %reduce_late.1 = (f32[205,8,128]{2,1,0:T(8,128)}, f32[2,8,128]{2,1,0:T(8,128)}, bf16[1024,1024]{1,0:T(8,128)(2,1)}, bf16[1024,1024]{1,0:T(8,128)(2,1)}) custom-call(f32[2048,8,128]{2,1,0:T(8,128)} %flat_product.3.flat_ref, f32[208,8,128]{2,1,0:T(8,128)} %get-tuple-element.61.early_ref, f32[1,1024]{1,0:T(1,128)} %bitcast.112, ...), custom_call_target="tpu_custom_call" | custom-call | tf_op jit(solution)/shard_map/reduce_late/pallas_call | solution.py:1229
  557.4 13.1 %all-reduce.9.cloned.1.call-done = f32[216,2048]{1,0:T(8,128)} async-done(((f32[216,2048]{1,0:T(8,128)}), f32[216,2048]{1,0:T(8,128)}) %all-reduce.9.cloned.1.call-update) | async-done | bytes 1769488 | tf_op jit(solution)/shard_map/psum | solution.py:1445
  572.9 1.7 reshape.191
  579.9 4.6 concatenate.82
  587.8 2.0 constant_dynamic-update-slice_fusion.3
  592.1 2.7 add_multiply_fusion
  (195 shorter events, 51.7 us)
Async XLA Ops:
  7.2 563.3 %all-reduce.9.cloned.1.call-start = ((), (), s32[]{:S(2)}) async-start(), calls=%async_computation | async-start | bytes 3538944 | tf_op jit(solution)/shard_map/psum | solution.py:1445
  10.3 12.8 %slice-start = ((s8[8388608]{0:T(1024)(128)(4,1)}), s8[4194304]{0:T(1024)(128)(4,1)S(1)}, s32[]{:S(2)}) async-start(s8[8388608]{0:T(1024)(128)(4,1)} %bitcast.102), calls=%async_computation.1 | async-start | bytes 8388608
  11.8 11.2 %copy-start.1 = (bf16[1024,1024]{1,0:T(8,128)(2,1)}, bf16[1024,1024]{1,0:T(8,128)(2,1)S(1)}, u32[]{:S(2)}) copy-start(bf16[1024,1024]{1,0:T(8,128)(2,1)S(1)} %multiply_convert_fusion.refs_0_) | copy-start | bytes 6291460
  11.8 11.2 %slice-start.1 = ((s8[8388608]{0:T(1024)(128)(4,1)}), s8[4194304]{0:T(1024)(128)(4,1)S(1)}, s32[]{:S(2)}) async-start(s8[8388608]{0:T(1024)(128)(4,1)} %bitcast.102), calls=%async_computation.2 | async-start | bytes 8388608
  19.0 10.9 %copy-start = (f32[1024,2048]{1,0:T(8,128)}, f32[1024,2048]{1,0:T(8,128)S(1)}, u32[]{:S(2)}) copy-start(f32[1024,2048]{1,0:T(8,128)S(1)} %fusion.2.stream_ref) | copy-start | bytes 25165828
  19.0 10.9 %copy-start.18 = (f32[3,8,2048]{2,1,0:T(8,128)}, f32[3,8,2048]{2,1,0:T(8,128)S(1)}, u32[]{:S(2)}) copy-start(f32[3,8,2048]{2,1,0:T(8,128)S(1)} %slice_bitcast_fusion.2) | copy-start | bytes 589828
  19.8 12.4 %copy-start.12 = (bf16[2048,96]{0,1:T(8,128)(2,1)S(1)}, bf16[2048,96]{0,1:T(8,128)(2,1)}, u32[]{:S(2)}) copy-start(bf16[2048,96]{0,1:T(8,128)(2,1)} %param.20) | copy-start | bytes 1179652
  19.8 43.1 %collective-permute-start = (f32[3,2048]{1,0:T(4,128)}, f32[3,2048]{1,0:T(4,128)}, u32[]{:S(2)}, u32[]{:S(2)}) collective-permute-start(f32[3,2048]{1,0:T(4,128)} %bitcast.97), channel_id=1, source_target_pairs={{0,1},{1,2},{2,3},{3,4},{4,5},{5,6},{6,7},{8,9},{9,10},{10,11},{11... | collective-permute-start | bytes 73736 | tf_op jit(solution)/shard_map/ppermute | solution.py:36
  35.0 5.9 copy-start.16
  41.0 11.0 %slice-start.2 = ((bf16[2048,96]{0,1:T(8,128)(2,1)}), bf16[2048,64]{0,1:T(8,128)(2,1)S(1)}, s32[]{:S(2)}) async-start(bf16[2048,96]{0,1:T(8,128)(2,1)} %param.20), calls=%async_computation.3 | async-start | bytes 524288 | tf_op jit(solution)/shard_map/jit(_roll_static)/slice | solution.py:1335
  41.0 11.0 %slice-start.3 = ((bf16[2048,96]{0,1:T(8,128)(2,1)}), bf16[2048,32]{0,1:T(8,128)(2,1)S(1)}, s32[]{:S(2)}) async-start(bf16[2048,96]{0,1:T(8,128)(2,1)} %param.20), calls=%async_computation.4 | async-start | bytes 262144 | tf_op jit(solution)/shard_map/jit(_roll_static)/slice | solution.py:1335
  41.0 12.0 %copy-start.36 = (f32[2048]{0:T(1024)S(1)}, f32[2048]{0:T(1024)}, u32[]{:S(2)}) copy-start(f32[2048]{0:T(1024)} %param.19) | copy-start | bytes 24580
  41.0 12.6 %copy-start.4 = (f32[192,8,128]{2,1,0:T(8,128)S(1)}, f32[192,8,128]{2,1,0:T(8,128)}, u32[]{:S(2)}) copy-start(f32[192,8,128]{2,1,0:T(8,128)} %reshape.199) | copy-start | bytes 2359300
  52.0 4.6 copy-start.29
  52.0 5.2 copy-start.30
  52.0 5.2 copy-start.38
  52.0 5.2 copy-start.43
  52.1 5.2 copy-start.44
  52.1 5.2 copy-start.45
  52.1 5.2 copy-start.46
  64.4 93.1 %copy-start.8 = (bf16[52,4096]{1,0:T(8,128)(2,1)S(1)}, bf16[52,4096]{1,0:T(8,128)(2,1)}, u32[]{:S(2)}) copy-start(bf16[52,4096]{1,0:T(8,128)(2,1)} %constant_dynamic-slice_fusion) | copy-start | bytes 1277956
  64.4 94.1 %copy-start.11 = (bf16[26,8,8,128]{3,1,2,0:T(8,128)(2,1)S(1)}, bf16[26,8,8,128]{3,1,2,0:T(8,128)(2,1)}, u32[]{:S(2)}) copy-start(bf16[26,8,8,128]{3,1,2,0:T(8,128)(2,1)} %dynamic-slice_bitcast_fusion) | copy-start | bytes 1277956
  154.9 6.1 %collective-permute-start.1 = (f32[48,2048]{1,0:T(8,128)}, f32[48,2048]{1,0:T(8,128)}, u32[]{:S(2)}, u32[]{:S(2)}) collective-permute-start(f32[48,2048]{1,0:T(8,128)} %get-tuple-element.43), channel_id=1, source_target_pairs={{0,1},{1,0},{2,3},{3,2},{4,5},{5,4},{6,7},{7,6},{8,9},{9,8},{10,11... | collective-permute-start | bytes 1179656 | tf_op jit(solution)/shard_map/ppermute | solution.py:1282
  158.5 5.3 copy-start.25
  161.0 14.1 %copy-start.7 = (bf16[1,1024,1024]{2,1,0:T(8,128)(2,1)S(1)}, bf16[1,1024,1024]{2,1,0:T(8,128)(2,1)}, u32[]{:S(2)}) copy-start(bf16[1,1024,1024]{2,1,0:T(8,128)(2,1)} %param.15) | copy-start | bytes 6291460
  162.3 11.1 %collective-permute-start.2 = (f32[48,2048]{1,0:T(8,128)S(1)}, f32[48,2048]{1,0:T(8,128)S(1)}, u32[]{:S(2)}, u32[]{:S(2)}) collective-permute-start(f32[48,2048]{1,0:T(8,128)S(1)} %pad_maximum_fusion), channel_id=1, source_target_pairs={{0,2},{1,3},{2,0},{3,1},{4,6},{5,7},{6,4},{7,5},{8,10},{9,11},{10,... | collective-permute-start | bytes 1179656 | tf_op jit(solution)/shard_map/ppermute | solution.py:1282
  173.5 10.3 %collective-permute-start.3 = (f32[48,2048]{1,0:T(8,128)S(1)}, f32[48,2048]{1,0:T(8,128)S(1)}, u32[]{:S(2)}, u32[]{:S(2)}) collective-permute-start(f32[48,2048]{1,0:T(8,128)S(1)} %pad_maximum_fusion.1), channel_id=1, source_target_pairs={{0,4},{1,5},{2,6},{3,7},{4,0},{5,1},{6,2},{7,3},{8,12},{9,13},{10,... | collective-permute-start | bytes 1179656 | tf_op jit(solution)/shard_map/ppermute | solution.py:1282
  256.7 24.1 %copy-start.14 = (f32[128,2048]{1,0:T(8,128)S(1)}, f32[128,2048]{1,0:T(8,128)}, u32[]{:S(2)}) copy-start(f32[128,2048]{1,0:T(8,128)} %get-tuple-element.42) | copy-start | bytes 3145732
  256.8 24.1 %copy-start.15 = (f32[128,2048]{1,0:T(8,128)S(1)}, f32[128,2048]{1,0:T(8,128)}, u32[]{:S(2)}) copy-start(f32[128,2048]{1,0:T(8,128)} %get-tuple-element.41) | copy-start | bytes 3145732
  425.0 6.3 %collective-permute-start.4 = (f32[3,2048]{1,0:T(4,128)}, f32[3,2048]{1,0:T(4,128)}, u32[]{:S(2)}, u32[]{:S(2)}) collective-permute-start(f32[3,2048]{1,0:T(4,128)} %bitcast.96), channel_id=1, source_target_pairs={{1,0},{2,1},{3,2},{4,3},{5,4},{6,5},{7,6},{9,8},{10,9},{11,10},{12... | collective-permute-start | bytes 73736 | tf_op jit(solution)/shard_map/ppermute | solution.py:36
  584.4 7.2 %copy-start.39 = (pred[205]{0:T(512)(128)(4,1)S(1)}, pred[205]{0:T(512)(128)(4,1)}, u32[]{:S(2)}) copy-start(pred[205]{0:T(512)(128)(4,1)} %get-tuple-element.108) | copy-start | bytes 619
  585.4 6.2 %copy-start.21 = (f32[205,8,128]{2,1,0:T(8,128)S(1)}, f32[205,8,128]{2,1,0:T(8,128)}, u32[]{:S(2)}) copy-start(f32[205,8,128]{2,1,0:T(8,128)} %get-tuple-element.65) | copy-start | bytes 2519044
  (26 other events, 68.8 us)
Sparse Core Ops, SparseCore 0:
  437.9 132.5 all-reduce.8

commit v4 on v3

--- a/solution.py
+++ b/solution.py
@@ -60,14 +60,9 @@
 
 
 def gather_lanes(src_ref, spots_ref, out_ref):
-    value = src_ref[...]
-    high = value.astype(bf16)
-    low = (value - high.astype(f32)).astype(bf16)
-    spots = spots_ref[0:LANE, 0 : value.shape[1]]
+    spots = spots_ref[0:LANE, 0 : src_ref.shape[1]]
     back = (((1,), (1,)), ((), ()))
-    out_ref[...] = lax.dot_general(high, spots, back, preferred_element_type=f32) + lax.dot_general(
-        low, spots, back, preferred_element_type=f32
-    )
+    out_ref[...] = lax.dot_general(src_ref[...].astype(bf16), spots, back, preferred_element_type=f32)
 
 
 def spread_table(count):
@@ -106,6 +101,7 @@
     prod_ref,
     select_ref,
     longer_ref,
+    wide_ref,
 ):
     tiles, state, inner, cols, group = shape
     turn = pl.program_id(0)
@@ -142,24 +138,29 @@
             grad_ref[here, lanes] = grad_gated_ref[here, lanes] * (gating * jax.nn.sigmoid(gating))
             return carry
 
-        lax.fori_loop(0, tiles // 2, pair, 0, unroll=4)
+        lax.fori_loop(0, tiles // 2, pair, 0, unroll=8)
         return carry
 
     lax.fori_loop(0, inner // (2 * LANE), convs, 0)
     lane = lax.broadcasted_iota(jnp.int32, (block, LANE), 1)
-    selectors = jnp.dot(conv_ref[...], select_in_ref[...], preferred_element_type=f32)
-    low = selectors.astype(bf16)
-    low_ref[...] = low
-    value = jnp.where(lane < 2 * state, selectors, 0.0)
+    rank = step_in_ref.shape[0]
+    used = rank + 2 * state
+    wide_ref[...] = jnp.zeros_like(wide_ref)
+    wide_ref[:, :used] = jnp.dot(conv_ref[...], select_in_ref[...], preferred_element_type=f32)
+    selectors = wide_ref[...]
+    low_ref[...] = selectors.astype(bf16)
+    low = low_ref[:, :rank]
+    value = jnp.where(lane < 2 * state, pltpu.roll(selectors, LANE - rank, 1), 0.0)
     high = value.astype(bf16).astype(f32)
     middle = (value - high).astype(bf16).astype(f32)
     rest = value - high - middle
     sel_ref[...] = (high + pltpu.roll(middle, 2 * state, 1) + pltpu.roll(rest, 4 * state, 1)).astype(bf16)
 
+    step_ref[...] = jnp.dot(low, step_in_ref[...], preferred_element_type=f32)
+
     def steps(c, carry):
         lanes = at(c * 2 * LANE, 2 * LANE)
         bias = step_bias_ref[:, lanes]
-        step_ref[:, lanes] = jnp.dot(low, step_in_ref[:, lanes], preferred_element_type=f32)
 
         def pair(i, carry):
             here = at(i * 2 * SUB, 2 * SUB)
@@ -169,7 +170,7 @@
             drive_ref[here, lanes] = step * conv_ref[here, lanes].astype(f32)
             return carry
 
-        lax.fori_loop(0, tiles // 2, pair, 0, unroll=4)
+        lax.fori_loop(0, tiles // 2, pair, 0, unroll=8)
         return carry
 
     lax.fori_loop(0, inner // (2 * LANE), steps, 0)
@@ -349,7 +350,7 @@
             return total + product[:SUB] + product[SUB:]
 
         zero = jnp.zeros((SUB, 2 * LANE), f32)
-        skip_grad_ref[:, lanes] += lax.fori_loop(0, tiles // 2, pair, zero, unroll=4)
+        skip_grad_ref[:, lanes] += lax.fori_loop(0, tiles // 2, pair, zero, unroll=8)
         return carry
 
     lax.fori_loop(0, inner // (2 * LANE), finish, 0)
@@ -361,7 +362,6 @@
     regions,
     bits,
     phases,
-    stride,
     step_ref,
     drive_ref,
     grad_ref,
@@ -392,14 +392,23 @@
     feed_ref,
     grad_conv_ref,
     inject_grad_ref,
+    low_grad_ref,
     *refs,
 ):
-    tiles, state, inner, cols, group = shape
+    tiles, state, inner, cols, group, rank = shape
     block = tiles * SUB
     width = taps_ref.shape[0]
     halo = (width - 1) * SUB
     turn = pl.program_id(0)
-    work = Reducer(regions.depth, bits, phases, stride, regions.early_start, flat_ref, refs)
+    work = Reducer(
+        regions.depth,
+        bits,
+        phases,
+        1,
+        lambda p, owner: regions.early_start(phases[p][0], owner) + phases[p][1],
+        flat_ref,
+        refs,
+    )
     turns = scan_turns
     early = max(work.slots - turns, 0)
     for g in range(turns):
@@ -495,26 +504,30 @@
             return total + pre[:SUB] + pre[SUB:]
 
         zero = jnp.zeros((SUB, 2 * LANE), f32)
-        taps_grad_ref[(width + 1) * SUB :, lanes] += lax.fori_loop(0, tiles // 2, pair, zero, unroll=4)
+        taps_grad_ref[(width + 1) * SUB :, lanes] += lax.fori_loop(0, tiles // 2, pair, zero, unroll=8)
         return carry
 
     lax.fori_loop(0, inner // (2 * LANE), steps, 0)
     lane = lax.broadcasted_iota(jnp.int32, (block, LANE), 1)
-    rank = LANE - 2 * state
-    grads = jnp.dot(grad_pre_ref[...], step_back_ref[...], preferred_element_type=f32)
-    grads = jnp.where(
-        lane < state,
-        inject_grad_ref[...],
-        jnp.where(lane < 2 * state, pltpu.roll(readout_grad_ref[...], state, 1), grads),
+    across = (((1,), (1,)), ((), ()))
+    low_grad_ref[:, :rank] = lax.dot_general(
+        grad_pre_ref[...], step_back_ref[...], across, preferred_element_type=f32
     )
+    grads = low_grad_ref[...]
+    inject_grad = pltpu.roll(inject_grad_ref[...], rank, 1)
+    readout_grad = pltpu.roll(readout_grad_ref[...], rank + state, 1)
+    grads = jnp.where(lane < rank, grads, jnp.where(lane < rank + state, inject_grad, readout_grad))
+    grads = jnp.where(lane < rank + 2 * state, grads, 0.0)
     grads = grads.astype(bf16)
     grad_select_ref[...] = grads
+
+    through_ref[...] = lax.dot_general(
+        grad_select_ref[:, : rank + 2 * state], select_back_ref[...], across, preferred_element_type=f32
+    )
 
     def convs(c, carry):
         lanes = at(c * 2 * LANE, 2 * LANE)
         skip = skip_ref[:, lanes]
-        feeds = jnp.dot(grads, select_back_ref[:, lanes], preferred_element_type=f32)
-        through_ref[:, lanes] = feeds
 
         def conv(i, carry):
             here = at(i * SUB, SUB)
@@ -547,7 +560,7 @@
             return tuple(totals)
 
         zero = jnp.zeros((SUB, 2 * LANE), f32)
-        totals = lax.fori_loop(0, tiles // 2, tap, (zero,) * (width + 1), unroll=4)
+        totals = lax.fori_loop(0, tiles // 2, tap, (zero,) * (width + 1), unroll=8)
         for k in range(width + 1):
             taps_grad_ref[k * SUB : (k + 1) * SUB, lanes] += totals[k]
         return carry
@@ -603,6 +616,7 @@
         + [
             pltpu.VMEM((tiles * SUB, 2 * state * LANE), f32),
             pltpu.VMEM((halo + tiles * SUB, inner), f32),
+            pltpu.VMEM((tiles * SUB, LANE), f32),
         ],
         compiler_params=pltpu.CompilerParams(vmem_limit_bytes=VMEM_BYTES),
     )(stream, gating, grad_gated, *constants)
@@ -648,13 +662,12 @@
     )(step, drive, grad, sel, spots, rates, pre_decay, pre_state, entry, conv, gating, grad_gated, skip)
 
 
-def backward_call(step, drive, grad, sel, spots, rates, begin, prior, conv_sum, stream, readout_grad, step_back, select_back, taps, skip, flat, regions):
+def backward_call(step, drive, grad, sel, spots, rates, begin, prior, conv_sum, stream, readout_grad, step_back, select_back, taps, skip, flat, regions, rank):
     rows, inner = step.shape
     state = rates.shape[0] // SUB
     tiles, count = scan_shapes(rows, state, inner, 8)
     bits = regions.count.bit_length() - 1
     phases = regions.early_phases()
-    stride = 1
 
     def back(t):
         return (count - 1 - t, 0)
@@ -670,9 +683,9 @@
     def fixed(x):
         return pl.BlockSpec(x.shape, lambda t: (0, 0), pipeline_mode=pl.Buffered(1))
 
-    shape = (tiles, state, inner, 2, 4)
+    shape = (tiles, state, inner, 2, 4, rank)
     return pl.pallas_call(
-        functools.partial(backward_kernel, shape, count, regions, bits, phases, stride),
+        functools.partial(backward_kernel, shape, count, regions, bits, phases),
         name="scan_backward",
         grid=(count,),
         in_specs=[wide, wide, wide, thin, table, whole, whole]
@@ -705,6 +718,7 @@
             pltpu.VMEM((tiles * SUB, inner), f32),
             pltpu.VMEM((tiles * SUB + halo, inner), f32),
             pltpu.VMEM((tiles * SUB, LANE), f32),
+            pltpu.VMEM((tiles * SUB, LANE), f32),
         ]
         + Reducer.scratch(regions.depth, bits, phases),
         compiler_params=pltpu.CompilerParams(
@@ -727,31 +741,89 @@
     return tiles
 
 
-def product_kernel(steps, shapes, *refs):
-    out_ref, held_ref = refs[-2:]
+def pack_columns(src_ref, used, out_ref):
+    part = LANE - used
+    rows = src_ref.shape[0] // 4
+    lane = lax.broadcasted_iota(jnp.int32, (SUB, LANE), 1)
+    flat = out_ref
+
+    def one(g, carry):
+        quads = [src_ref[pl.ds(g * 4 * SUB + q, SUB, stride=4), :] for q in range(4)]
+        for m in range(3):
+            first = quads[m] if m == 0 else pltpu.roll(quads[m], LANE - m * part, 1)
+            second = pltpu.roll(quads[m + 1], used - m * part, 1)
+            flat[pl.ds(g * 3 * SUB + m, SUB, stride=3), :] = jnp.where(lane < used - m * part, first, second)
+        return carry
+
+    lax.fori_loop(0, rows // SUB, one, 0, unroll=4)
+
+
+def row_tile(src_ref, r, q):
+    return jnp.concatenate(
+        [src_ref[r : r + 1, (q * SUB + a) * LANE : (q * SUB + a + 1) * LANE] for a in range(SUB)], 0
+    )
+
+
+def product_kernel(steps, shapes, used, *refs):
+    if used:
+        out_ref, held_ref, packed_ref = refs[-3:]
+    else:
+        out_ref, held_ref = refs[-2:]
     contract = (((0,), (0,)), ((), ()))
+    step = pl.program_id(0)
+
+    def lay(src_ref, first, rows, base, per, q):
+        def one(r, carry):
+            tiles = [
+                src_ref[at(r * SUB, SUB), (first + a) * LANE : (first + a + 1) * LANE] for a in range(SUB)
+            ]
+            for b, tile in enumerate(turn_tiles(tiles)):
+                out_ref[base + (r * SUB + b) * per + q] = tile
+            return carry
+
+        lax.fori_loop(0, rows // SUB, one, 0, unroll=rows // SUB)
+
     for turn, (rows, width) in enumerate(shapes):
         left_ref, right_ref = refs[2 * turn : 2 * turn + 2]
         per = width // ROW
 
-        @pl.when(pl.program_id(0) // steps == turn)
+        @pl.when(step // steps == turn)
         def _():
             for q in range(per):
-                held_ref[:rows] = lax.dot_general(
+                held_ref[q, :rows] = lax.dot_general(
                     left_ref[...], right_ref[:, q * ROW : (q + 1) * ROW], contract, preferred_element_type=f32
                 )
-
-                def one(r, carry):
-                    tiles = [held_ref[at(r * SUB, SUB), a * LANE : (a + 1) * LANE] for a in range(SUB)]
-                    for b, tile in enumerate(turn_tiles(tiles)):
-                        out_ref[(r * SUB + b) * per + q] = tile
-                    return carry
-
-                lax.fori_loop(0, rows // SUB, one, 0, unroll=4)
-
-
-def product_call(*pairs):
-    steps = 8
+                lay(held_ref.at[q], 0, rows, 0, per, q)
+
+    if not used:
+        return
+    wide_ref, *thin_refs = refs[2 * len(shapes) : -3]
+    tiles = packed_ref.shape[0] // SUB
+
+    @pl.when(step == steps * len(shapes))
+    def _():
+        pack_columns(wide_ref, used, packed_ref)
+
+        def one(i, carry):
+            out_ref[i] = packed_ref[at(i * SUB, SUB), :]
+            return carry
+
+        out_ref[...] = jnp.zeros_like(out_ref)
+        lax.fori_loop(0, tiles, one, 0, unroll=8)
+        base = tiles
+        for ref in thin_refs:
+            rows, per = ref.shape[0], ref.shape[1] // ROW
+            for q in range(per):
+                if rows % SUB == 0:
+                    lay(ref, q * SUB, rows, base, per, q)
+                else:
+                    for r in range(rows):
+                        out_ref[base + r * per + q] = row_tile(ref, r, q)
+            base += rows * per
+
+
+def product_call(*pairs, small=None):
+    steps = 4
     shapes = [(left.shape[1] // steps, right.shape[1]) for left, right in pairs]
     size = shapes[0][0] * shapes[0][1] // ROW
 
@@ -762,20 +834,31 @@
     for k, (left, right) in enumerate(pairs):
         specs.append(pl.BlockSpec((left.shape[0], left.shape[1] // steps), block(k)))
         specs.append(pl.BlockSpec(right.shape, lambda t: (0, 0), pipeline_mode=pl.Buffered(1)))
+    args = [x for pair in pairs for x in pair]
+    scratch = [pltpu.VMEM((shapes[0][1] // ROW, max(rows for rows, _ in shapes), ROW), f32)]
+    used, extra = 0, 0
+    if small is not None:
+        wide, thin, used = small
+        extra = 1
+        scratch.append(pltpu.VMEM((wide.shape[0] * used // LANE, LANE), f32))
+        for x in (wide,) + thin:
+            specs.append(pl.BlockSpec(x.shape, lambda t: (0, 0), pipeline_mode=pl.Buffered(1)))
+            args.append(x)
+    grid = steps * len(pairs) + extra
     return pl.pallas_call(
-        functools.partial(product_kernel, steps, shapes),
+        functools.partial(product_kernel, steps, shapes, used),
         name="flat_product",
-        grid=(steps * len(pairs),),
+        grid=(grid,),
         in_specs=specs,
         out_specs=pl.BlockSpec((size, SUB, LANE), lambda t: (t, 0, 0)),
-        out_shape=jax.ShapeDtypeStruct((size * steps * len(pairs), SUB, LANE), f32),
-        scratch_shapes=[pltpu.VMEM((max(rows for rows, _ in shapes), ROW), f32)],
+        out_shape=jax.ShapeDtypeStruct((size * grid, SUB, LANE), f32),
+        scratch_shapes=scratch,
         compiler_params=pltpu.CompilerParams(vmem_limit_bytes=VMEM_BYTES),
-    )(*[x for pair in pairs for x in pair])
+    )(*args)
 
 
 class Regions:
-    def __init__(self, depth, count, span, gain, in_shape, small, out_shape):
+    def __init__(self, depth, count, span, gain, in_shape, small, out_shape, small_parts):
         self.depth, self.count, self.span = depth, count, span
         self.per = in_shape[1] // ROW
         self.in_rows = in_shape[0]
@@ -788,6 +871,10 @@
         self.half = self.lines * self.per // 2
         self.pieces = -(-self.need // self.half)
         self.slot = self.pieces * self.half
+        self.line_rows = min(-(-(self.lines + 15) // 16) * 16, self.in_rows)
+        self.slot_rows = min(-(-(self.slot + 15) // 16) * 16, self.out_rows)
+        self.small_parts = small_parts
+        self.small_tiles = sum(length for _, _, length in small_parts)
 
     def base(self, owner):
         return owner * self.span // ROW
@@ -821,17 +908,33 @@
         for z in range(self.depth):
             for piece in range((self.pieces if self.meets_out(z) else 1) * cut):
                 phases.append((z, piece * size, size))
-        return phases
+        return sorted(phases, key=lambda phase: -max(self.depth - 1 - phase[0], phase[0]))
 
     def late_phases(self):
         cut = 2 if self.half % 4 == 0 else 1
         size = self.half // cut
-        return [(z, piece * size, size) for z in range(self.depth) if self.meets_in(z) for piece in range(cut)]
+        owners = [k for k in range(self.depth * self.count) if self.meets_small(k)]
+        goals = {k // self.count for k in owners}
+        assert len(goals) == 1
+        goal = goals.pop()
+        small = [(goal, None, size)] * -(-self.small_tiles // (self.count * size))
+        stream = [(z, piece * size, size) for z in range(self.depth) if self.meets_in(z) for piece in range(cut)]
+        return small, stream, [k % self.count for k in owners]
+
+    def meets_small(self, owner):
+        base = self.base(owner)
+        return base < self.out_base and base + self.need > self.small_base
+
+    def late_start(self, phases, p, owner):
+        goal, offset, size = phases[p]
+        if offset is None:
+            return self.in_rows * self.per // 2 + (p * self.count + owner % self.count) * size
+        return self.in_first(owner) * (self.per // 2) + offset
 
 
 class Reducer:
-    def __init__(self, depth, bits, phases, stride, start, src_ref, refs):
-        self.depth, self.bits, self.phases, self.stride = depth, bits, phases, stride
+    def __init__(self, depth, bits, phases, gap, start, src_ref, refs):
+        self.depth, self.bits, self.phases = depth, bits, phases
         self.start, self.src = start, src_ref
         self.n = bits - 1
         self.half = phases[0][2] // 2
@@ -851,7 +954,11 @@
         self.mine = [(self.blk // 2**b) % 2 for b in range(bits)]
         self.partner = [self.blk + (1 - 2 * self.mine[b]) * 2**b for b in range(bits)]
         self.last = self.n + depth - 1
-        self.slots = stride * (len(phases) - 1) + self.last + 1
+        self.slot = [0] + [1 + 2 * s for s in range(self.n)]
+        self.slot += [max(2 * self.n, 1) + gap * u for u in range(depth - 1)]
+        self.done = self.slot[-1] + 1
+        hops = [max(depth - 1 - goal, goal) for goal, _, _ in phases]
+        self.slots = max(p + self.slot[self.n + h] + 1 for p, h in enumerate(hops))
 
     @staticmethod
     def scratch(depth, bits, phases):
@@ -862,19 +969,19 @@
             [pltpu.VMEM((count,) + (2,) * n + (size,) + tile, f32)] * 2
             + [pltpu.VMEM((count, 2) + (2,) * (n - 1 - s) + (size // 2,) + tile, f32) for s in range(n)]
             + [pltpu.VMEM((count, size) + tile, f32)] * 2
-            + [dma((count * 2**n,))] * 3
-            + [dma((max(count * n * 2, 1),))] * 2
+            + [dma((count,))] * 3
+            + [dma((max(count * n, 1),))] * 2
             + [dma((count,)), dma((2 * count,))]
         )
 
     def greet(self):
         barrier = pltpu.get_barrier_semaphore()
-        for other in self.partner:
-            pl.semaphore_signal(barrier, inc=1, device_id={"blk": other}, device_id_type=MESH)
-        for by in (1, self.depth - 1):
-            other = lax.rem(self.z + by, self.depth)
-            pl.semaphore_signal(barrier, inc=1, device_id={"batch": other}, device_id_type=MESH)
-        pl.semaphore_wait(barrier, self.bits + 2)
+        peers = ("blk", self.blk, 2**self.bits), ("batch", self.z, self.depth)
+        for axis, index, count in peers:
+            for by in range(1, count):
+                other = lax.rem(index + by, count)
+                pl.semaphore_signal(barrier, inc=1, device_id={axis: other}, device_id_type=MESH)
+        pl.semaphore_wait(barrier, 2**self.bits + self.depth - 2)
 
     def digits(self, r):
         return tuple((r // 2**i) % 2 for i in reversed(range(self.n)))
@@ -882,17 +989,16 @@
     def window(self, p, r, core):
         goal, offset, size = self.phases[p]
         owner = goal * 2**self.bits + 2 * r + core
-        return pl.ds(self.start(goal, owner) + offset, size)
+        return pl.ds(self.start(p, owner), size)
 
     def core_copies(self, p, own=False):
         copies = []
         for r in range(2**self.n):
-            spot = p * 2**self.n + r
             where = (p,) + self.digits(r)
             if own:
                 copies.append(
                     pltpu.make_async_copy(
-                        self.src.at[self.window(p, r, self.mine[0])], self.acc.at[where], self.local_sem.at[spot]
+                        self.src.at[self.window(p, r, self.mine[0])], self.acc.at[where], self.local_sem.at[p]
                     )
                 )
             else:
@@ -900,8 +1006,8 @@
                     pltpu.make_async_remote_copy(
                         src_ref=self.src.at[self.window(p, r, 1 - self.mine[0])],
                         dst_ref=self.first.at[where],
-                        send_sem=self.core_send.at[spot],
-                        recv_sem=self.core_recv.at[spot],
+                        send_sem=self.core_send.at[p],
+                        recv_sem=self.core_recv.at[p],
                         device_id={"blk": self.partner[0]},
                         device_id_type=MESH,
                     )
@@ -922,7 +1028,7 @@
         copies = []
         for part in range(2):
             i = self.order(part)[s]
-            spot = (p * self.n + s) * 2 + part
+            spot = p * self.n + s
             copies.append(
                 pltpu.make_async_remote_copy(
                     src_ref=self.acc.at[self.place(p, part, s, 1 - self.mine[i + 1])],
@@ -951,18 +1057,36 @@
     def add(self, dst, dst_at, src, src_at):
         dst[dst_at] += src[src_at]
 
+    def all_core(self, p):
+        return pltpu.make_async_remote_copy(
+            src_ref=self.first.at[p],
+            dst_ref=self.first.at[p],
+            send_sem=self.core_send.at[p],
+            recv_sem=self.core_recv.at[p],
+            device_id={"blk": self.partner[0]},
+            device_id_type=MESH,
+        )
+
+    def all_bit(self, p, s):
+        return pltpu.make_async_remote_copy(
+            src_ref=self.bit_recvs[s].at[p],
+            dst_ref=self.bit_recvs[s].at[p],
+            send_sem=self.bit_send.at[p * self.n + s],
+            recv_sem=self.bit_recv.at[p * self.n + s],
+            device_id={"blk": self.partner[0]},
+            device_id_type=MESH,
+        )
+
     def finish_core(self, p):
-        for copy in self.core_copies(p, True):
-            copy.wait()
-        for copy in self.core_copies(p):
-            copy.wait_recv()
+        pltpu.make_async_copy(self.first.at[p], self.acc.at[p], self.local_sem.at[p]).wait()
+        self.all_core(p).wait_recv()
         for r in range(2**self.n):
             where = (p,) + self.digits(r)
             self.add(self.acc, where, self.first, where)
 
     def finish_bit(self, p, s):
-        for part, copy in enumerate(self.bit_copies(p, s)):
-            copy.wait_recv()
+        self.all_bit(p, s).wait_recv()
+        for part in range(2):
             kept = self.place(p, part, s, self.mine[self.order(part)[s] + 1])
             free = [i for i in range(1, 1 + self.n) if isinstance(kept[i], slice)]
             for r in range(2 ** len(free)):
@@ -1010,27 +1134,29 @@
 
     def run(self, t):
         for stage in reversed(range(self.last + 1)):
-            p, odd = divmod(t - stage, self.stride)
-            if odd == 0 and 0 <= p < len(self.phases):
+            p = t - self.slot[stage]
+            if 0 <= p < len(self.phases):
                 self.act(p, stage)
 
-    def collect(self, out_ref):
-        for p, (goal, offset, size) in enumerate(self.phases):
+    def finish(self, p):
+        goal = self.phases[p][0]
+        if goal < self.depth - 1:
+            self.take(p, False)
+        if goal > 0:
+            self.take(p, True)
+
+    def collect(self, out_ref, first=0):
+        for p, (goal, offset, size) in list(enumerate(self.phases))[first:]:
 
             @pl.when(self.z == goal)
             def _():
-                if goal < self.depth - 1:
-                    self.take(p, False)
-                if goal > 0:
-                    self.take(p, True)
+                self.finish(p)
                 out_ref[offset : offset + size] = self.acc[self.settled(p)]
 
         for p in range(len(self.phases)):
-            for copy in self.core_copies(p):
-                copy.wait_send()
+            self.all_core(p).wait_send()
             for s in range(self.n):
-                for copy in self.bit_copies(p, s):
-                    copy.wait_send()
+                self.all_bit(p, s).wait_send()
             for u in range(self.depth - 1):
                 for mover, up in self.z_moves(p, u):
 
@@ -1055,7 +1181,9 @@
 def late_kernel(
     regions,
     bits,
-    phases,
+    small_phases,
+    stream_phases,
+    targets,
     blocks,
     flat_ref,
     early_ref,
@@ -1063,27 +1191,160 @@
     *refs,
 ):
     depth, span = regions.depth, regions.span
-    sources, refs = refs[:7], refs[7:]
-    window_ref, totals_ref, result_ref, grad_ref = refs[:4]
-    held, refs = refs[4:11], refs[11:]
+    sources, weights, refs = refs[:7], refs[7:14], refs[14:]
+    window_ref, totals_ref, result_ref, grad_ref, params_ref = refs[:5]
+    held, refs = refs[5:12], refs[12:]
     gate_back, stream_back, in_w, token, cot, gated, out_w = held
-    late_ref, turn_ref, gain_sum, sums, ring, load_sem, ring_send, ring_recv = refs[:8]
-    work = Reducer(depth, bits, phases, 1, lambda z, owner: regions.in_first(owner) * (regions.per // 2), flat_ref, refs[8:])
+    late_ref, small_ref, wide_window, turn_ref, gain_sum, sums, ring = refs[:7]
+    columns_ref, packed_ref, small_params = refs[7:10]
+    load_sem, ring_send, ring_recv, small_send, small_recv = refs[10:15]
+    phases = small_phases + stream_phases
+    few = len(small_phases)
+    work = Reducer(
+        depth, bits, phases, 2, lambda p, owner: regions.late_start(phases, p, owner), flat_ref, refs[15:]
+    )
     blk, z = work.blk, work.z
-    inner = gated.shape[1]
-    loads = [pltpu.make_async_copy(src, dst, load_sem.at[i]) for i, (src, dst) in enumerate(zip(sources, held))]
-    for load in loads:
+    inner = gated.shape[2]
+    size = token.shape[0] // blocks
+    loads = [
+        pltpu.make_async_copy(src, dst, load_sem.at[i])
+        for i, (src, dst) in enumerate(zip(sources, held))
+        if src.shape == dst.shape
+    ]
+
+    def pieces(t):
+        here = pl.ds(pl.multiple_of(t * size, size), size)
+        return [
+            pltpu.make_async_copy(src.at[here], dst.at[t % 2], load_sem.at[len(held) + 2 * i + t % 2])
+            for i, (src, dst) in enumerate(zip(sources, held))
+            if src.shape != dst.shape
+        ]
+
+    for load in loads + pieces(0):
         load.start()
     work.greet()
     gain_sum[...] = jnp.zeros_like(gain_sum)
-    size = token.shape[0] // blocks
     across = (((1,), (1,)), ((), ()))
+
+    goal = small_phases[0][0]
+    owner = z * 2**bits + blk
+    base = regions.base(owner)
+    margin = (wide_window.shape[0] - regions.need) // 2
+
+    def spread_rows(src_ref, first, rows, put):
+        per = src_ref.shape[1] // ROW
+
+        def one(r, carry):
+            here = pl.ds(pl.multiple_of(first + r * 2 * SUB, 2 * SUB), 2 * SUB)
+            for q in range(per):
+                both = src_ref[here, q * ROW : (q + 1) * ROW].astype(f32)
+                for side in range(2):
+                    half = both[side * SUB : (side + 1) * SUB]
+                    tiles = turn_tiles([half[:, a * LANE : (a + 1) * LANE] for a in range(SUB)])
+                    for b, tile in enumerate(tiles):
+                        put((first + r * 2 * SUB + side * SUB + b) * per + q, tile)
+            return carry
+
+        lax.fori_loop(0, rows // (2 * SUB), one, 0)
+
+    def lay_params():
+        conv_w, conv_b, select_w, step_w, step_b, rate, skip = weights
+        used = select_w.shape[1]
+        part = columns_ref.shape[0]
+        for c in range(select_w.shape[0] // part):
+            columns_ref[:, :used] = select_w[c * part : (c + 1) * part].astype(f32)
+            pack_columns(columns_ref, used, packed_ref.at[c * part * used // LANE : (c + 1) * part * used // LANE])
+        spot = 0
+        for ref in (conv_w, conv_b, select_w, step_w, step_b, rate, skip):
+            count = ref.shape[0] * ref.shape[1] // ROW
+            if ref is select_w:
+
+                def one(i, carry, spot=spot):
+                    small_params[spot + i] = packed_ref[at(i * SUB, SUB), :]
+                    return carry
+
+                lax.fori_loop(0, count, one, 0, unroll=8)
+            elif ref is step_w:
+
+                def put(i, tile, spot=spot):
+                    small_params[spot + i] = tile
+
+                spread_rows(step_w, 0, step_w.shape[0], put)
+            else:
+                per = ref.shape[1] // ROW
+                for i in range(count):
+                    small_params[spot + i] = row_tile(ref, i // per, i % per)
+            spot += count
+
+    def place_params():
+        params_ref[...] = jnp.zeros_like(params_ref)
+        wide_window[...] = jnp.zeros_like(wide_window)
+
+        @pl.when(base < regions.small_base)
+        def _():
+            first = regions.in_first(owner) // (2 * SUB) * (2 * SUB)
+            first = lax.min(first, regions.in_rows - regions.line_rows)
+
+            def put(i, tile):
+                wide_window[regions.in_base + i - base + margin] = tile
+
+            spread_rows(in_w, first, regions.line_rows, put)
+
+        @pl.when(base >= regions.small_base)
+        def _():
+            first = regions.out_first(owner) // (2 * SUB) * (2 * SUB)
+            first = lax.min(first, regions.out_rows - regions.slot_rows)
+
+            def put(i, tile):
+                wide_window[regions.out_base + i - base + margin] = tile
+
+            spread_rows(out_w, first, regions.slot_rows, put)
+
+        @pl.when((base < regions.out_base) & (base + regions.need > regions.small_base))
+        def _():
+            def line(i, carry):
+                row = base + i
+                tile = lax.max(lax.min(row - regions.small_base, small_params.shape[0] - 1), 0)
+                here = (row >= regions.small_base) & (row < regions.out_base)
+                wide_window[margin + i] = jnp.where(here, small_params[tile], wide_window[margin + i])
+                return carry
+
+            lax.fori_loop(0, regions.need, line, 0, unroll=2)
+
+        params_ref[...] = wide_window[margin : margin + regions.need]
+
+        @pl.when(base < regions.in_base)
+        def _():
+            params_ref[0] = row_tile(gain_ref, 0, 0)
+
+    def hand_out(p, target):
+        return pltpu.make_async_remote_copy(
+            src_ref=small_ref.at[p, blk],
+            dst_ref=small_ref.at[p, blk],
+            send_sem=small_send.at[p, targets.index(target)],
+            recv_sem=small_recv.at[p, blk],
+            device_id={"blk": target},
+            device_id_type=MESH,
+        )
+
+    def give_small(p):
+        @pl.when(z == goal)
+        def _():
+            work.finish(p)
+            small_ref[p, blk] = work.acc[work.settled(p)]
+            for target in targets:
+
+                @pl.when(blk != target)
+                def _():
+                    hand_out(p, target).start()
 
     def slot(t, carry):
         for k in range(work.slots):
 
             @pl.when(t == k)
             def _():
+                if 0 <= k - work.done < few:
+                    give_small(k - work.done)
                 work.run(k)
                 if k == 0:
                     for load in loads:
@@ -1092,122 +1353,150 @@
         @pl.when(t < blocks)
         def _():
             here = pl.ds(pl.multiple_of(t * size, size), size)
+            part = t % 2
+            for piece in pieces(t):
+                piece.wait()
+
+            @pl.when(t + 1 < blocks)
+            def _():
+                for piece in pieces(t + 1):
+                    piece.start()
+
             source = token[here, :].astype(f32)
-            output = jnp.dot(gated[here, :], out_w[...], preferred_element_type=f32)
+            output = jnp.dot(gated[part], out_w[...], preferred_element_type=f32)
             put_restored(source + output, turn_ref, result_ref, t)
             grad_normed = lax.dot_general(
-                stream_back[here, :], in_w[:, :inner], across, preferred_element_type=f32
-            ) + lax.dot_general(gate_back[here, :], in_w[:, inner:], across, preferred_element_type=f32)
+                stream_back[part], in_w[:, :inner], across, preferred_element_type=f32
+            ) + lax.dot_general(gate_back[part], in_w[:, inner:], across, preferred_element_type=f32)
             scale = lax.rsqrt(jnp.mean(source * source, axis=-1, keepdims=True) + EPS)
             scaled = source * scale
-            part = grad_normed * scaled
-            gain_sum[...] += jnp.sum(part.reshape(size // SUB, SUB, part.shape[1]), 0)
+            product = grad_normed * scaled
+            gain_sum[...] += jnp.sum(product.reshape(size // SUB, SUB, product.shape[1]), 0)
             weighted = grad_normed * gain_ref[...]
             mean = jnp.mean(weighted * source, axis=-1, keepdims=True)
             back = scale * weighted - source * (scale * scale * scale) * mean + cot[here, :].astype(f32)
             put_restored(back, turn_ref, grad_ref, t)
 
+        @pl.when(t == blocks)
+        def _():
+            lay_params()
+
+        @pl.when(t == blocks + 1)
+        def _():
+            place_params()
+
         return carry
 
-    lax.fori_loop(0, max(work.slots, blocks), slot, 0)
+    lax.fori_loop(0, max(work.slots, blocks + 2), slot, 0)
+    for p in range(few):
+        if p + work.done >= work.slots:
+            give_small(p)
     late_ref[...] = jnp.zeros_like(late_ref)
-    work.collect(late_ref)
-
-    owner = z * 2**bits + blk
-    base = regions.base(owner)
+    work.collect(late_ref, few)
+    for target in targets:
+        for p in range(few):
+
+            @pl.when((z == goal) & (blk != target))
+            def _():
+                hand_out(p, target).wait_send()
+
+            for source in range(2**bits):
+                if source != target:
+
+                    @pl.when((z == goal) & (blk == target))
+                    def _():
+                        pltpu.make_async_remote_copy(
+                            src_ref=small_ref.at[p, source],
+                            dst_ref=small_ref.at[p, source],
+                            send_sem=small_send.at[p, 0],
+                            recv_sem=small_recv.at[p, source],
+                            device_id={"blk": source},
+                            device_id_type=MESH,
+                        ).wait_recv()
+
     inside = lax.broadcasted_iota(jnp.int32, (SUB, LANE), 0) * LANE + lax.broadcasted_iota(
         jnp.int32, (SUB, LANE), 1
     )
-    sums[0, 0] = jnp.zeros((SUB, LANE), f32)
+    sums[blk, 0] = jnp.zeros((SUB, LANE), f32)
     gain = jnp.sum(gain_sum[...], 0, keepdims=True)
     for a in range(SUB):
-        sums[0, 1, a : a + 1, :] = gain[:, a * LANE : (a + 1) * LANE]
+        sums[blk, 1, a : a + 1, :] = gain[:, a * LANE : (a + 1) * LANE]
     half = regions.per // 2
-    window_ref[...] = jnp.zeros_like(window_ref)
-
-    def keep(value, row):
-        place = row - base
-
-        @pl.when((place >= 0) & (place < regions.need))
-        def _():
-            spot = inside + (row * ROW - owner * span)
-            own = jnp.where((spot >= 0) & (spot < span), value, 0.0)
-            sums[0, 0] += own * own
-            window_ref[place] = value
+    wide_window[...] = jnp.zeros_like(wide_window)
+
+    def own(value, row):
+        spot = inside + (row * ROW - owner * span)
+        return jnp.where((spot >= 0) & (spot < span), value, 0.0)
+
+    def keep(total, value, row):
+        wide_window[row - base + margin] = value
+        part = own(value, row)
+        return total + part * part
+
+    zero = jnp.zeros((SUB, LANE), f32)
 
     @pl.when(base < regions.small_base)
     def _():
-        def line(d, carry):
+        def line(d, total):
             row = regions.in_base + (regions.in_first(owner) + d) * regions.per
             for q in range(half):
-                keep(late_ref[d * half + q], row + q)
-                keep(early_ref[d * half + q], row + half + q)
-            return carry
-
-        lax.fori_loop(0, regions.lines, line, 0)
+                total = keep(total, late_ref[d * half + q], row + q)
+                total = keep(total, early_ref[d * half + q], row + half + q)
+            return total
+
+        sums[blk, 0] += lax.fori_loop(0, regions.lines, line, zero, unroll=2)
 
     @pl.when(base >= regions.small_base)
     def _():
-        def line(i, carry):
-            keep(early_ref[i], regions.out_base + regions.out_first(owner) + i)
-            return carry
-
-        lax.fori_loop(0, regions.slot, line, 0)
-
-    for b in range(bits):
-        copy = pltpu.make_async_remote_copy(
-            src_ref=sums.at[b],
-            dst_ref=sums.at[bits + 1 + b],
-            send_sem=ring_send.at[b],
-            recv_sem=ring_recv.at[b],
-            device_id={"blk": work.partner[b]},
-            device_id_type=MESH,
-        )
-        copy.start()
-        copy.wait()
-        sums[b + 1] = sums[b] + sums[bits + 1 + b]
-    ring[z] = sums[bits]
-    for u in range(depth - 1):
-        moves = (
-            ((z + u < depth) & (z > 0), lax.min(z + u, depth - 1), depth - 1, 0),
-            ((z - u >= 0) & (z < depth - 1), lax.max(z - u, 0), 1, 1),
-        )
-        gets = (
-            ((z < depth - 1) & (z + 1 + u < depth), lax.min(z + 1 + u, depth - 1), depth - 1, 0),
-            ((z > 0) & (z - 1 - u >= 0), lax.max(z - 1 - u, 0), 1, 1),
-        )
-
-        def hop(origin, by, way):
-            return pltpu.make_async_remote_copy(
-                src_ref=ring.at[origin],
-                dst_ref=ring.at[origin],
-                send_sem=ring_send.at[bits + u * 2 + way],
-                recv_sem=ring_recv.at[bits + u * 2 + way],
-                device_id={"batch": lax.rem(z + by, depth)},
+        def line(i, total):
+            return keep(total, early_ref[i], regions.out_base + regions.out_first(owner) + i)
+
+        sums[blk, 0] += lax.fori_loop(0, regions.slot, line, zero, unroll=4)
+
+    size = small_phases[0][2]
+
+    @pl.when((base < regions.out_base) & (base + regions.need > regions.small_base))
+    def _():
+        def line(i, total):
+            row = base + i
+            tile = 0
+            for first, spot, length in regions.small_parts:
+                offset = row - regions.small_base - first
+                tile = jnp.where(offset >= 0, spot + lax.min(offset, length - 1), tile)
+            lot = tile // size
+            value = small_ref[lot // 2**bits, lot % 2**bits, tile % size]
+            here = (row >= regions.small_base) & (row < regions.out_base)
+            wide_window[margin + i] = jnp.where(here, value, wide_window[margin + i])
+            part = jnp.where(here, own(value, row), 0.0)
+            return total + part * part
+
+        sums[blk, 0] += lax.fori_loop(0, regions.need, line, zero, unroll=2)
+
+    window_ref[...] = wide_window[margin : margin + regions.need]
+
+    def everyone(slots, axis, index, count, first_sem):
+        copies = [
+            pltpu.make_async_remote_copy(
+                src_ref=slots.at[index],
+                dst_ref=slots.at[index],
+                send_sem=ring_send.at[first_sem + by],
+                recv_sem=ring_recv.at[first_sem + by],
+                device_id={axis: lax.rem(index + by, count)},
                 device_id_type=MESH,
             )
-
-        for cond, origin, by, way in moves:
-
-            @pl.when(cond)
-            def _():
-                hop(origin, by, way).start()
-
-        for cond, origin, by, way in gets:
-
-            @pl.when(cond)
-            def _():
-                hop(origin, by, way).wait_recv()
-
-        for cond, origin, by, way in moves:
-
-            @pl.when(cond)
-            def _():
-                hop(origin, by, way).wait_send()
-
-    total = ring[0]
-    for zz in range(1, depth):
-        total = total + ring[zz]
+            for by in range(1, count)
+        ]
+        for copy in copies:
+            copy.start()
+        for copy in copies:
+            copy.wait()
+        total = slots[0]
+        for k in range(1, count):
+            total = total + slots[k]
+        return total
+
+    ring[z] = everyone(sums, "blk", blk, 2**bits, 0)
+    total = everyone(ring, "batch", z, depth, 2**bits)
     totals_ref[...] = total
 
     @pl.when(base < regions.in_base)
@@ -1215,82 +1504,138 @@
         window_ref[0] = total[1]
 
 
-def late_call(flat, early, gain, sources, regions):
+def late_call(flat, early, gain, sources, weights, regions):
     bits = regions.count.bit_length() - 1
     depth = regions.depth
-    phases = regions.late_phases()
+    small_phases, stream_phases, targets = regions.late_phases()
+    phases = small_phases + stream_phases
+    few, size = len(small_phases), phases[0][2]
+    margin = max(regions.slot_rows, regions.line_rows * regions.per) + SUB
+    wide, used = weights[2].shape
+    small_count = sum(x.size for x in weights) // ROW
     tile = (SUB, LANE)
     dma = pltpu.SemaphoreType.DMA
-    hops = bits + 2 * (depth - 1)
+    hops = 2**bits + depth
     vmem = pl.BlockSpec(memory_space=pltpu.VMEM)
     far = pl.BlockSpec(memory_space=pl.ANY)
     rows, model = sources[3].shape
     blocks = 8
     return pl.pallas_call(
-        functools.partial(late_kernel, regions, bits, phases, blocks),
+        functools.partial(late_kernel, regions, bits, small_phases, stream_phases, targets, blocks),
         name="reduce_late",
-        in_specs=[far, vmem, vmem] + [far] * len(sources),
-        out_specs=[vmem] * 4,
+        in_specs=[far, vmem, vmem] + [far] * len(sources) + [vmem] * len(weights),
+        out_specs=[vmem] * 5,
         out_shape=[
             jax.ShapeDtypeStruct((regions.need,) + tile, f32),
             jax.ShapeDtypeStruct((2,) + tile, f32),
             jax.ShapeDtypeStruct((rows, model), bf16),
             jax.ShapeDtypeStruct((rows, model), bf16),
+            jax.ShapeDtypeStruct((regions.need,) + tile, f32),
         ],
-        scratch_shapes=[pltpu.VMEM(x.shape, x.dtype) for x in sources]
+        scratch_shapes=[
+            pltpu.VMEM((2, rows // blocks, x.shape[1]) if n in (0, 1, 5) else x.shape, x.dtype)
+            for n, x in enumerate(sources)
+        ]
         + [
             pltpu.VMEM((regions.half,) + tile, f32),
+            pltpu.VMEM((few, 2**bits, size) + tile, f32),
+            pltpu.VMEM((regions.need + 2 * margin,) + tile, f32),
             pltpu.VMEM((model // LANE, rows // blocks, LANE), f32),
             pltpu.VMEM((SUB, model), f32),
-            pltpu.VMEM((2 * bits + 1, 2) + tile, f32),
+            pltpu.VMEM((2**bits, 2) + tile, f32),
             pltpu.VMEM((depth, 2) + tile, f32),
-            dma((len(sources),)),
+            pltpu.VMEM((wide // blocks, LANE), f32),
+            pltpu.VMEM((wide * used // LANE, LANE), f32),
+            pltpu.VMEM((small_count,) + tile, f32),
+            dma((3 * len(sources),)),
             dma((hops,)),
             dma((hops,)),
+            dma((few, len(targets))),
+            dma((few, 2**bits)),
         ]
         + Reducer.scratch(depth, bits, phases),
         compiler_params=pltpu.CompilerParams(
             vmem_limit_bytes=62 * 2**20, collective_id=1, has_side_effects=True
         ),
-    )(flat, early, gain, *sources)
-
-
-def share(regions, gain, in_part, small, out_part, owner):
-    base, high = regions.base(owner), regions.need
-    place = (base + lax.iota(jnp.int32, high))[:, None, None]
-    total = jnp.broadcast_to(gain, (high, SUB, LANE))
-    for part, origin, low in (
-        (in_part, regions.in_base + regions.in_first(owner) * regions.per, regions.in_base),
-        (small, regions.small_base, regions.small_base),
-        (out_part, regions.out_base + regions.out_first(owner), regions.out_base),
-    ):
-        padded = jnp.pad(part, ((high, high), (0, 0), (0, 0)))
-        offset = jnp.clip(base - origin + high, 0, part.shape[0] + high)
-        total = jnp.where(place >= low, lax.dynamic_slice_in_dim(padded, offset, high), total)
-    return lax.dynamic_slice_in_dim(total.reshape(-1), owner * regions.span % ROW, regions.span)
+    )(flat, early, gain, *sources, *weights)
+
+
+def exchange_kernel(bits, state, totals_ref, entry_ref, arriving_ref, here, far, pre, post, send_sem, recv_sem):
+    blk = lax.axis_index("blk")
+    mine = [(blk // 2**b) % 2 for b in range(bits)]
+    partner = [blk + (1 - 2 * mine[b]) * 2**b for b in range(bits)]
+    barrier = pltpu.get_barrier_semaphore()
+    for other in partner:
+        pl.semaphore_signal(barrier, inc=1, device_id={"blk": other}, device_id_type=MESH)
+    pl.semaphore_wait(barrier, bits)
+    first, second, third = (slice(k * state, (k + 1) * state) for k in range(3))
+    here[0] = totals_ref[...]
+    entry_ref[...] = jnp.zeros_like(entry_ref)
+    arriving_ref[...] = jnp.zeros_like(arriving_ref)
+    pre[...] = jnp.ones_like(pre)
+    post[...] = jnp.ones_like(post)
+    for b in range(bits):
+        if b < bits - 1:
+            src, dst = here.at[b], far.at[b]
+        else:
+            src = here.at[b, pl.ds(pl.multiple_of((1 + mine[b]) * state, state), state)]
+            dst = far.at[b, first]
+        copy = pltpu.make_async_remote_copy(
+            src_ref=src,
+            dst_ref=dst,
+            send_sem=send_sem.at[b],
+            recv_sem=recv_sem.at[b],
+            device_id={"blk": partner[b]},
+            device_id_type=MESH,
+        )
+        copy.start()
+        copy.wait()
+        if b == bits - 1:
+
+            @pl.when(mine[b] == 1)
+            def _():
+                entry_ref[...] += pre[...] * far[b, first]
+
+            @pl.when(mine[b] == 0)
+            def _():
+                arriving_ref[...] += post[...] * far[b, first]
+
+            continue
+
+        @pl.when(mine[b] == 1)
+        def _():
+            entry_ref[...] += pre[...] * far[b, second]
+            pre[...] *= far[b, first]
+            here[b + 1, second] = here[b, second] + here[b, first] * far[b, second]
+            here[b + 1, third] = far[b, third] + far[b, first] * here[b, third]
+
+        @pl.when(mine[b] == 0)
+        def _():
+            arriving_ref[...] += post[...] * far[b, third]
+            post[...] *= far[b, first]
+            here[b + 1, second] = far[b, second] + far[b, first] * here[b, second]
+            here[b + 1, third] = here[b, third] + here[b, first] * far[b, third]
+
+        here[b + 1, first] = here[b, first] * far[b, first]
 
 
 def exchange(totals, state):
-    count = lax.axis_size("blk")
-    index = lax.axis_index("blk")
-    decay, end, leave = totals[:state], totals[state : 2 * state], totals[2 * state :]
-    pre_decay, pre_state = jnp.ones_like(decay), jnp.zeros_like(end)
-    post_decay, post_state = jnp.ones_like(decay), jnp.zeros_like(end)
-    bit = 1
-    while bit < count:
-        pairs = [(i, i ^ bit) for i in range(count)]
-        far = lax.ppermute(jnp.concatenate([decay, end, leave], 0), "blk", pairs)
-        far_decay, far_end, far_leave = far[:state], far[state : 2 * state], far[2 * state :]
-        upper = (index & bit) != 0
-        pre_state = jnp.where(upper, pre_state + pre_decay * far_end, pre_state)
-        pre_decay = jnp.where(upper, pre_decay * far_decay, pre_decay)
-        post_state = jnp.where(upper, post_state, post_state + post_decay * far_leave)
-        post_decay = jnp.where(upper, post_decay, post_decay * far_decay)
-        end = jnp.where(upper, end + decay * far_end, far_end + far_decay * end)
-        leave = jnp.where(upper, far_leave + far_decay * leave, leave + decay * far_leave)
-        decay = decay * far_decay
-        bit *= 2
-    return pre_state, post_state
+    bits = lax.axis_size("blk").bit_length() - 1
+    rows, inner = totals.shape
+    vmem = pl.BlockSpec(memory_space=pltpu.VMEM)
+    return pl.pallas_call(
+        functools.partial(exchange_kernel, bits, state),
+        name="exchange",
+        in_specs=[vmem],
+        out_specs=[vmem] * 2,
+        out_shape=[jax.ShapeDtypeStruct((state, inner), f32)] * 2,
+        scratch_shapes=[pltpu.VMEM((bits, rows, inner), f32)] * 2
+        + [pltpu.VMEM((state, inner), f32)] * 2
+        + [pltpu.SemaphoreType.DMA((bits,))] * 2,
+        compiler_params=pltpu.CompilerParams(
+            vmem_limit_bytes=VMEM_BYTES, collective_id=3, has_side_effects=True
+        ),
+    )(totals)
 
 
 def local(
@@ -1331,9 +1676,6 @@
     rates = -jnp.exp(a_log)
     rates_wide = jnp.repeat(rates * LOG2E, SUB, axis=0)
     spots = spread_table(2 * state)
-    spare = LANE - rank - 2 * state
-    select_in = jnp.pad(jnp.roll(xproj_weight, 2 * state, 1), ((0, 0), (0, spare)))
-    step_in = jnp.pad(dt_weight, ((2 * state, spare), (0, 0)))
     (
         conv_sum,
         conv_low,
@@ -1354,8 +1696,8 @@
         head,
         conv_weight,
         conv_bias[None],
-        select_in,
-        step_in,
+        xproj_weight,
+        dt_weight,
         dt_bias[None],
         spots,
         rates_wide,
@@ -1382,6 +1724,10 @@
     small_rows = sum(
         value.size for value in (conv_weight, conv_bias, xproj_weight, dt_weight, dt_bias, a_log, d_skip)
     ) // ROW
+    lead = (conv_weight.size + conv_bias.size) // ROW
+    packed = xproj_weight.size // ROW
+    rest = small_rows - lead - packed
+    small_parts = ((0, packed, lead), (lead, 0, packed), (lead + packed, packed + lead, rest))
     regions = Regions(
         lax.axis_size("batch"),
         lax.axis_size("blk"),
@@ -1390,10 +1736,9 @@
         in_weight.shape,
         small_rows,
         out_weight.shape,
+        small_parts,
     )
     flat_early = product_call((normed, grad_gating), (gated, cot_low))
-    step_back = step_in.T
-    select_back = select_in.T
     grad_stream_low, grad_pre_low, grad_selectors, rate_grads, taps_grads, edges, early = backward_call(
         step_size,
         drive,
@@ -1406,20 +1751,19 @@
         conv_sum,
         stream,
         readout_grads,
-        step_back,
-        select_back,
+        dt_weight,
+        xproj_weight,
         conv_weight,
         d_skip[None],
         flat_early,
         regions,
+        rank,
     )
     grad_a_log = LN2 * jnp.sum(rate_grads.reshape(state, SUB, inner), 1)
     begins = edges[:halo].reshape(width - 1, SUB, inner)
     ahead = shifted(begins[:, 0], "blk", -1)
-    grad_dt_weight = lax.dot_general(sel_low, grad_pre_low, contract, preferred_element_type=f32)[
-        2 * state : 2 * state + rank
-    ]
-    grad_xproj = lax.dot_general(grad_selectors, conv_low, contract, preferred_element_type=f32)
+    grad_dt_weight = lax.dot_general(sel_low, grad_pre_low, contract, preferred_element_type=f32)[:rank]
+    grad_xproj = lax.dot_general(conv_low, grad_selectors, contract, preferred_element_type=f32)
     foot = jnp.concatenate([begins[:, 1:], ahead[:, None]], 1)
     lasts = edges[halo:].reshape(width - 1, SUB, inner)
     further = jnp.concatenate([lasts, foot], 0)
@@ -1439,51 +1783,21 @@
     grad_stream_low = lax.dynamic_update_slice_in_dim(
         grad_stream_low, grad_last.reshape(halo, inner).astype(bf16), length - halo, 0
     )
-    thin = (grad_xproj, grad_dt_weight, grad_a_log, grad_conv_weight, grad_conv_bias, grad_dt_bias, grad_d_skip)
-    thin = jnp.concatenate([value.reshape(-1, inner) for value in thin], 0)
-    grad_stream_low, thin = lax.optimization_barrier((grad_stream_low, thin))
-    thin = lax.psum(jnp.pad(thin, ((0, -thin.shape[0] % SUB), (0, 0))), ("batch", "blk"))
-    parts = []
-    for value in (LANE, rank, state, width, 1, 1, 1):
-        start = sum(part.shape[0] for part in parts)
-        parts.append(thin[start : start + value])
-    used = rank + 2 * state
-    xproj = jnp.roll(parts[0][:used], rank, 0).T
-    order = (parts[3], parts[4], xproj, parts[1], parts[5], parts[2], parts[6])
-    small = jnp.concatenate([value.reshape(-1, ROW) for value in order], 0)
-    window, totals, result, grad_tokens = late_call(
-        product_call((normed, grad_stream_low)),
+    thin = (grad_conv_weight, grad_conv_bias[None], grad_dt_weight, grad_dt_bias[None], grad_a_log, grad_d_skip[None])
+    window, totals, result, grad_tokens, owned = late_call(
+        product_call((normed, grad_stream_low), small=(grad_xproj, thin, rank + 2 * state)),
         early,
         norm_gain[None],
         (grad_gating, grad_stream_low, in_weight, token_rows, cot_low, gated, out_weight),
+        (conv_weight, conv_bias[None], xproj_weight, dt_weight, dt_bias[None], a_log, d_skip[None]),
         regions,
     )
     result, grad_tokens = result[None], grad_tokens[None]
-    grad_norm = jnp.sqrt(jnp.sum(totals[0]) + jnp.sum(totals[1] * totals[1]) + jnp.sum(small * small))
+    grad_norm = jnp.sqrt(jnp.sum(totals[0]) + jnp.sum(totals[1] * totals[1]))
     owner = lax.axis_index(("batch", "blk"))
     begin = owner * span
-    base, high = regions.base(owner), regions.need
-    place = (base + lax.iota(jnp.int32, high))[:, None, None]
-    padded = jnp.pad(small.reshape(-1, SUB, LANE), ((high, high), (0, 0), (0, 0)))
-    offset = jnp.clip(base - regions.small_base + high, 0, small_rows + high)
-    window = jnp.where(
-        (place >= regions.small_base) & (place < regions.out_base),
-        lax.dynamic_slice_in_dim(padded, offset, high),
-        window,
-    )
     shard = lax.dynamic_slice_in_dim(window.reshape(-1), begin % ROW, span)
-    in_part = lax.dynamic_slice_in_dim(in_weight, regions.in_first(owner), regions.lines)
-    out_part = lax.dynamic_slice_in_dim(out_weight, regions.out_first(owner), regions.slot)
-    small_params = (conv_weight, conv_bias, xproj_weight, dt_weight, dt_bias, a_log, d_skip)
-    small_params = jnp.concatenate([value.reshape(-1, ROW).astype(f32) for value in small_params], 0)
-    owned = share(
-        regions,
-        norm_gain.reshape(-1, SUB, LANE),
-        in_part.astype(f32).reshape(-1, SUB, LANE),
-        small_params.reshape(-1, SUB, LANE),
-        out_part.astype(f32).reshape(-1, SUB, LANE),
-        owner,
-    )
+    owned = lax.dynamic_slice_in_dim(owned.reshape(-1), begin % ROW, span)
     lower = norm_gain.size + in_weight.size + sum(
         value.size for value in (conv_weight, conv_bias, xproj_weight, dt_weight)
     )

time: 612 us -> 497 us (0.81)
  local copies, waits for them, and re-layouts: 54.8 us -> 11.3 us
  waiting for transfers between devices: 26.4 us -> 0.01 us
  Pallas kernels: 440 us -> 423 us
  between operations: 18.4 us -> 3.98 us
  other arithmetic: 28.8 us -> 21.8 us
    pallas_call x1, Pallas kernels: 90.4 us -> 74.2 us  [summary_call(): pl.pallas_call(functools.partial(summary_kernel, shape), name='scan_summa...]
    unnamed x118 -> x49, local copies, waits for them, and re-layouts: 19.8 us -> 3.78 us
    ppermute x3 -> x0, waiting for transfers between devices: 13.3 us -> none  [exchange(): far = lax.ppermute(jnp.concatenate([decay, end, leave], 0), 'blk', pairs)]
    psum x1 -> x0, waiting for transfers between devices: 13.1 us -> none  [local(): lax.psum(jnp.pad(thin, ((0, -thin.shape[0] % SUB), (0, 0))), ('batch', 'b...]
    pallas_call x3 -> x4, Pallas kernels: 137 us -> 149 us  [the longest x1 97 us: late_call(): pl.pallas_call(functools.partial(late_kernel, regions, bits, small_phases...]
    concatenate x10 -> x0, local copies, waits for them, and re-layouts: 10.2 us -> none  [the longest x6 6.71 us: local(): small = jnp.concatenate([value.reshape(-1, ROW) for value in order], 0)]
    pallas_call x1, Pallas kernels: 141 us -> 133 us  [backward_call(): pl.pallas_call(functools.partial(backward_kernel, shape, count, regions,...]
    reshape x9 -> x0, local copies, waits for them, and re-layouts: 7.91 us -> none  [the longest x1 4.31 us: interleave(): x.reshape(SUB, rows // SUB, width).transpose(1, 0, 2).reshape(rows, width)]
  transfers between devices with their start and end apart: 6 -> 2, of which waited for: 3 -> 0; matrix products, arithmetic and copies ran while one was open for 9% -> 6% of each run, Pallas kernels for 19% -> 0%
where the time goes in v4:
time: 497 us; the launch traced here: 492 us
  Pallas kernels  423 us (85%)
  matrix products  27.3 us (5%)
  other arithmetic  21.8 us (4%)
  local copies, waits for them, and re-layouts  11.3 us (2%)
    pallas_call x1, Pallas kernels, backward_call(): pl.pallas_call(functools.partial(backward_kernel, shape, count, regions,...  133 us
    pallas_call x1, Pallas kernels, late_call(): pl.pallas_call(functools.partial(late_kernel, regions, bits, small_phases...  97 us
    pallas_call x1, Pallas kernels, summary_call(): pl.pallas_call(functools.partial(summary_kernel, shape), name='scan_summa...  74.2 us
    pallas_call x1, Pallas kernels, forward_call(): pl.pallas_call(functools.partial(forward_kernel, shape), name='scan_forwa...  67.4 us
    pallas_call x2, Pallas kernels, product_call(): pl.pallas_call(functools.partial(product_kernel, steps, shapes, used), na...  29.6 us
    pallas_call x1, Pallas kernels, exchange(): pl.pallas_call(functools.partial(exchange_kernel, bits, state), name='exc...  22 us
  transfers between devices with their start and end apart: 2, of which 0 were waited for; matrix products, arithmetic and copies ran while one was open for 6% of the time, Pallas kernels for 0%

profile of v4, /device:TPU:0, one launch (start us, length us, event | category | flops | bytes accessed | tf_op | source)
XLA Modules:
  0.0 492.3 jit_solution(4998386708683100143)
XLA Ops:
  0.6 2.8 multiply_reduce_fusion
  3.5 3.2 multiply_convert_fusion.refs_0_
  6.8 7.1 %fusion.2.stream_ref = f32[1024,2048]{1,0:T(8,128)S(1)} fusion(bf16[1024,1024]{1,0:T(8,128)(2,1)S(1)} %multiply_convert_fusion.refs_0_, bf16[1024,4096]{1,0:T(8,128)(2,1)} %refs_2_.1), kind=kOutput, calls=%fused_computation.2 | convolution fusion | flops 4294967296 | bytes 14680064 | tf_op jit(solution)/shard_map/dot_general | solution.py:1670
  14.1 2.9 collective-permute-start
  17.0 6.8 %fusion.gating_ref = f32[1024,2048]{1,0:T(8,128)} fusion(bf16[1024,1024]{1,0:T(8,128)(2,1)S(1)} %multiply_convert_fusion.refs_0_, bf16[1024,4096]{1,0:T(8,128)(2,1)S(1)} %bitcast.86), kind=kOutput, calls=%fused_computation | convolution fusion | flops 4294967296 | bytes 14680064 | tf_op jit(solution)/shard_map/dot_general | solution.py:1673
  23.9 1.1 broadcast_bitcast_fusion.rates_ref
  25.0 7.2 %fusion.26.grad_gated_ref = f32[1024,2048]{1,0:T(8,128)} fusion(bf16[2048,1024]{1,0:T(8,128)(2,1)S(1)} %copy-done.3, bf16[8,128,1024]{2,1,0:T(8,128)(2,1)S(1)} %bitcast.88), kind=kOutput, calls=%fused_computation.74 | convolution fusion | flops 4294967296 | bytes 14680064 | tf_op jit(solution)/shard_map/dot_general | solution.py:1674
  32.2 1.4 fusion.5.spots_ref
  33.6 2.5 copy.45
  36.1 2.5 copy.46
  38.6 1.0 copy.31.select_in_ref.select_back_ref.refs_9_
  39.6 0.8 maximum_bitcast_fusion.head_ref
  40.4 74.2 %scan_summary.1 = (f32[1024,2048]{1,0:T(8,128)}, bf16[1024,2048]{1,0:T(8,128)(2,1)}, f32[1024,2048]{1,0:T(8,128)}, f32[1024,2048]{1,0:T(8,128)}, f32[1024,2048]{...) custom-call(f32[1024,2048]{1,0:T(8,128)} %copy-done, ...), custom_call_target="tpu_custom_call" | custom-call | tf_op jit(solution)/shard_map/scan_summary/pallas_call | solution.py:606
  114.6 22.0 %exchange.1 = (f32[16,2048]{1,0:T(8,128)}, f32[16,2048]{1,0:T(8,128)}) custom-call(f32[48,2048]{1,0:T(8,128)} %get-tuple-element.44.totals_ref), custom_call_target="tpu_custom_call" | custom-call | tf_op jit(solution)/shard_map/exchange/pallas_call | solution.py:1626
  136.6 67.4 %scan_forward.1 = (bf16[16384,2048]{1,0:T(8,128)(2,1)}, f32[1024,128]{1,0:T(8,128)}, bf16[1024,2048]{1,0:T(8,128)(2,1)}, bf16[1024,2048]{1,0:T(8,128)(2,1)}, f32[8,2048]{1,0:T(8,128)}) custom-call(f32[1024,2048]{1,0:T(8,128)} %get-tuple-element.38.step_ref, f32[1024,2048]{1,0:T(8,128)} %get-tuple-element.39.drive_ref, ...), custom_call_target="tpu_custom_call" | custom-call | tf_op jit(solution)/shard_map/scan_forward/pallas_call | solution.py:636
  204.0 17.7 %flat_product.2.flat_ref = f32[4096,8,128]{2,1,0:T(8,128)} custom-call(bf16[1024,1024]{1,0:T(8,128)(2,1)} %copy-done.1, bf16[1024,2048]{1,0:T(8,128)(2,1)} %get-tuple-element.53.refs_1_.refs_0_, bf16[1024,2048]{1,0:T(8,128)(2,1)} %get-tuple-element.54.refs_2_.refs_5_, bf16[1024,1024]{1,0:T(8,128)(2,1)} %bitcast.80), custom_call_target="tpu_custom_call" | custom-call | tf_op jit(solution)/shard_map/flat_product/pallas_call | solution.py:848
  221.8 1.2 fusion.6.begin_ref
  222.9 133.2 %scan_backward.1 = (bf16[1024,2048]{1,0:T(8,128)(2,1)}, bf16[1024,2048]{1,0:T(8,128)(2,1)}, bf16[1024,128]{1,0:T(8,128)(2,1)}, f32[128,2048]{1,0:T(8,128)}, f32[...) custom-call(f32[1024,2048]{1,0:T(8,128)} %get-tuple-element.38.step_ref, ...), custom_call_target="tpu_custom_call" | custom-call | tf_op jit(solution)/shard_map/scan_backward/pallas_call | solution.py:687
  356.1 1.2 slice_bitcast_fusion.1
  357.4 1.7 collective-permute-start.1
  359.1 4.5 fusion.30.refs_2_
  364.5 1.7 fusion.11.refs_5_
  366.9 1.0 fusion.16
  367.9 1.0 fusion.19
  368.9 0.9 fusion.22
  371.1 0.7 bitcast_dynamic-update-slice_fusion.refs_1_
  371.9 11.9 %flat_product.3.flat_ref = f32[2560,8,128]{2,1,0:T(8,128)} custom-call(bf16[1024,1024]{1,0:T(8,128)(2,1)} %copy-done.1, bf16[1024,2048]{1,0:T(8,128)(2,1)} %bitcast_dynamic-update-slice_fusion.refs_1_, f32[2048,128]{1,0:T(8,128)} %fusion.30.refs_2_, f32[4,2048]{1,0:T(4,128)} %pad_maximum_fusion.1.refs_3_, f32[1,2048]{1,0:T(1,128)} %get-tuple-element.78.refs_4_, ...), custom_call_target="tpu_custom_call" | custom-call | tf_op jit(solution)/shard_map/flat_product/pallas_call | solution.py:848
  383.8 97.0 %reduce_late.1 = (f32[205,8,128]{2,1,0:T(8,128)}, f32[2,8,128]{2,1,0:T(8,128)}, bf16[1024,1024]{1,0:T(8,128)(2,1)}, bf16[1024,1024]{1,0:T(8,128)(2,1)}, f32[205,8,128]{2,1,0:T(8,128)}) custom-call(f32[2560,8,128]{2,1,0:T(8,128)} %flat_product.3.flat_ref, f32[208,8,128]{2,1,0:T(8,128)} %get-tuple-element.63.early_ref, f32[1,1024]{1,0:T(1,128)} %bitcast.113, ...), custom_call_target="tpu_custom_call" | custom-call | tf_op jit(solution)/shard_map/reduce_late/pallas_call | solution.py:1523
  480.8 1.4 multiply_reduce_fusion.1
  483.6 4.5 add_multiply_fusion
  488.1 1.3 copy.52
  489.4 1.3 copy.53
  (70 shorter events, 3.4 us)
Async XLA Ops:
  3.5 13.5 %slice-start = ((s8[8388608]{0:T(1024)(128)(4,1)}), s8[4194304]{0:T(1024)(128)(4,1)S(1)}, s32[]{:S(2)}) async-start(s8[8388608]{0:T(1024)(128)(4,1)} %bitcast.85), calls=%async_computation | async-start | bytes 8388608
  6.8 10.2 %copy-start.1 = (bf16[1024,1024]{1,0:T(8,128)(2,1)}, bf16[1024,1024]{1,0:T(8,128)(2,1)S(1)}, u32[]{:S(2)}) copy-start(bf16[1024,1024]{1,0:T(8,128)(2,1)S(1)} %multiply_convert_fusion.refs_0_) | copy-start | bytes 6291460
  6.8 10.2 %slice-start.1 = ((s8[8388608]{0:T(1024)(128)(4,1)}), s8[4194304]{0:T(1024)(128)(4,1)S(1)}, s32[]{:S(2)}) async-start(s8[8388608]{0:T(1024)(128)(4,1)} %bitcast.85), calls=%async_computation.1 | async-start | bytes 8388608
  13.9 9.9 %copy-start = (f32[1024,2048]{1,0:T(8,128)}, f32[1024,2048]{1,0:T(8,128)S(1)}, u32[]{:S(2)}) copy-start(f32[1024,2048]{1,0:T(8,128)S(1)} %fusion.2.stream_ref) | copy-start | bytes 25165828
  14.0 9.8 %copy-start.13 = (f32[16,2048]{1,0:T(8,128)S(1)}, f32[16,2048]{1,0:T(8,128)}, u32[]{:S(2)}) copy-start(f32[16,2048]{1,0:T(8,128)} %refs_12_.1) | copy-start | bytes 393220
  14.0 11.0 %copy-start.3 = (bf16[2048,1024]{1,0:T(8,128)(2,1)S(1)}, bf16[2048,1024]{1,0:T(8,128)(2,1)}, u32[]{:S(2)}) copy-start(bf16[2048,1024]{1,0:T(8,128)(2,1)} %refs_6_.1) | copy-start | bytes 12582916
  14.0 10.9 %copy-start.5 = (bf16[1,1024,1024]{2,1,0:T(8,128)(2,1)S(1)}, bf16[1,1024,1024]{2,1,0:T(8,128)(2,1)}, u32[]{:S(2)}) copy-start(bf16[1,1024,1024]{2,1,0:T(8,128)(2,1)} %param.15) | copy-start | bytes 6291460
  14.1 25.6 %collective-permute-start = (f32[3,2048]{1,0:T(4,128)S(1)}, f32[3,2048]{1,0:T(4,128)S(1)}, u32[]{:S(2)}, u32[]{:S(2)}) collective-permute-start(f32[3,2048]{1,0:T(4,128)S(1)} %bitcast.103), channel_id=1, source_target_pairs={{0,1},{1,2},{2,3},{3,4},{4,5},{5,6},{6,7},{8,9},{9,10},{10,11},{11... | collective-permute-start | bytes 73736 | tf_op jit(solution)/shard_map/ppermute | solution.py:36
  25.0 8.6 %copy-start.14 = (f32[4,2048]{1,0:T(4,128)S(1)}, f32[4,2048]{1,0:T(4,128)}, u32[]{:S(2)}) copy-start(f32[4,2048]{1,0:T(4,128)} %refs_7_.1) | copy-start | bytes 98308
  32.2 3.9 copy-start.2
  33.6 5.0 %copy-start.15 = (bf16[2048,96]{0,1:T(8,128)(2,1)S(1)}, bf16[2048,96]{0,1:T(8,128)(2,1)}, u32[]{:S(2)}) copy-start(bf16[2048,96]{0,1:T(8,128)(2,1)} %param.20) | copy-start | bytes 1179652
  204.0 17.8 %copy-start.8 = (f32[128,2048]{1,0:T(8,128)S(1)}, f32[128,2048]{1,0:T(8,128)}, u32[]{:S(2)}) copy-start(f32[128,2048]{1,0:T(8,128)} %get-tuple-element.43) | copy-start | bytes 3145732
  204.0 17.7 %copy-start.9 = (f32[128,2048]{1,0:T(8,128)S(1)}, f32[128,2048]{1,0:T(8,128)}, u32[]{:S(2)}) copy-start(f32[128,2048]{1,0:T(8,128)} %get-tuple-element.42) | copy-start | bytes 3145732
  204.0 17.7 %copy-start.18 = (f32[16,2048]{1,0:T(8,128)S(1)}, f32[16,2048]{1,0:T(8,128)}, u32[]{:S(2)}) copy-start(f32[16,2048]{1,0:T(8,128)} %get-tuple-element.45) | copy-start | bytes 393220
  356.1 7.5 %copy-start.10 = (f32[128,2048]{1,0:T(8,128)S(1)}, f32[128,2048]{1,0:T(8,128)}, u32[]{:S(2)}) copy-start(f32[128,2048]{1,0:T(8,128)} %get-tuple-element.61) | copy-start | bytes 3145732
  356.1 8.4 %copy-start.4 = (bf16[1024,2048]{1,0:T(8,128)(2,1)S(1)}, bf16[1024,2048]{1,0:T(8,128)(2,1)}, u32[]{:S(2)}) copy-start(bf16[1024,2048]{1,0:T(8,128)(2,1)} %get-tuple-element.60) | copy-start | bytes 12582916
  356.1 8.4 %copy-start.17 = (bf16[1024,128]{1,0:T(8,128)(2,1)S(1)}, bf16[1024,128]{1,0:T(8,128)(2,1)}, u32[]{:S(2)}) copy-start(bf16[1024,128]{1,0:T(8,128)(2,1)} %get-tuple-element.59) | copy-start | bytes 786436
  357.4 9.5 %collective-permute-start.1 = (f32[3,2048]{1,0:T(4,128)S(1)}, f32[3,2048]{1,0:T(4,128)S(1)}, u32[]{:S(2)}, u32[]{:S(2)}) collective-permute-start(f32[3,2048]{1,0:T(4,128)S(1)} %bitcast.105), channel_id=1, source_target_pairs={{1,0},{2,1},{3,2},{4,3},{5,4},{6,5},{7,6},{9,8},{10,9},{11,10},{12... | collective-permute-start | bytes 73736 | tf_op jit(solution)/shard_map/ppermute | solution.py:36
  363.6 2.6 copy-start.16
  363.6 2.7 copy-start.19
  363.8 7.3 %copy-start.11 = (f32[48,2048]{1,0:T(8,128)S(1)}, f32[48,2048]{1,0:T(8,128)}, u32[]{:S(2)}) copy-start(f32[48,2048]{1,0:T(8,128)} %get-tuple-element.56) | copy-start | bytes 1179652
  383.8 99.8 %copy-start.12 = (f32[208352]{0:T(1024)S(1)}, f32[208352]{0:T(1024)}, u32[]{:S(2)}) copy-start(f32[208352]{0:T(1024)} %param.26) | copy-start | bytes 2500228
  480.7 7.3 %copy-start.7 = (bf16[1024,1024]{1,0:T(8,128)(2,1)S(1)}, bf16[1024,1024]{1,0:T(8,128)(2,1)}, u32[]{:S(2)}) copy-start(bf16[1024,1024]{1,0:T(8,128)(2,1)} %get-tuple-element.64) | copy-start | bytes 6291460
  483.6 5.8 %copy-start.6 = (bf16[1024,1024]{1,0:T(8,128)(2,1)S(1)}, bf16[1024,1024]{1,0:T(8,128)(2,1)}, u32[]{:S(2)}) copy-start(bf16[1024,1024]{1,0:T(8,128)(2,1)} %get-tuple-element.65) | copy-start | bytes 6291460

commit v5 on v4

--- a/solution.py
+++ b/solution.py
@@ -59,10 +59,14 @@
     out_ref[...] = jnp.dot(sel_ref[...], spots_ref[...], preferred_element_type=f32)
 
 
-def gather_lanes(src_ref, spots_ref, out_ref):
-    spots = spots_ref[0:LANE, 0 : src_ref.shape[1]]
-    back = (((1,), (1,)), ((), ()))
-    out_ref[...] = lax.dot_general(src_ref[...].astype(bf16), spots, back, preferred_element_type=f32)
+def gather_table(out_ref):
+    row = lax.broadcasted_iota(jnp.int32, (LANE, LANE), 1)
+    for n in range(out_ref.shape[0] // LANE):
+        out_ref[n * LANE : (n + 1) * LANE, :] = jnp.where(row == n, 1.0, 0.0).astype(bf16)
+
+
+def gather_lanes(src_ref, table_ref, out_ref):
+    out_ref[...] = jnp.dot(src_ref[...].astype(bf16), table_ref[...], preferred_element_type=f32)
 
 
 def spread_table(count):
@@ -138,7 +142,7 @@
             grad_ref[here, lanes] = grad_gated_ref[here, lanes] * (gating * jax.nn.sigmoid(gating))
             return carry
 
-        lax.fori_loop(0, tiles // 2, pair, 0, unroll=8)
+        lax.fori_loop(0, tiles // 2, pair, 0, unroll=tiles // 2)
         return carry
 
     lax.fori_loop(0, inner // (2 * LANE), convs, 0)
@@ -170,7 +174,7 @@
             drive_ref[here, lanes] = step * conv_ref[here, lanes].astype(f32)
             return carry
 
-        lax.fori_loop(0, tiles // 2, pair, 0, unroll=8)
+        lax.fori_loop(0, tiles // 2, pair, 0, unroll=tiles // 2)
         return carry
 
     lax.fori_loop(0, inner // (2 * LANE), steps, 0)
@@ -269,12 +273,14 @@
     select_ref,
     sums_ref,
     scanned_ref,
+    table_ref,
 ):
     tiles, state, inner, cols, group = shape
 
     @pl.when(pl.program_id(0) == 0)
     def _():
         skip_grad_ref[...] = jnp.zeros_like(skip_grad_ref)
+        gather_table(table_ref)
         for n in range(state):
             here = slice(n * SUB, (n + 1) * SUB)
             state_ref[here, :] = pre_state_ref[here, :] + pre_decay_ref[here, :] * entry_ref[n : n + 1, :]
@@ -330,7 +336,7 @@
         return carry
 
     lax.fori_loop(0, inner // (LANE * cols), columns, 0)
-    gather_lanes(sums_ref, spots_ref, readout_grad_ref)
+    gather_lanes(sums_ref, table_ref, readout_grad_ref)
 
     def finish(c, carry):
         lanes = at(c * 2 * LANE, 2 * LANE)
@@ -350,7 +356,7 @@
             return total + product[:SUB] + product[SUB:]
 
         zero = jnp.zeros((SUB, 2 * LANE), f32)
-        skip_grad_ref[:, lanes] += lax.fori_loop(0, tiles // 2, pair, zero, unroll=8)
+        skip_grad_ref[:, lanes] += lax.fori_loop(0, tiles // 2, pair, zero, unroll=tiles // 2)
         return carry
 
     lax.fori_loop(0, inner // (2 * LANE), finish, 0)
@@ -393,6 +399,7 @@
     grad_conv_ref,
     inject_grad_ref,
     low_grad_ref,
+    table_ref,
     *refs,
 ):
     tiles, state, inner, cols, group, rank = shape
@@ -422,6 +429,7 @@
 
     @pl.when(pl.program_id(0) == 0)
     def _():
+        gather_table(table_ref)
         rate_grad_ref[...] = jnp.zeros_like(rate_grad_ref)
         taps_grad_ref[...] = jnp.zeros_like(taps_grad_ref)
         grad_conv_ref[tiles * SUB :, :] = jnp.zeros((grad_conv_ref.shape[0] - tiles * SUB, inner), f32)
@@ -487,7 +495,7 @@
         return carry
 
     lax.fori_loop(0, inner // (LANE * cols), columns, 0)
-    gather_lanes(sums_ref, spots_ref, inject_grad_ref)
+    gather_lanes(sums_ref, table_ref, inject_grad_ref)
 
     def steps(c, carry):
         lanes = at(c * 2 * LANE, 2 * LANE)
@@ -504,7 +512,7 @@
             return total + pre[:SUB] + pre[SUB:]
 
         zero = jnp.zeros((SUB, 2 * LANE), f32)
-        taps_grad_ref[(width + 1) * SUB :, lanes] += lax.fori_loop(0, tiles // 2, pair, zero, unroll=8)
+        taps_grad_ref[(width + 1) * SUB :, lanes] += lax.fori_loop(0, tiles // 2, pair, zero, unroll=tiles // 2)
         return carry
 
     lax.fori_loop(0, inner // (2 * LANE), steps, 0)
@@ -560,7 +568,7 @@
             return tuple(totals)
 
         zero = jnp.zeros((SUB, 2 * LANE), f32)
-        totals = lax.fori_loop(0, tiles // 2, tap, (zero,) * (width + 1), unroll=8)
+        totals = lax.fori_loop(0, tiles // 2, tap, (zero,) * (width + 1), unroll=tiles // 2)
         for k in range(width + 1):
             taps_grad_ref[k * SUB : (k + 1) * SUB, lanes] += totals[k]
         return carry
@@ -657,6 +665,7 @@
             pltpu.VMEM((tiles * SUB, 2 * state * LANE), f32),
             pltpu.VMEM((tiles * SUB, state * LANE), f32),
             pltpu.VMEM((tiles * SUB, inner), f32),
+            pltpu.VMEM((state * LANE, LANE), bf16),
         ],
         compiler_params=pltpu.CompilerParams(vmem_limit_bytes=VMEM_BYTES),
     )(step, drive, grad, sel, spots, rates, pre_decay, pre_state, entry, conv, gating, grad_gated, skip)
@@ -719,6 +728,7 @@
             pltpu.VMEM((tiles * SUB + halo, inner), f32),
             pltpu.VMEM((tiles * SUB, LANE), f32),
             pltpu.VMEM((tiles * SUB, LANE), f32),
+            pltpu.VMEM((state * LANE, LANE), bf16),
         ]
         + Reducer.scratch(regions.depth, bits, phases),
         compiler_params=pltpu.CompilerParams(

time: 497 us -> 483 us (0.972)
  Pallas kernels: 423 us -> 410 us
    pallas_call x1, Pallas kernels: 133 us -> 121 us  [backward_call(): pl.pallas_call(functools.partial(backward_kernel, shape, count, regions,...]
where the time goes in v5:
time: 483 us; the launch traced here: 479 us
  Pallas kernels  410 us (85%)
  matrix products  27.3 us (6%)
  other arithmetic  21.8 us (5%)
  local copies, waits for them, and re-layouts  11.3 us (2%)
    pallas_call x1, Pallas kernels, backward_call(): pl.pallas_call(functools.partial(backward_kernel, shape, count, regions,...  121 us
    pallas_call x1, Pallas kernels, late_call(): pl.pallas_call(functools.partial(late_kernel, regions, bits, small_phases...  97.6 us
    pallas_call x1, Pallas kernels, summary_call(): pl.pallas_call(functools.partial(summary_kernel, shape), name='scan_summa...  74.2 us
    pallas_call x1, Pallas kernels, forward_call(): pl.pallas_call(functools.partial(forward_kernel, shape), name='scan_forwa...  65.5 us
    pallas_call x2, Pallas kernels, product_call(): pl.pallas_call(functools.partial(product_kernel, steps, shapes, used), na...  29.6 us
    pallas_call x1, Pallas kernels, exchange(): pl.pallas_call(functools.partial(exchange_kernel, bits, state), name='exc...  22 us
  transfers between devices with their start and end apart: 2, of which 0 were waited for; matrix products, arithmetic and copies ran while one was open for 6% of the time, Pallas kernels for 0%

profile of v5, /device:TPU:0, one launch (start us, length us, event | category | flops | bytes accessed | tf_op | source)
XLA Modules:
  0.0 478.6 jit_solution(3403157898331130809)
XLA Ops:
  0.6 2.8 multiply_reduce_fusion
  3.5 3.2 multiply_convert_fusion.refs_0_
  6.8 7.1 %fusion.2.stream_ref = f32[1024,2048]{1,0:T(8,128)S(1)} fusion(bf16[1024,1024]{1,0:T(8,128)(2,1)S(1)} %multiply_convert_fusion.refs_0_, bf16[1024,4096]{1,0:T(8,128)(2,1)} %refs_2_.1), kind=kOutput, calls=%fused_computation.2 | convolution fusion | flops 4294967296 | bytes 14680064 | tf_op jit(solution)/shard_map/dot_general | solution.py:1680
  14.1 2.9 collective-permute-start
  17.0 6.8 %fusion.gating_ref = f32[1024,2048]{1,0:T(8,128)} fusion(bf16[1024,1024]{1,0:T(8,128)(2,1)S(1)} %multiply_convert_fusion.refs_0_, bf16[1024,4096]{1,0:T(8,128)(2,1)S(1)} %bitcast.86), kind=kOutput, calls=%fused_computation | convolution fusion | flops 4294967296 | bytes 14680064 | tf_op jit(solution)/shard_map/dot_general | solution.py:1683
  23.9 1.1 broadcast_bitcast_fusion.rates_ref
  25.0 7.2 %fusion.26.grad_gated_ref = f32[1024,2048]{1,0:T(8,128)} fusion(bf16[2048,1024]{1,0:T(8,128)(2,1)S(1)} %copy-done.3, bf16[8,128,1024]{2,1,0:T(8,128)(2,1)S(1)} %bitcast.88), kind=kOutput, calls=%fused_computation.74 | convolution fusion | flops 4294967296 | bytes 14680064 | tf_op jit(solution)/shard_map/dot_general | solution.py:1684
  32.2 1.4 fusion.5.spots_ref
  33.6 2.5 copy.45
  36.1 2.5 copy.46
  38.6 1.0 copy.31.select_in_ref.select_back_ref.refs_9_
  39.6 0.8 maximum_bitcast_fusion.head_ref
  40.4 74.2 %scan_summary.1 = (f32[1024,2048]{1,0:T(8,128)}, bf16[1024,2048]{1,0:T(8,128)(2,1)}, f32[1024,2048]{1,0:T(8,128)}, f32[1024,2048]{1,0:T(8,128)}, f32[1024,2048]{...) custom-call(f32[1024,2048]{1,0:T(8,128)} %copy-done, ...), custom_call_target="tpu_custom_call" | custom-call | tf_op jit(solution)/shard_map/scan_summary/pallas_call | solution.py:614
  114.6 22.0 %exchange.1 = (f32[16,2048]{1,0:T(8,128)}, f32[16,2048]{1,0:T(8,128)}) custom-call(f32[48,2048]{1,0:T(8,128)} %get-tuple-element.44.totals_ref), custom_call_target="tpu_custom_call" | custom-call | tf_op jit(solution)/shard_map/exchange/pallas_call | solution.py:1636
  136.6 65.5 %scan_forward.1 = (bf16[16384,2048]{1,0:T(8,128)(2,1)}, f32[1024,128]{1,0:T(8,128)}, bf16[1024,2048]{1,0:T(8,128)(2,1)}, bf16[1024,2048]{1,0:T(8,128)(2,1)}, f32[8,2048]{1,0:T(8,128)}) custom-call(f32[1024,2048]{1,0:T(8,128)} %get-tuple-element.38.step_ref, f32[1024,2048]{1,0:T(8,128)} %get-tuple-element.39.drive_ref, ...), custom_call_target="tpu_custom_call" | custom-call | tf_op jit(solution)/shard_map/scan_forward/pallas_call | solution.py:644
  202.2 17.7 %flat_product.2.flat_ref = f32[4096,8,128]{2,1,0:T(8,128)} custom-call(bf16[1024,1024]{1,0:T(8,128)(2,1)} %copy-done.1, bf16[1024,2048]{1,0:T(8,128)(2,1)} %get-tuple-element.53.refs_1_.refs_0_, bf16[1024,2048]{1,0:T(8,128)(2,1)} %get-tuple-element.54.refs_2_.refs_5_, bf16[1024,1024]{1,0:T(8,128)(2,1)} %bitcast.80), custom_call_target="tpu_custom_call" | custom-call | tf_op jit(solution)/shard_map/flat_product/pallas_call | solution.py:858
  219.9 1.2 fusion.6.begin_ref
  221.1 120.7 %scan_backward.1 = (bf16[1024,2048]{1,0:T(8,128)(2,1)}, bf16[1024,2048]{1,0:T(8,128)(2,1)}, bf16[1024,128]{1,0:T(8,128)(2,1)}, f32[128,2048]{1,0:T(8,128)}, f32[...) custom-call(f32[1024,2048]{1,0:T(8,128)} %get-tuple-element.38.step_ref, ...), custom_call_target="tpu_custom_call" | custom-call | tf_op jit(solution)/shard_map/scan_backward/pallas_call | solution.py:696
  341.8 1.2 slice_bitcast_fusion.1
  343.1 1.7 collective-permute-start.1
  344.7 4.5 fusion.30.refs_2_
  350.2 1.7 fusion.11.refs_5_
  352.6 1.0 fusion.16
  353.6 1.0 fusion.19
  354.6 0.9 fusion.22
  356.8 0.7 bitcast_dynamic-update-slice_fusion.refs_1_
  357.5 11.9 %flat_product.3.flat_ref = f32[2560,8,128]{2,1,0:T(8,128)} custom-call(bf16[1024,1024]{1,0:T(8,128)(2,1)} %copy-done.1, bf16[1024,2048]{1,0:T(8,128)(2,1)} %bitcast_dynamic-update-slice_fusion.refs_1_, f32[2048,128]{1,0:T(8,128)} %fusion.30.refs_2_, f32[4,2048]{1,0:T(4,128)} %pad_maximum_fusion.1.refs_3_, f32[1,2048]{1,0:T(1,128)} %get-tuple-element.78.refs_4_, ...), custom_call_target="tpu_custom_call" | custom-call | tf_op jit(solution)/shard_map/flat_product/pallas_call | solution.py:858
  369.4 97.6 %reduce_late.1 = (f32[205,8,128]{2,1,0:T(8,128)}, f32[2,8,128]{2,1,0:T(8,128)}, bf16[1024,1024]{1,0:T(8,128)(2,1)}, bf16[1024,1024]{1,0:T(8,128)(2,1)}, f32[205,8,128]{2,1,0:T(8,128)}) custom-call(f32[2560,8,128]{2,1,0:T(8,128)} %flat_product.3.flat_ref, f32[208,8,128]{2,1,0:T(8,128)} %get-tuple-element.63.early_ref, f32[1,1024]{1,0:T(1,128)} %bitcast.113, ...), custom_call_target="tpu_custom_call" | custom-call | tf_op jit(solution)/shard_map/reduce_late/pallas_call | solution.py:1533
  467.0 1.4 multiply_reduce_fusion.1
  469.9 4.5 add_multiply_fusion
  474.3 1.3 copy.52
  475.7 1.3 copy.53
  (70 shorter events, 3.4 us)
Async XLA Ops:
  3.5 13.5 %slice-start = ((s8[8388608]{0:T(1024)(128)(4,1)}), s8[4194304]{0:T(1024)(128)(4,1)S(1)}, s32[]{:S(2)}) async-start(s8[8388608]{0:T(1024)(128)(4,1)} %bitcast.85), calls=%async_computation | async-start | bytes 8388608
  6.8 10.2 %copy-start.1 = (bf16[1024,1024]{1,0:T(8,128)(2,1)}, bf16[1024,1024]{1,0:T(8,128)(2,1)S(1)}, u32[]{:S(2)}) copy-start(bf16[1024,1024]{1,0:T(8,128)(2,1)S(1)} %multiply_convert_fusion.refs_0_) | copy-start | bytes 6291460
  6.8 10.2 %slice-start.1 = ((s8[8388608]{0:T(1024)(128)(4,1)}), s8[4194304]{0:T(1024)(128)(4,1)S(1)}, s32[]{:S(2)}) async-start(s8[8388608]{0:T(1024)(128)(4,1)} %bitcast.85), calls=%async_computation.1 | async-start | bytes 8388608
  13.9 9.9 %copy-start = (f32[1024,2048]{1,0:T(8,128)}, f32[1024,2048]{1,0:T(8,128)S(1)}, u32[]{:S(2)}) copy-start(f32[1024,2048]{1,0:T(8,128)S(1)} %fusion.2.stream_ref) | copy-start | bytes 25165828
  14.0 9.8 %copy-start.13 = (f32[16,2048]{1,0:T(8,128)S(1)}, f32[16,2048]{1,0:T(8,128)}, u32[]{:S(2)}) copy-start(f32[16,2048]{1,0:T(8,128)} %refs_12_.1) | copy-start | bytes 393220
  14.0 11.0 %copy-start.3 = (bf16[2048,1024]{1,0:T(8,128)(2,1)S(1)}, bf16[2048,1024]{1,0:T(8,128)(2,1)}, u32[]{:S(2)}) copy-start(bf16[2048,1024]{1,0:T(8,128)(2,1)} %refs_6_.1) | copy-start | bytes 12582916
  14.0 10.9 %copy-start.5 = (bf16[1,1024,1024]{2,1,0:T(8,128)(2,1)S(1)}, bf16[1,1024,1024]{2,1,0:T(8,128)(2,1)}, u32[]{:S(2)}) copy-start(bf16[1,1024,1024]{2,1,0:T(8,128)(2,1)} %param.15) | copy-start | bytes 6291460
  14.1 25.6 %collective-permute-start = (f32[3,2048]{1,0:T(4,128)S(1)}, f32[3,2048]{1,0:T(4,128)S(1)}, u32[]{:S(2)}, u32[]{:S(2)}) collective-permute-start(f32[3,2048]{1,0:T(4,128)S(1)} %bitcast.103), channel_id=1, source_target_pairs={{0,1},{1,2},{2,3},{3,4},{4,5},{5,6},{6,7},{8,9},{9,10},{10,11},{11... | collective-permute-start | bytes 73736 | tf_op jit(solution)/shard_map/ppermute | solution.py:36
  25.0 8.6 %copy-start.14 = (f32[4,2048]{1,0:T(4,128)S(1)}, f32[4,2048]{1,0:T(4,128)}, u32[]{:S(2)}) copy-start(f32[4,2048]{1,0:T(4,128)} %refs_7_.1) | copy-start | bytes 98308
  32.2 3.9 copy-start.2
  33.6 5.0 %copy-start.15 = (bf16[2048,96]{0,1:T(8,128)(2,1)S(1)}, bf16[2048,96]{0,1:T(8,128)(2,1)}, u32[]{:S(2)}) copy-start(bf16[2048,96]{0,1:T(8,128)(2,1)} %param.20) | copy-start | bytes 1179652
  202.1 17.8 %copy-start.8 = (f32[128,2048]{1,0:T(8,128)S(1)}, f32[128,2048]{1,0:T(8,128)}, u32[]{:S(2)}) copy-start(f32[128,2048]{1,0:T(8,128)} %get-tuple-element.43) | copy-start | bytes 3145732
  202.1 17.8 %copy-start.9 = (f32[128,2048]{1,0:T(8,128)S(1)}, f32[128,2048]{1,0:T(8,128)}, u32[]{:S(2)}) copy-start(f32[128,2048]{1,0:T(8,128)} %get-tuple-element.42) | copy-start | bytes 3145732
  202.2 17.7 %copy-start.18 = (f32[16,2048]{1,0:T(8,128)S(1)}, f32[16,2048]{1,0:T(8,128)}, u32[]{:S(2)}) copy-start(f32[16,2048]{1,0:T(8,128)} %get-tuple-element.45) | copy-start | bytes 393220
  341.8 7.5 %copy-start.10 = (f32[128,2048]{1,0:T(8,128)S(1)}, f32[128,2048]{1,0:T(8,128)}, u32[]{:S(2)}) copy-start(f32[128,2048]{1,0:T(8,128)} %get-tuple-element.61) | copy-start | bytes 3145732
  341.8 8.4 %copy-start.4 = (bf16[1024,2048]{1,0:T(8,128)(2,1)S(1)}, bf16[1024,2048]{1,0:T(8,128)(2,1)}, u32[]{:S(2)}) copy-start(bf16[1024,2048]{1,0:T(8,128)(2,1)} %get-tuple-element.60) | copy-start | bytes 12582916
  341.8 8.4 %copy-start.17 = (bf16[1024,128]{1,0:T(8,128)(2,1)S(1)}, bf16[1024,128]{1,0:T(8,128)(2,1)}, u32[]{:S(2)}) copy-start(bf16[1024,128]{1,0:T(8,128)(2,1)} %get-tuple-element.59) | copy-start | bytes 786436
  343.1 9.5 %collective-permute-start.1 = (f32[3,2048]{1,0:T(4,128)S(1)}, f32[3,2048]{1,0:T(4,128)S(1)}, u32[]{:S(2)}, u32[]{:S(2)}) collective-permute-start(f32[3,2048]{1,0:T(4,128)S(1)} %bitcast.105), channel_id=1, source_target_pairs={{1,0},{2,1},{3,2},{4,3},{5,4},{6,5},{7,6},{9,8},{10,9},{11,10},{12... | collective-permute-start | bytes 73736 | tf_op jit(solution)/shard_map/ppermute | solution.py:36
  349.2 2.6 copy-start.16
  349.2 2.7 copy-start.19
  349.5 7.3 %copy-start.11 = (f32[48,2048]{1,0:T(8,128)S(1)}, f32[48,2048]{1,0:T(8,128)}, u32[]{:S(2)}) copy-start(f32[48,2048]{1,0:T(8,128)} %get-tuple-element.56) | copy-start | bytes 1179652
  369.4 100.4 %copy-start.12 = (f32[208352]{0:T(1024)S(1)}, f32[208352]{0:T(1024)}, u32[]{:S(2)}) copy-start(f32[208352]{0:T(1024)} %param.26) | copy-start | bytes 2500228
  467.0 7.3 %copy-start.7 = (bf16[1024,1024]{1,0:T(8,128)(2,1)S(1)}, bf16[1024,1024]{1,0:T(8,128)(2,1)}, u32[]{:S(2)}) copy-start(bf16[1024,1024]{1,0:T(8,128)(2,1)} %get-tuple-element.64) | copy-start | bytes 6291460
  469.9 5.8 %copy-start.6 = (bf16[1024,1024]{1,0:T(8,128)(2,1)S(1)}, bf16[1024,1024]{1,0:T(8,128)(2,1)}, u32[]{:S(2)}) copy-start(bf16[1024,1024]{1,0:T(8,128)(2,1)} %get-tuple-element.65) | copy-start | bytes 6291460

commit v6 on v5

--- a/solution.py
+++ b/solution.py
@@ -1257,6 +1257,41 @@
 
         lax.fori_loop(0, rows // (2 * SUB), one, 0)
 
+    inside = lax.broadcasted_iota(jnp.int32, (SUB, LANE), 0) * LANE + lax.broadcasted_iota(
+        jnp.int32, (SUB, LANE), 1
+    )
+    def own(value, row):
+        spot = inside + (row * ROW - owner * span)
+        return jnp.where((spot >= 0) & (spot < span), value, 0.0)
+
+    def keep(total, value, row):
+        wide_window[row - base + margin] = value
+        part = own(value, row)
+        return total + part * part
+
+    half = regions.per // 2
+    zero = jnp.zeros((SUB, LANE), f32)
+
+    def place_early():
+        wide_window[...] = jnp.zeros_like(wide_window)
+
+        @pl.when(base < regions.small_base)
+        def _():
+            def line(d, total):
+                row = regions.in_base + (regions.in_first(owner) + d) * regions.per + half
+                for q in range(half):
+                    total = keep(total, early_ref[d * half + q], row + q)
+                return total
+
+            sums[blk, 0] = lax.fori_loop(0, regions.lines, line, zero, unroll=4)
+
+        @pl.when(base >= regions.small_base)
+        def _():
+            def line(i, total):
+                return keep(total, early_ref[i], regions.out_base + regions.out_first(owner) + i)
+
+            sums[blk, 0] = lax.fori_loop(0, regions.slot, line, zero, unroll=8)
+
     def lay_params():
         conv_w, conv_b, select_w, step_w, step_b, rate, skip = weights
         used = select_w.shape[1]
@@ -1395,9 +1430,13 @@
         def _():
             place_params()
 
+        @pl.when(t == blocks + 2)
+        def _():
+            place_early()
+
         return carry
 
-    lax.fori_loop(0, max(work.slots, blocks + 2), slot, 0)
+    lax.fori_loop(0, max(work.slots, blocks + 3), slot, 0)
     for p in range(few):
         if p + work.done >= work.slots:
             give_small(p)
@@ -1424,26 +1463,9 @@
                             device_id_type=MESH,
                         ).wait_recv()
 
-    inside = lax.broadcasted_iota(jnp.int32, (SUB, LANE), 0) * LANE + lax.broadcasted_iota(
-        jnp.int32, (SUB, LANE), 1
-    )
-    sums[blk, 0] = jnp.zeros((SUB, LANE), f32)
     gain = jnp.sum(gain_sum[...], 0, keepdims=True)
     for a in range(SUB):
         sums[blk, 1, a : a + 1, :] = gain[:, a * LANE : (a + 1) * LANE]
-    half = regions.per // 2
-    wide_window[...] = jnp.zeros_like(wide_window)
-
-    def own(value, row):
-        spot = inside + (row * ROW - owner * span)
-        return jnp.where((spot >= 0) & (spot < span), value, 0.0)
-
-    def keep(total, value, row):
-        wide_window[row - base + margin] = value
-        part = own(value, row)
-        return total + part * part
-
-    zero = jnp.zeros((SUB, LANE), f32)
 
     @pl.when(base < regions.small_base)
     def _():
@@ -1451,17 +1473,9 @@
             row = regions.in_base + (regions.in_first(owner) + d) * regions.per
             for q in range(half):
                 total = keep(total, late_ref[d * half + q], row + q)
-                total = keep(total, early_ref[d * half + q], row + half + q)
             return total
 
-        sums[blk, 0] += lax.fori_loop(0, regions.lines, line, zero, unroll=2)
-
-    @pl.when(base >= regions.small_base)
-    def _():
-        def line(i, total):
-            return keep(total, early_ref[i], regions.out_base + regions.out_first(owner) + i)
-
-        sums[blk, 0] += lax.fori_loop(0, regions.slot, line, zero, unroll=4)
+        sums[blk, 0] += lax.fori_loop(0, regions.lines, line, zero, unroll=4)
 
     size = small_phases[0][2]
 
@@ -1480,7 +1494,7 @@
             part = jnp.where(here, own(value, row), 0.0)
             return total + part * part
 
-        sums[blk, 0] += lax.fori_loop(0, regions.need, line, zero, unroll=2)
+        sums[blk, 0] += lax.fori_loop(0, regions.need, line, zero, unroll=5)
 
     window_ref[...] = wide_window[margin : margin + regions.need]
 

time: 483 us -> 482 us (level)
  no operation moved by 1% of the time
where the time goes in v6:
time: 482 us; the launch traced here: 478 us
  Pallas kernels  409 us (85%)
  matrix products  27.3 us (6%)
  other arithmetic  21.8 us (5%)
  local copies, waits for them, and re-layouts  11.3 us (2%)
    pallas_call x1, Pallas kernels, backward_call(): pl.pallas_call(functools.partial(backward_kernel, shape, count, regions,...  121 us
    pallas_call x1, Pallas kernels, late_call(): pl.pallas_call(functools.partial(late_kernel, regions, bits, small_phases...  96.8 us
    pallas_call x1, Pallas kernels, summary_call(): pl.pallas_call(functools.partial(summary_kernel, shape), name='scan_summa...  74.2 us
    pallas_call x1, Pallas kernels, forward_call(): pl.pallas_call(functools.partial(forward_kernel, shape), name='scan_forwa...  65.5 us
    pallas_call x2, Pallas kernels, product_call(): pl.pallas_call(functools.partial(product_kernel, steps, shapes, used), na...  29.6 us
    pallas_call x1, Pallas kernels, exchange(): pl.pallas_call(functools.partial(exchange_kernel, bits, state), name='exc...  22 us
  transfers between devices with their start and end apart: 2, of which 0 were waited for; matrix products, arithmetic and copies ran while one was open for 6% of the time, Pallas kernels for 0%

profile of v6, /device:TPU:0, one launch (start us, length us, event | category | flops | bytes accessed | tf_op | source)
XLA Modules:
  0.0 477.8 jit_solution(12424186714458664738)
XLA Ops:
  0.6 2.8 multiply_reduce_fusion
  3.5 3.2 multiply_convert_fusion.refs_0_
  6.8 7.1 %fusion.2.stream_ref = f32[1024,2048]{1,0:T(8,128)S(1)} fusion(bf16[1024,1024]{1,0:T(8,128)(2,1)S(1)} %multiply_convert_fusion.refs_0_, bf16[1024,4096]{1,0:T(8,128)(2,1)} %refs_2_.1), kind=kOutput, calls=%fused_computation.2 | convolution fusion | flops 4294967296 | bytes 14680064 | tf_op jit(solution)/shard_map/dot_general | solution.py:1694
  14.1 2.9 collective-permute-start
  17.0 6.8 %fusion.gating_ref = f32[1024,2048]{1,0:T(8,128)} fusion(bf16[1024,1024]{1,0:T(8,128)(2,1)S(1)} %multiply_convert_fusion.refs_0_, bf16[1024,4096]{1,0:T(8,128)(2,1)S(1)} %bitcast.86), kind=kOutput, calls=%fused_computation | convolution fusion | flops 4294967296 | bytes 14680064 | tf_op jit(solution)/shard_map/dot_general | solution.py:1697
  23.9 1.1 broadcast_bitcast_fusion.rates_ref
  25.0 7.2 %fusion.26.grad_gated_ref = f32[1024,2048]{1,0:T(8,128)} fusion(bf16[2048,1024]{1,0:T(8,128)(2,1)S(1)} %copy-done.3, bf16[8,128,1024]{2,1,0:T(8,128)(2,1)S(1)} %bitcast.88), kind=kOutput, calls=%fused_computation.74 | convolution fusion | flops 4294967296 | bytes 14680064 | tf_op jit(solution)/shard_map/dot_general | solution.py:1698
  32.2 1.4 fusion.5.spots_ref
  33.6 2.5 copy.45
  36.1 2.5 copy.46
  38.6 1.0 copy.31.select_in_ref.select_back_ref.refs_9_
  39.6 0.8 maximum_bitcast_fusion.head_ref
  40.4 74.2 %scan_summary.1 = (f32[1024,2048]{1,0:T(8,128)}, bf16[1024,2048]{1,0:T(8,128)(2,1)}, f32[1024,2048]{1,0:T(8,128)}, f32[1024,2048]{1,0:T(8,128)}, f32[1024,2048]{...) custom-call(f32[1024,2048]{1,0:T(8,128)} %copy-done, ...), custom_call_target="tpu_custom_call" | custom-call | tf_op jit(solution)/shard_map/scan_summary/pallas_call | solution.py:614
  114.6 22.0 %exchange.1 = (f32[16,2048]{1,0:T(8,128)}, f32[16,2048]{1,0:T(8,128)}) custom-call(f32[48,2048]{1,0:T(8,128)} %get-tuple-element.44.totals_ref), custom_call_target="tpu_custom_call" | custom-call | tf_op jit(solution)/shard_map/exchange/pallas_call | solution.py:1650
  136.6 65.5 %scan_forward.1 = (bf16[16384,2048]{1,0:T(8,128)(2,1)}, f32[1024,128]{1,0:T(8,128)}, bf16[1024,2048]{1,0:T(8,128)(2,1)}, bf16[1024,2048]{1,0:T(8,128)(2,1)}, f32[8,2048]{1,0:T(8,128)}) custom-call(f32[1024,2048]{1,0:T(8,128)} %get-tuple-element.38.step_ref, f32[1024,2048]{1,0:T(8,128)} %get-tuple-element.39.drive_ref, ...), custom_call_target="tpu_custom_call" | custom-call | tf_op jit(solution)/shard_map/scan_forward/pallas_call | solution.py:644
  202.2 17.7 %flat_product.2.flat_ref = f32[4096,8,128]{2,1,0:T(8,128)} custom-call(bf16[1024,1024]{1,0:T(8,128)(2,1)} %copy-done.1, bf16[1024,2048]{1,0:T(8,128)(2,1)} %get-tuple-element.53.refs_1_.refs_0_, bf16[1024,2048]{1,0:T(8,128)(2,1)} %get-tuple-element.54.refs_2_.refs_5_, bf16[1024,1024]{1,0:T(8,128)(2,1)} %bitcast.80), custom_call_target="tpu_custom_call" | custom-call | tf_op jit(solution)/shard_map/flat_product/pallas_call | solution.py:858
  219.9 1.2 fusion.6.begin_ref
  221.1 120.7 %scan_backward.1 = (bf16[1024,2048]{1,0:T(8,128)(2,1)}, bf16[1024,2048]{1,0:T(8,128)(2,1)}, bf16[1024,128]{1,0:T(8,128)(2,1)}, f32[128,2048]{1,0:T(8,128)}, f32[...) custom-call(f32[1024,2048]{1,0:T(8,128)} %get-tuple-element.38.step_ref, ...), custom_call_target="tpu_custom_call" | custom-call | tf_op jit(solution)/shard_map/scan_backward/pallas_call | solution.py:696
  341.8 1.2 slice_bitcast_fusion.1
  343.1 1.7 collective-permute-start.1
  344.7 4.5 fusion.30.refs_2_
  350.2 1.7 fusion.11.refs_5_
  352.6 1.0 fusion.16
  353.6 1.0 fusion.19
  354.6 0.9 fusion.22
  356.8 0.7 bitcast_dynamic-update-slice_fusion.refs_1_
  357.5 11.9 %flat_product.3.flat_ref = f32[2560,8,128]{2,1,0:T(8,128)} custom-call(bf16[1024,1024]{1,0:T(8,128)(2,1)} %copy-done.1, bf16[1024,2048]{1,0:T(8,128)(2,1)} %bitcast_dynamic-update-slice_fusion.refs_1_, f32[2048,128]{1,0:T(8,128)} %fusion.30.refs_2_, f32[4,2048]{1,0:T(4,128)} %pad_maximum_fusion.1.refs_3_, f32[1,2048]{1,0:T(1,128)} %get-tuple-element.78.refs_4_, ...), custom_call_target="tpu_custom_call" | custom-call | tf_op jit(solution)/shard_map/flat_product/pallas_call | solution.py:858
  369.4 96.8 %reduce_late.1 = (f32[205,8,128]{2,1,0:T(8,128)}, f32[2,8,128]{2,1,0:T(8,128)}, bf16[1024,1024]{1,0:T(8,128)(2,1)}, bf16[1024,1024]{1,0:T(8,128)(2,1)}, f32[205,8,128]{2,1,0:T(8,128)}) custom-call(f32[2560,8,128]{2,1,0:T(8,128)} %flat_product.3.flat_ref, f32[208,8,128]{2,1,0:T(8,128)} %get-tuple-element.63.early_ref, f32[1,1024]{1,0:T(1,128)} %bitcast.113, ...), custom_call_target="tpu_custom_call" | custom-call | tf_op jit(solution)/shard_map/reduce_late/pallas_call | solution.py:1547
  466.3 1.4 multiply_reduce_fusion.1
  469.1 4.5 add_multiply_fusion
  473.6 1.3 copy.52
  474.9 1.3 copy.53
  (70 shorter events, 3.4 us)
Async XLA Ops:
  3.5 13.5 %slice-start = ((s8[8388608]{0:T(1024)(128)(4,1)}), s8[4194304]{0:T(1024)(128)(4,1)S(1)}, s32[]{:S(2)}) async-start(s8[8388608]{0:T(1024)(128)(4,1)} %bitcast.85), calls=%async_computation | async-start | bytes 8388608
  6.8 10.2 %copy-start.1 = (bf16[1024,1024]{1,0:T(8,128)(2,1)}, bf16[1024,1024]{1,0:T(8,128)(2,1)S(1)}, u32[]{:S(2)}) copy-start(bf16[1024,1024]{1,0:T(8,128)(2,1)S(1)} %multiply_convert_fusion.refs_0_) | copy-start | bytes 6291460
  6.8 10.2 %slice-start.1 = ((s8[8388608]{0:T(1024)(128)(4,1)}), s8[4194304]{0:T(1024)(128)(4,1)S(1)}, s32[]{:S(2)}) async-start(s8[8388608]{0:T(1024)(128)(4,1)} %bitcast.85), calls=%async_computation.1 | async-start | bytes 8388608
  13.9 9.9 %copy-start = (f32[1024,2048]{1,0:T(8,128)}, f32[1024,2048]{1,0:T(8,128)S(1)}, u32[]{:S(2)}) copy-start(f32[1024,2048]{1,0:T(8,128)S(1)} %fusion.2.stream_ref) | copy-start | bytes 25165828
  14.0 9.8 %copy-start.13 = (f32[16,2048]{1,0:T(8,128)S(1)}, f32[16,2048]{1,0:T(8,128)}, u32[]{:S(2)}) copy-start(f32[16,2048]{1,0:T(8,128)} %refs_12_.1) | copy-start | bytes 393220
  14.0 11.0 %copy-start.3 = (bf16[2048,1024]{1,0:T(8,128)(2,1)S(1)}, bf16[2048,1024]{1,0:T(8,128)(2,1)}, u32[]{:S(2)}) copy-start(bf16[2048,1024]{1,0:T(8,128)(2,1)} %refs_6_.1) | copy-start | bytes 12582916
  14.0 10.9 %copy-start.5 = (bf16[1,1024,1024]{2,1,0:T(8,128)(2,1)S(1)}, bf16[1,1024,1024]{2,1,0:T(8,128)(2,1)}, u32[]{:S(2)}) copy-start(bf16[1,1024,1024]{2,1,0:T(8,128)(2,1)} %param.15) | copy-start | bytes 6291460
  14.1 25.6 %collective-permute-start = (f32[3,2048]{1,0:T(4,128)S(1)}, f32[3,2048]{1,0:T(4,128)S(1)}, u32[]{:S(2)}, u32[]{:S(2)}) collective-permute-start(f32[3,2048]{1,0:T(4,128)S(1)} %bitcast.103), channel_id=1, source_target_pairs={{0,1},{1,2},{2,3},{3,4},{4,5},{5,6},{6,7},{8,9},{9,10},{10,11},{11... | collective-permute-start | bytes 73736 | tf_op jit(solution)/shard_map/ppermute | solution.py:36
  25.0 8.6 %copy-start.14 = (f32[4,2048]{1,0:T(4,128)S(1)}, f32[4,2048]{1,0:T(4,128)}, u32[]{:S(2)}) copy-start(f32[4,2048]{1,0:T(4,128)} %refs_7_.1) | copy-start | bytes 98308
  32.2 3.9 copy-start.2
  33.6 5.0 %copy-start.15 = (bf16[2048,96]{0,1:T(8,128)(2,1)S(1)}, bf16[2048,96]{0,1:T(8,128)(2,1)}, u32[]{:S(2)}) copy-start(bf16[2048,96]{0,1:T(8,128)(2,1)} %param.20) | copy-start | bytes 1179652
  202.1 17.8 %copy-start.8 = (f32[128,2048]{1,0:T(8,128)S(1)}, f32[128,2048]{1,0:T(8,128)}, u32[]{:S(2)}) copy-start(f32[128,2048]{1,0:T(8,128)} %get-tuple-element.43) | copy-start | bytes 3145732
  202.1 17.8 %copy-start.9 = (f32[128,2048]{1,0:T(8,128)S(1)}, f32[128,2048]{1,0:T(8,128)}, u32[]{:S(2)}) copy-start(f32[128,2048]{1,0:T(8,128)} %get-tuple-element.42) | copy-start | bytes 3145732
  202.2 17.7 %copy-start.18 = (f32[16,2048]{1,0:T(8,128)S(1)}, f32[16,2048]{1,0:T(8,128)}, u32[]{:S(2)}) copy-start(f32[16,2048]{1,0:T(8,128)} %get-tuple-element.45) | copy-start | bytes 393220
  341.8 7.5 %copy-start.10 = (f32[128,2048]{1,0:T(8,128)S(1)}, f32[128,2048]{1,0:T(8,128)}, u32[]{:S(2)}) copy-start(f32[128,2048]{1,0:T(8,128)} %get-tuple-element.61) | copy-start | bytes 3145732
  341.8 8.4 %copy-start.4 = (bf16[1024,2048]{1,0:T(8,128)(2,1)S(1)}, bf16[1024,2048]{1,0:T(8,128)(2,1)}, u32[]{:S(2)}) copy-start(bf16[1024,2048]{1,0:T(8,128)(2,1)} %get-tuple-element.60) | copy-start | bytes 12582916
  341.8 8.4 %copy-start.17 = (bf16[1024,128]{1,0:T(8,128)(2,1)S(1)}, bf16[1024,128]{1,0:T(8,128)(2,1)}, u32[]{:S(2)}) copy-start(bf16[1024,128]{1,0:T(8,128)(2,1)} %get-tuple-element.59) | copy-start | bytes 786436
  343.1 9.5 %collective-permute-start.1 = (f32[3,2048]{1,0:T(4,128)S(1)}, f32[3,2048]{1,0:T(4,128)S(1)}, u32[]{:S(2)}, u32[]{:S(2)}) collective-permute-start(f32[3,2048]{1,0:T(4,128)S(1)} %bitcast.105), channel_id=1, source_target_pairs={{1,0},{2,1},{3,2},{4,3},{5,4},{6,5},{7,6},{9,8},{10,9},{11,10},{12... | collective-permute-start | bytes 73736 | tf_op jit(solution)/shard_map/ppermute | solution.py:36
  349.2 2.6 copy-start.16
  349.2 2.7 copy-start.19
  349.5 7.3 %copy-start.11 = (f32[48,2048]{1,0:T(8,128)S(1)}, f32[48,2048]{1,0:T(8,128)}, u32[]{:S(2)}) copy-start(f32[48,2048]{1,0:T(8,128)} %get-tuple-element.56) | copy-start | bytes 1179652
  369.4 99.7 %copy-start.12 = (f32[208352]{0:T(1024)S(1)}, f32[208352]{0:T(1024)}, u32[]{:S(2)}) copy-start(f32[208352]{0:T(1024)} %param.26) | copy-start | bytes 2500228
  466.2 7.3 %copy-start.7 = (bf16[1024,1024]{1,0:T(8,128)(2,1)S(1)}, bf16[1024,1024]{1,0:T(8,128)(2,1)}, u32[]{:S(2)}) copy-start(bf16[1024,1024]{1,0:T(8,128)(2,1)} %get-tuple-element.64) | copy-start | bytes 6291460
  469.1 5.8 %copy-start.6 = (bf16[1024,1024]{1,0:T(8,128)(2,1)S(1)}, bf16[1024,1024]{1,0:T(8,128)(2,1)}, u32[]{:S(2)}) copy-start(bf16[1024,1024]{1,0:T(8,128)(2,1)} %get-tuple-element.65) | copy-start | bytes 6291460
